TPU v7x, 512 devices: a whole 4x8x8 slice. The times are simulated.
512 devices in a mesh: gx: 8 (over z), gy: 8 (over y), gz: 8 (over x, core).
Axes of the slice: x: 4, y: 8, z: 8, core: 2. Of those that a mesh axis runs over, the one named last changes fastest.
Arguments:
- fluid_state: float32 [5, 32, 128, 2048], P(None, 'gx', 'gy', 'gz'), may hold values from -4 to 20, as said below
- parcel_data: float32 [24, 24, 24, 8, 64], P('gx', 'gy', 'gz'), may hold values from -2 to 2, as said below
- host_element: int32 [24, 24, 24, 64], P('gx', 'gy', 'gz'), may hold values from 0 to 255
- slot_counts: int32 [24, 24, 24], P('gx', 'gy', 'gz'), may hold values from 0 to 64, as said below
Outputs:
- fluid_next: float32 [5, 32, 128, 2048], P(None, 'gx', 'gy', 'gz')
- parcel_velocity: float32 [24, 24, 24, 3, 64], P('gx', 'gy', 'gz')
Inputs may be any that keep to these rules, and one draw needn't show every extreme that they name: `fluid_state`: every node holds the conserved variables of a state with density 0.6 to 2.7, velocity components within 1.2 and pressure 0.6 to 4.5. `parcel_data`: entries 0 to 2 along the fourth dimension are reference coordinates within -1 to 1, entries 3 to 5 velocities, entry 6 a relaxation time of 0.05 to 0.5, entry 7 a parcel mass of 0.01 to 0.1. `host_element`: element numbers (a * 4 + b) * 64 + c of the destination device's block. `slot_counts`: counts toward offsets that leave the grid are 0; in every draw some destination devices receive 64 live slots from each of their neighbouring sources, themselves included.
All inputs are finite; a program needn't handle non-finite values.
Results may differ from a plain program's by a relative error of at most 0.0003.
Values sent between devices are 32-bit elements; how exact they have to be, the bound alone decides.
No kernel may reach another device: no remote copies, remote signals or barrier semaphores. Data moves between devices by JAX's collectives and lax.ppermute only.
A program may use at most 64 MiB of HBM per device.

v0:
```python
import jax
import jax.numpy as jnp
import numpy as np
from jax import lax
from jax.sharding import PartitionSpec as P

GAS_GAMMA = 1.4
COURANT = 0.5
INV_END = 6.0


def extended_2(cells, sides, width):
    for axis, dim in sides:
        count = lax.axis_size(axis)
        ends = count - 1
        head = lax.slice_in_dim(cells, 0, width, axis=dim)
        tail = lax.slice_in_dim(cells, cells.shape[dim] - width, cells.shape[dim], axis=dim)
        cells = jnp.concatenate(
            [
                lax.ppermute(tail, axis, [(i, (i + 1) % count) for i in range(ends)]),
                cells,
                lax.ppermute(head, axis, [((i + 1) % count, i) for i in range(ends)]),
            ],
            axis=dim,
        )
    return cells


def lobatto_tables():
    points = np.array([-1.0, -1.0 / np.sqrt(5.0), 1.0 / np.sqrt(5.0), 1.0])
    weights = np.array([1.0 / 6.0, 5.0 / 6.0, 5.0 / 6.0, 1.0 / 6.0])
    factor = np.array(
        [
            np.prod(
                [
                    points[row_index] - points[col_index]
                    for col_index in range(4)
                    if col_index != row_index
                ]
            )
            for row_index in range(4)
        ]
    )
    derivative = np.zeros((4, 4))
    for row_index in range(4):
        for col_index in range(4):
            if row_index != col_index:
                derivative[row_index, col_index] = factor[row_index] / (
                    factor[col_index] * (points[row_index] - points[col_index])
                )
        derivative[row_index, row_index] = sum(
            (
                1.0 / (points[row_index] - points[col_index])
                for col_index in range(4)
                if col_index != row_index
            )
        )
    return (points, weights, derivative)


def primitive(conserved):
    density = conserved[0]
    velocity = conserved[1:4] / density
    pressure = (GAS_GAMMA - 1.0) * (
        conserved[4] - 0.5 * density * jnp.sum(velocity * velocity, axis=0)
    )
    sound_speed = jnp.sqrt(GAS_GAMMA * pressure / density)
    return (velocity, pressure, sound_speed)


def normal_flux(conserved, direction):
    velocity, pressure, sound_speed = primitive(conserved)
    normal_speed = velocity[direction]
    momentum = conserved[1:4] * normal_speed
    unit_vec = (jnp.arange(3) == direction).astype(jnp.float32)
    momentum = momentum + unit_vec.reshape((3,) + (1,) * (conserved.ndim - 1)) * pressure
    flux_vec = jnp.concatenate(
        [
            conserved[direction + 1][None],
            momentum,
            ((conserved[4] + pressure) * normal_speed)[None],
        ],
        axis=0,
    )
    return (flux_vec, jnp.abs(normal_speed) + sound_speed)


def face_flux(left_side, right_side, direction):
    flux_left, speed_left = normal_flux(left_side, direction)
    flux_right, speed_right = normal_flux(right_side, direction)
    spread = jnp.maximum(speed_left, speed_right)
    common = 0.5 * (flux_left + flux_right) - 0.5 * spread * (right_side - left_side)
    return (common, flux_left, flux_right)


def mirror(conserved, direction):
    flip_sign = 1.0 - 2.0 * (jnp.arange(5) == direction + 1).astype(jnp.float32)
    return conserved * flip_sign.reshape((5,) + (1,) * (conserved.ndim - 1))


def surface_term(padded, direction, elem_along):
    axis_pos = direction + 1
    left_side = lax.slice_in_dim(padded, 0, 4 * elem_along + 1, 4, axis_pos)
    right_side = lax.slice_in_dim(padded, 1, 4 * elem_along + 2, 4, axis_pos)
    common, flux_left, flux_right = face_flux(left_side, right_side, direction)
    lower_corr = INV_END * (
        lax.slice_in_dim(common, 0, elem_along, 1, axis_pos)
        - lax.slice_in_dim(flux_right, 0, elem_along, 1, axis_pos)
    )
    upper_corr = -INV_END * (
        lax.slice_in_dim(common, 1, elem_along + 1, 1, axis_pos)
        - lax.slice_in_dim(flux_left, 1, elem_along + 1, 1, axis_pos)
    )
    zero_fill = jnp.zeros_like(lower_corr)
    stacked = jnp.stack([lower_corr, zero_fill, zero_fill, upper_corr], axis=axis_pos + 1)
    shape_out = list(lower_corr.shape)
    shape_out[axis_pos] = 4 * elem_along
    return stacked.reshape(shape_out)


def along_nodes(field_data, axis_pos, elem_along, derivative):
    dim_sizes = field_data.shape
    split_shape = dim_sizes[:axis_pos] + (elem_along, 4) + dim_sizes[axis_pos + 1 :]
    applied = jnp.tensordot(
        field_data.reshape(split_shape),
        derivative,
        axes=([axis_pos + 1], [1]),
        precision=lax.Precision.HIGHEST,
    )
    return jnp.moveaxis(applied, -1, axis_pos + 1).reshape(dim_sizes)


def fluid_rate(interior, rim_pairs, counts_elem, derivative):
    tendency = jnp.zeros_like(interior)
    for direction in range(3):
        axis_pos = direction + 1
        flux_vec, _ = normal_flux(interior, direction)
        tendency = tendency - along_nodes(flux_vec, axis_pos, counts_elem[direction], derivative)
        padded_dir = jnp.concatenate(
            [rim_pairs[direction][0], interior, rim_pairs[direction][1]], axis=axis_pos
        )
        tendency = tendency + surface_term(padded_dir, direction, counts_elem[direction])
    return tendency


def lagrange_rows(ref_coord, points):
    basis_rows = []
    for node_index in range(4):
        product_term = jnp.ones_like(ref_coord)
        for other_index in range(4):
            if other_index != node_index:
                product_term = (
                    product_term
                    * (ref_coord - float(points[other_index]))
                    / float(points[node_index] - points[other_index])
                )
        basis_rows.append(product_term)
    return jnp.stack(basis_rows, axis=0)


def parcel_forces(payload, gathered, live_mask, time_step, points):
    basis_x = lagrange_rows(payload[0], points)
    basis_y = lagrange_rows(payload[1], points)
    basis_z = lagrange_rows(payload[2], points)
    shape_weight = (
        basis_x[:, None, None, :] * basis_y[None, :, None, :] * basis_z[None, None, :, :]
    ).reshape(64, payload.shape[1])
    fluid_vel = jnp.einsum("ps,spc->cs", shape_weight, gathered, precision=lax.Precision.HIGHEST)
    parcel_vel = payload[3:6]
    relax_time = jnp.where(live_mask > 0, payload[6], 1.0)
    acceleration = (fluid_vel - parcel_vel) / relax_time
    parcel_mass = payload[7] * live_mask
    source = jnp.concatenate(
        [
            -parcel_mass * acceleration,
            (-parcel_mass * jnp.sum(acceleration * parcel_vel, axis=0))[None],
        ],
        axis=0,
    )
    new_velocity = (parcel_vel + time_step * acceleration) * live_mask
    return (shape_weight, source, new_velocity)


def wall_rims(interior, rim_pair, direction, at_low, at_high):
    axis_pos = direction + 1
    extent = interior.shape[axis_pos]
    first_layer = lax.slice_in_dim(interior, 0, 1, 1, axis_pos)
    last_layer = lax.slice_in_dim(interior, extent - 1, extent, 1, axis_pos)
    lower_rim = jnp.where(at_low, mirror(first_layer, direction), rim_pair[0])
    upper_rim = jnp.where(at_high, mirror(last_layer, direction), rim_pair[1])
    return (lower_rim, upper_rim)


def local(fluid_state, parcel_data, host_element, slot_counts):
    points, weights, derivative_np = lobatto_tables()
    derivative = jnp.asarray(derivative_np, dtype=jnp.float32)
    cube_weights = weights[:, None, None] * weights[None, :, None] * weights[None, None, :]
    inv_mass = jnp.asarray((1.0 / cube_weights).reshape(64), dtype=jnp.float32)
    counts_elem = (fluid_state.shape[1] // 4, fluid_state.shape[2] // 4, fluid_state.shape[3] // 4)
    elem_count = counts_elem[0] * counts_elem[1] * counts_elem[2]
    slot_cap = host_element.shape[3]
    slot_total = 27 * slot_cap
    slot_index = lax.broadcasted_iota(jnp.int32, host_element.shape, 3)
    live_sent = slot_index < slot_counts[:, :, :, None]
    host_code = jnp.where(live_sent, host_element + 1, 0).astype(jnp.float32)
    packet = jnp.concatenate([parcel_data, host_code[:, :, :, None, :]], axis=3)
    extended_packet = extended_2(packet, (("gx", 0), ("gy", 1), ("gz", 2)), 1)
    arrived = extended_packet[0::2, 0::2, 0::2]
    payload_full = arrived.transpose(3, 0, 1, 2, 4).reshape((9, slot_total))
    payload = payload_full[:8]
    host_ids = payload_full[8].astype(jnp.int32) - 1
    velocity, pressure, sound_speed = primitive(fluid_state)
    local_top = jnp.max(jnp.sqrt(jnp.sum(velocity * velocity, axis=0)) + sound_speed)
    global_top = lax.pmax(local_top, ("gx", "gy", "gz"))
    time_step = COURANT * 2.0 / (7.0 * global_top)
    extended = extended_2(fluid_state, (("gx", 1), ("gy", 2), ("gz", 3)), 1)
    rims_x = (extended[:, :1, 1:-1, 1:-1], extended[:, -1:, 1:-1, 1:-1])
    rims_y = (extended[:, 1:-1, :1, 1:-1], extended[:, 1:-1, -1:, 1:-1])
    rims_z = (extended[:, 1:-1, 1:-1, :1], extended[:, 1:-1, 1:-1, -1:])
    rim_pairs = (
        wall_rims(
            fluid_state,
            rims_x,
            0,
            lax.axis_index("gx") == 0,
            lax.axis_index("gx") == lax.axis_size("gx") - 1,
        ),
        wall_rims(
            fluid_state,
            rims_y,
            1,
            lax.axis_index("gy") == 0,
            lax.axis_index("gy") == lax.axis_size("gy") - 1,
        ),
        wall_rims(
            fluid_state,
            rims_z,
            2,
            lax.axis_index("gz") == 0,
            lax.axis_index("gz") == lax.axis_size("gz") - 1,
        ),
    )
    tendency = fluid_rate(fluid_state, rim_pairs, counts_elem, derivative)
    node_vel = (
        velocity.reshape((3, counts_elem[0], 4, counts_elem[1], 4, counts_elem[2], 4))
        .transpose(1, 3, 5, 2, 4, 6, 0)
        .reshape((elem_count, 64, 3))
    )
    host_safe = jnp.maximum(host_ids, 0)
    live_mask = (host_ids >= 0).astype(jnp.float32)
    gathered = jnp.take(node_vel, host_safe, axis=0)
    shape_weight, source, new_velocity = parcel_forces(
        payload, gathered, live_mask, time_step, points
    )
    contrib = (source[:, None, :] * shape_weight[None, :, :] * inv_mass[None, :, None]).reshape(
        (256, slot_total)
    )
    onehot = (host_ids[:, None] == lax.broadcasted_iota(jnp.int32, (1, elem_count), 1)).astype(
        jnp.float32
    )
    deposit = jnp.dot(
        contrib, onehot, precision=lax.Precision.HIGHEST, preferred_element_type=jnp.float32
    )
    deposit = (
        deposit.reshape((4, 4, 4, 4, counts_elem[0], counts_elem[1], counts_elem[2]))
        .transpose(0, 4, 1, 5, 2, 6, 3)
        .reshape((4,) + fluid_state.shape[1:])
    )
    tendency = tendency + jnp.concatenate([jnp.zeros_like(deposit[:1]), deposit], axis=0)
    fluid_next = fluid_state + time_step * tendency
    velocity_out = new_velocity.reshape((3, 3, 3, 3, slot_cap)).transpose(1, 2, 3, 0, 4)
    return (fluid_next, velocity_out)


def solution(mesh):
    placed = (
        P(None, "gx", "gy", "gz"),
        P("gx", "gy", "gz", None, None),
        P("gx", "gy", "gz", None),
        P("gx", "gy", "gz"),
    )
    return jax.shard_map(
        local,
        mesh=mesh,
        in_specs=placed,
        out_specs=(P(None, "gx", "gy", "gz"), P("gx", "gy", "gz", None, None)),
        check_vma=False,
    )
```

profile of v0, /device:TPU:1, one launch (start us, length us, event | category | flops | bytes accessed | tf_op | source)
XLA Modules:
  0.0 251.3 jit_solution(10534735870388506028)
XLA Ops:
  3.2 4.8 %collective-permute-start.6 = (f32[1,3,3,9,64]{4,3,2,1,0:T(8,128)}, f32[1,3,3,9,64]{4,3,2,1,0:T(8,128)S(1)}, u32[]{:S(2)}, u32[]{:S(2)}) collective-permute-start(f32[1,3,3,9,64]{4,3,2,1,0:T(8,128)} %get-tuple-element.86), channel_id=1, source_target_pairs={{0,64},{64,128},{128,192},{192,256},{256,320},{320,384},{384,448},... | collective-permute-start | bytes 62216 | tf_op jit(solution)/shard_map/ppermute | solution.py:20
  11.3 5.2 %collective-permute-start = (f32[5,1,16,256]{3,1,2,0:T(1,128)}, f32[5,1,16,256]{3,1,2,0:T(1,128)}, u32[]{:S(2)}, u32[]{:S(2)}) collective-permute-start(f32[5,1,16,256]{3,1,2,0:T(1,128)} %get-tuple-element.82), channel_id=1, source_target_pairs={{0,64},{64,128},{128,192},{192,256},{256,320},{320,384},{384,448},... | collective-permute-start | bytes 245768 | tf_op jit(solution)/shard_map/ppermute | solution.py:20
  25.8 2.2 fusion.26
  30.6 3.8 %collective-permute-start.8 = (f32[5,1,3,9,64]{4,3,2,1,0:T(8,128)}, f32[5,1,3,9,64]{4,3,2,1,0:T(8,128)}, u32[]{:S(2)}, u32[]{:S(2)}) collective-permute-start(f32[5,1,3,9,64]{4,3,2,1,0:T(8,128)} %get-tuple-element.70), channel_id=1, source_target_pairs={{0,8},{8,16},{16,24},{24,32},{32,40},{40,48},{48,56},{1,9},{9,17},... | collective-permute-start | bytes 103688 | tf_op jit(solution)/shard_map/ppermute | solution.py:20
  36.3 106.2 %pmax.7 = f32[]{:T(128)} all-reduce(f32[]{:T(128)} %add_reduce_fusion), channel_id=1, replica_groups=mesh['gx'=8,'gy'=8,'gz'=8] {'gx','gy','gz'}, use_global_device_ids=true, to_apply=%region_2.3 | all-reduce | flops 1 | bytes 8 | tf_op jit(solution)/shard_map/pmax | solution.py:214
  142.6 7.8 %reshape.747 = f32[3,1,4,4,4,64,4]{6,5,4,3,2,0,1:T(8,128)} reshape(f32[3,4,16,256]{3,2,1,0:T(8,128)S(1)} %copy.166) | data formatting | bytes 393216 | tf_op jit(solution)/shard_map/reshape | solution.py:245
  150.4 4.6 %copy.167 = f32[1,4,64,4,4,4,3]{2,1,5,4,3,6,0:T(4,128)S(1)} copy(f32[1,4,64,4,4,4,3]{5,2,4,1,3,6,0:T(8,128)} %bitcast.215) | data formatting | bytes 393216 | tf_op jit(solution)/shard_map/transpose | solution.py:246
  155.5 2.9 %copy.160 = f32[5,4,16,64,4]{2,4,3,1,0:T(4,128)S(1)} copy(f32[5,4,16,64,4]{3,4,2,1,0:T(4,128)} %fusion.26) | data formatting | bytes 655360 | tf_op jit(solution)/shard_map/dot_general | solution.py:124
  160.1 1.9 copy.149
  164.6 3.1 %collective-permute-start.10 = (f32[5,5,1,9,64]{4,3,2,1,0:T(8,128)}, f32[5,5,1,9,64]{4,3,2,1,0:T(8,128)}, u32[]{:S(2)}, u32[]{:S(2)}) collective-permute-start(f32[5,5,1,9,64]{4,3,2,1,0:T(8,128)} %get-tuple-element.61), channel_id=1, source_target_pairs={{0,1},{1,2},{2,3},{3,4},{4,5},{5,6},{6,7},{8,9},{9,10},{10,11},{11... | collective-permute-start | bytes 172808 | tf_op jit(solution)/shard_map/ppermute | solution.py:20
  167.7 2.0 collective-permute-start.11
  174.2 2.6 %collective-permute-start.2 = (f32[5,6,1,256]{3,2,1,0:T(1,128)S(1)}, f32[5,6,1,256]{3,2,1,0:T(1,128)S(1)}, u32[]{:S(2)}, u32[]{:S(2)}) collective-permute-start(f32[5,6,1,256]{3,2,1,0:T(1,128)S(1)} %get-tuple-element.65), channel_id=1, source_target_pairs={{0,8},{8,16},{16,24},{24,32},{32,40},{40,48},{48,56},{1,9},{9,17},... | collective-permute-start | bytes 92168 | tf_op jit(solution)/shard_map/ppermute | solution.py:20
  179.4 2.8 %collective-permute-done.3 = f32[5,6,1,256]{3,2,1,0:T(1,128)S(1)} collective-permute-done((f32[5,6,1,256]{3,2,1,0:T(1,128)S(1)}, f32[5,6,1,256]{3,2,1,0:T(1,128)S(1)}, u32[]{:S(2)}, u32[]{:S(2)}) %collective-permute-start.3) | collective-permute-done | bytes 30752 | tf_op jit(solution)/shard_map/ppermute | solution.py:22
  185.0 4.4 %collective-permute-start.4 = (f32[5,6,18,1]{3,2,1,0:T(8,128)}, f32[5,6,18,1]{3,2,1,0:T(8,128)}, u32[]{:S(2)}, u32[]{:S(2)}) collective-permute-start(f32[5,6,18,1]{3,2,1,0:T(8,128)} %get-tuple-element.59), channel_id=1, source_target_pairs={{0,1},{1,2},{2,3},{3,4},{4,5},{5,6},{6,7},{8,9},{9,10},{10,11},{11... | collective-permute-start | bytes 6488 | tf_op jit(solution)/shard_map/ppermute | solution.py:20
  189.3 1.9 collective-permute-start.5
  196.4 6.4 %gather_fusion = f32[1728,64,3]{1,2,0:T(4,128)} fusion(f32[256,64,3]{1,2,0:T(4,128)S(1)} %copy.168, s32[2048]{0:T(1024)S(1)} %pad_clamp_fusion), kind=kCustom, calls=%fused_computation | custom fusion | bytes 2661120 | tf_op jit(solution)/shard_map/jit(_take)/gather | solution.py:251
  202.8 11.6 %multiply_reduce_fusion = f32[1728,3]{1,0:T(8,128)S(1)} fusion(f32[1728,64,3]{1,2,0:T(4,128)} %gather_fusion, f32[1728,64]{1,0:T(8,128)S(1)} %copy.186, pred[1728]{0:T(1024)(128)(4,1)S(1)} %get-tuple-element.127), kind=kLoop, calls=%fused_computation.1 | loop fusion | flops 990144 | bytes 1791936
  215.3 4.1 %fusion.6 = f32[4,1,4,4,4,64,4]{5,6,3,4,2,0,1:T(4,128)S(1)} fusion(s32[4,64]{1,0:T(4,128)S(1)} %copy-done.13, s32[1728]{0:T(1024)S(1)} %sub.240, f32[4,4,4]{2,1,0:T(4,128)S(1)} %copy-done.16, f32[4,4,4,1728]{3,2,1,0:T(4,128)S(1)} %broadcast_multiply_fusion, f32[4,1728]{1,0:T(4,128)S(1)} %pad_maximum_fusion.24), kind=kOutput, calls=%fused_computation.9 | convolution fusion | flops 1360281600 | bytes 740352 | tf_op jit(solution)/shard_map/dot_general | solution.py:261
  219.3 4.8 %copy.184 = f32[4,1,4,4,4,64,4]{6,5,2,4,3,0,1:T(8,128)} copy(f32[4,1,4,4,4,64,4]{5,6,3,4,2,0,1:T(4,128)S(1)} %fusion.6) | data formatting | bytes 524288 | tf_op jit(solution)/shard_map/reshape | solution.py:267
  224.2 8.3 %reshape.821 = f32[4,4,16,256]{3,1,2,0:T(4,128)S(1)} reshape(f32[4,1,4,4,4,64,4]{6,5,2,4,3,0,1:T(8,128)} %copy.184) | data formatting | bytes 524288 | tf_op jit(solution)/shard_map/reshape | solution.py:267
  234.7 3.2 %slice.362 = f32[5,4,16,65]{3,2,1,0:T(8,128)S(1)} slice(f32[5,4,16,258]{3,2,1,0:T(8,128)S(1)} %pad_maximum_fusion.5), slice={[0:5:1], [0:4:1], [0:16:1], [1:258:4]} | slice | bytes 166400 | tf_op jit(solution)/shard_map/slice | solution.py:104
  237.9 3.1 %slice.356 = f32[5,4,16,65]{3,2,1,0:T(8,128)S(1)} slice(f32[5,4,16,258]{3,2,1,0:T(8,128)S(1)} %pad_maximum_fusion.5), slice={[0:5:1], [0:4:1], [0:16:1], [0:257:4]} | slice | bytes 166400 | tf_op jit(solution)/shard_map/slice | solution.py:103
  243.6 2.7 %pad_maximum_fusion = f32[5,4,16,64,4]{2,4,3,1,0:T(4,128)S(1)} fusion(f32[5,4,16,64,1]{2,4,3,1,0:T(1,128)} %copy.163, f32[5,4,16,64,1]{2,4,3,1,0:T(1,128)} %copy.162, f32[4]{0:T(128)S(1)} %pad.64.clone), kind=kLoop, calls=%fused_computation.2 | loop fusion | flops 163840 | bytes 491536 | tf_op jit(solution)/shard_map/stack | solution.py:115
  248.0 2.5 fusion.20
  (180 shorter events, 46.0 us)
Async XLA Ops:
  2.5 148.0 %copy-start.1 = (f32[3,3,3,9,64]{4,3,2,1,0:T(8,128)}, f32[3,3,3,9,64]{4,3,2,1,0:T(8,128)S(1)}, u32[]{:S(2)}) copy-start(f32[3,3,3,9,64]{4,3,2,1,0:T(8,128)S(1)} %dynamic-update-slice.1) | copy-start | bytes 186628
  3.2 26.7 %collective-permute-start.6 = (f32[1,3,3,9,64]{4,3,2,1,0:T(8,128)}, f32[1,3,3,9,64]{4,3,2,1,0:T(8,128)S(1)}, u32[]{:S(2)}, u32[]{:S(2)}) collective-permute-start(f32[1,3,3,9,64]{4,3,2,1,0:T(8,128)} %get-tuple-element.86), channel_id=1, source_target_pairs={{0,64},{64,128},{128,192},{192,256},{256,320},{320,384},{384,448},... | collective-permute-start | bytes 62216 | tf_op jit(solution)/shard_map/ppermute | solution.py:20
  8.0 21.9 %collective-permute-start.7 = (f32[1,3,3,9,64]{4,3,2,1,0:T(8,128)}, f32[1,3,3,9,64]{4,3,2,1,0:T(8,128)S(1)}, u32[]{:S(2)}, u32[]{:S(2)}) collective-permute-start(f32[1,3,3,9,64]{4,3,2,1,0:T(8,128)} %get-tuple-element.87), channel_id=1, source_target_pairs={{64,0},{128,64},{192,128},{256,192},{320,256},{384,320},{448,384},... | collective-permute-start | bytes 62216 | tf_op jit(solution)/shard_map/ppermute | solution.py:22
  11.3 158.4 %collective-permute-start = (f32[5,1,16,256]{3,1,2,0:T(1,128)}, f32[5,1,16,256]{3,1,2,0:T(1,128)}, u32[]{:S(2)}, u32[]{:S(2)}) collective-permute-start(f32[5,1,16,256]{3,1,2,0:T(1,128)} %get-tuple-element.82), channel_id=1, source_target_pairs={{0,64},{64,128},{128,192},{192,256},{256,320},{320,384},{384,448},... | collective-permute-start | bytes 245768 | tf_op jit(solution)/shard_map/ppermute | solution.py:20
  16.5 153.2 %collective-permute-start.1 = (f32[5,1,16,256]{3,1,2,0:T(1,128)}, f32[5,1,16,256]{3,1,2,0:T(1,128)}, u32[]{:S(2)}, u32[]{:S(2)}) collective-permute-start(f32[5,1,16,256]{3,1,2,0:T(1,128)} %get-tuple-element.81), channel_id=1, source_target_pairs={{64,0},{128,64},{192,128},{256,192},{320,256},{384,320},{448,384},... | collective-permute-start | bytes 245768 | tf_op jit(solution)/shard_map/ppermute | solution.py:22
  19.0 5.7 %copy-start.11 = (f32[3]{0:T(128)}, f32[3]{0:T(128)S(1)}, u32[]{:S(2)}) copy-start(f32[3]{0:T(128)S(1)} %compare_convert_fusion.2) | copy-start | bytes 40
  19.0 5.7 %copy-start.9 = (f32[3]{0:T(128)}, f32[3]{0:T(128)S(1)}, u32[]{:S(2)}) copy-start(f32[3]{0:T(128)S(1)} %get-tuple-element.139) | copy-start | bytes 40
  29.9 120.6 %copy-start.3 = (f32[1,3,3,9,64]{4,3,2,1,0:T(8,128)}, f32[1,3,3,9,64]{4,3,2,1,0:T(8,128)S(1)}, u32[]{:S(2)}) copy-start(f32[1,3,3,9,64]{4,3,2,1,0:T(8,128)S(1)} %collective-permute-done.7) | copy-start | bytes 62212
  30.6 132.2 %collective-permute-start.8 = (f32[5,1,3,9,64]{4,3,2,1,0:T(8,128)}, f32[5,1,3,9,64]{4,3,2,1,0:T(8,128)}, u32[]{:S(2)}, u32[]{:S(2)}) collective-permute-start(f32[5,1,3,9,64]{4,3,2,1,0:T(8,128)} %get-tuple-element.70), channel_id=1, source_target_pairs={{0,8},{8,16},{16,24},{24,32},{32,40},{40,48},{48,56},{1,9},{9,17},... | collective-permute-start | bytes 103688 | tf_op jit(solution)/shard_map/ppermute | solution.py:20
  34.5 128.3 %collective-permute-start.9 = (f32[5,1,3,9,64]{4,3,2,1,0:T(8,128)}, f32[5,1,3,9,64]{4,3,2,1,0:T(8,128)}, u32[]{:S(2)}, u32[]{:S(2)}) collective-permute-start(f32[5,1,3,9,64]{4,3,2,1,0:T(8,128)} %get-tuple-element.71), channel_id=1, source_target_pairs={{8,0},{16,8},{24,16},{32,24},{40,32},{48,40},{56,48},{9,1},{17,9},... | collective-permute-start | bytes 103688 | tf_op jit(solution)/shard_map/ppermute | solution.py:22
  162.0 11.2 %copy-start = (f32[5,4,16,256]{3,2,1,0:T(8,128)S(1)}, f32[5,4,16,256]{3,2,1,0:T(8,128)}, u32[]{:S(2)}) copy-start(f32[5,4,16,256]{3,2,1,0:T(8,128)} %param.6) | copy-start | bytes 983044
  164.6 13.5 %copy-start.12 = (f32[3]{0:T(128)S(1)}, f32[3]{0:T(128)}, u32[]{:S(2)}) copy-start(f32[3]{0:T(128)} %copy-done.11) | copy-start | bytes 40
  164.6 27.6 %collective-permute-start.10 = (f32[5,5,1,9,64]{4,3,2,1,0:T(8,128)}, f32[5,5,1,9,64]{4,3,2,1,0:T(8,128)}, u32[]{:S(2)}, u32[]{:S(2)}) collective-permute-start(f32[5,5,1,9,64]{4,3,2,1,0:T(8,128)} %get-tuple-element.61), channel_id=1, source_target_pairs={{0,1},{1,2},{2,3},{3,4},{4,5},{5,6},{6,7},{8,9},{9,10},{10,11},{11... | collective-permute-start | bytes 172808 | tf_op jit(solution)/shard_map/ppermute | solution.py:20
  167.7 24.4 %collective-permute-start.11 = (f32[5,5,1,9,64]{4,3,2,1,0:T(8,128)S(1)}, f32[5,5,1,9,64]{4,3,2,1,0:T(8,128)}, u32[]{:S(2)}, u32[]{:S(2)}) collective-permute-start(f32[5,5,1,9,64]{4,3,2,1,0:T(8,128)S(1)} %get-tuple-element.62), channel_id=1, source_target_pairs={{1,0},{2,1},{3,2},{4,3},{5,4},{6,5},{7,6},{9,8},{10,9},{11,10},{12... | collective-permute-start | bytes 172808 | tf_op jit(solution)/shard_map/ppermute | solution.py:22
  171.5 10.7 %copy-start.15 = (f32[5]{0:T(128)S(1)}, f32[5]{0:T(128)}, u32[]{:S(2)}) copy-start(f32[5]{0:T(128)} %fusion.69) | copy-start | bytes 64
  174.2 5.2 %collective-permute-start.2 = (f32[5,6,1,256]{3,2,1,0:T(1,128)S(1)}, f32[5,6,1,256]{3,2,1,0:T(1,128)S(1)}, u32[]{:S(2)}, u32[]{:S(2)}) collective-permute-start(f32[5,6,1,256]{3,2,1,0:T(1,128)S(1)} %get-tuple-element.65), channel_id=1, source_target_pairs={{0,8},{8,16},{16,24},{24,32},{32,40},{40,48},{48,56},{1,9},{9,17},... | collective-permute-start | bytes 92168 | tf_op jit(solution)/shard_map/ppermute | solution.py:20
  176.8 5.5 %collective-permute-start.3 = (f32[5,6,1,256]{3,2,1,0:T(1,128)S(1)}, f32[5,6,1,256]{3,2,1,0:T(1,128)S(1)}, u32[]{:S(2)}, u32[]{:S(2)}) collective-permute-start(f32[5,6,1,256]{3,2,1,0:T(1,128)S(1)} %get-tuple-element.66), channel_id=1, source_target_pairs={{8,0},{16,8},{24,16},{32,24},{40,32},{48,40},{56,48},{9,1},{17,9},... | collective-permute-start | bytes 92168 | tf_op jit(solution)/shard_map/ppermute | solution.py:22
  183.6 8.5 %copy-start.2 = (f32[3,3,3,9,64]{4,3,2,1,0:T(8,128)S(1)}, f32[3,3,3,9,64]{4,3,2,1,0:T(8,128)}, u32[]{:S(2)}) copy-start(f32[3,3,3,9,64]{4,3,2,1,0:T(8,128)} %copy-done.1) | copy-start | bytes 186628
  183.6 8.5 %copy-start.4 = (f32[1,3,3,9,64]{4,3,2,1,0:T(8,128)S(1)}, f32[1,3,3,9,64]{4,3,2,1,0:T(8,128)}, u32[]{:S(2)}) copy-start(f32[1,3,3,9,64]{4,3,2,1,0:T(8,128)} %copy-done.3) | copy-start | bytes 62212
  185.0 48.2 %collective-permute-start.4 = (f32[5,6,18,1]{3,2,1,0:T(8,128)}, f32[5,6,18,1]{3,2,1,0:T(8,128)}, u32[]{:S(2)}, u32[]{:S(2)}) collective-permute-start(f32[5,6,18,1]{3,2,1,0:T(8,128)} %get-tuple-element.59), channel_id=1, source_target_pairs={{0,1},{1,2},{2,3},{3,4},{4,5},{5,6},{6,7},{8,9},{9,10},{10,11},{11... | collective-permute-start | bytes 6488 | tf_op jit(solution)/shard_map/ppermute | solution.py:20
  189.3 43.9 %collective-permute-start.5 = (f32[5,6,18,1]{3,2,1,0:T(8,128)}, f32[5,6,18,1]{3,2,1,0:T(8,128)}, u32[]{:S(2)}, u32[]{:S(2)}) collective-permute-start(f32[5,6,18,1]{3,2,1,0:T(8,128)} %get-tuple-element.60), channel_id=1, source_target_pairs={{1,0},{2,1},{3,2},{4,3},{5,4},{6,5},{7,6},{9,8},{10,9},{11,10},{12... | collective-permute-start | bytes 6488 | tf_op jit(solution)/shard_map/ppermute | solution.py:22
  202.8 12.4 %copy-start.13 = (s32[4,64]{1,0:T(4,128)S(1)}, s32[4,64]{1,0:T(4,128)}, u32[]{:S(2)}) copy-start(s32[4,64]{1,0:T(4,128)} %multiply_add_fusion.9) | copy-start | bytes 3076
  202.8 12.4 %copy-start.16 = (f32[4,4,4]{2,1,0:T(4,128)S(1)}, f32[4,4,4]{2,1,0:T(4,128)}, u32[]{:S(2)}) copy-start(f32[4,4,4]{2,1,0:T(4,128)} %constant.183) | copy-start | bytes 772
  224.2 9.1 %copy-start.14 = (f32[5]{0:T(128)S(1)}, f32[5]{0:T(128)}, u32[]{:S(2)}) copy-start(f32[5]{0:T(128)} %fusion.70) | copy-start | bytes 64
  (7 other events, 18.8 us)
where the time goes:
time: 254 us; the launch traced here: 251 us
  blocking collectives  106 us (42%)
  local copies, waits for them, and re-layouts  65 us (26%)
  starting transfers between devices  33 us (13%)
  other arithmetic  31.9 us (13%)
  matrix products  10.1 us (4%)
  waiting for transfers between devices  2.83 us (1%)
    pmax x1, blocking collectives, local(): global_top = lax.pmax(local_top, ('gx', 'gy', 'gz'))  106 us
    ppermute x6, starting transfers between devices, extended_2(): lax.ppermute(tail, axis, [(i, (i + 1) % count) for i in range(ends)])  23.9 us
    reshape x2, local copies, waits for them, and re-layouts, local(): deposit = deposit.reshape((4, 4, 4, 4, counts_elem[0], counts_elem[1], co...  13.1 us
    unnamed x1, other arithmetic  11.6 us
    ppermute x6, starting transfers between devices, extended_2(): lax.ppermute(head, axis, [((i + 1) % count, i) for i in range(ends)])  9.08 us
    reshape x1, local copies, waits for them, and re-layouts, local(): velocity.reshape((3, counts_elem[0], 4, counts_elem[1], 4, counts_elem[2]...  7.84 us
    gather x1, local copies, waits for them, and re-layouts, local(): gathered = jnp.take(node_vel, host_safe, axis=0)  6.43 us
    dot_general x3, matrix products, along_nodes(): jnp.tensordot(field_data.reshape(split_shape), derivative, axes=([axis_po...  6.07 us
  transfers between devices with their start and end apart: 12, of which 1 were waited for; matrix products, arithmetic and copies ran while one was open for 34% of the time, Pallas kernels for 0%

commit v1 on v0

v1 whole, which is shorter than its diff:
```python
import jax
import jax.numpy as jnp
import numpy as np
from jax import lax
from jax.experimental import pallas as pl
from jax.experimental.pallas import tpu as pltpu
from jax.sharding import PartitionSpec as P

F32 = jnp.float32
BF16 = jnp.bfloat16
AXES = ("gx", "gy", "gz")
VMEM_BYTES = 24 * 1024 * 1024

NODES = np.array([-1.0, -1.0 / np.sqrt(5.0), 1.0 / np.sqrt(5.0), 1.0])
WEIGHTS = np.array([1.0 / 6.0, 5.0 / 6.0, 5.0 / 6.0, 1.0 / 6.0])


def derivative_table():
    factor = [np.prod([NODES[i] - NODES[j] for j in range(4) if j != i]) for i in range(4)]
    table = np.zeros((4, 4))
    for i in range(4):
        for j in range(4):
            if i != j:
                table[i, j] = factor[i] / (factor[j] * (NODES[i] - NODES[j]))
    return table


DERIV = derivative_table()
SCALE = [1.0 / np.prod([NODES[i] - NODES[j] for j in range(4) if j != i]) for i in range(4)]

GROUPS, TOP, FACE = 0, 9, 10


def by_pos(pos, values):
    out = jnp.full(pos.shape, float(values[3]), F32)
    for k in range(3):
        out = jnp.where(pos == k, float(values[k]), out)
    return out


def primitives(state):
    inverse = 1.0 / state[0]
    vel = [state[d + 1] * inverse for d in range(3)]
    square = vel[0] * vel[0] + vel[1] * vel[1] + vel[2] * vel[2]
    pressure = 0.4 * (state[4] - 0.5 * state[0] * square)
    sound = jnp.sqrt(1.4 * pressure * inverse)
    return vel, pressure, sound, square


def flux(state, vel, pressure, d):
    normal = vel[d]
    out = [state[d + 1]]
    for k in range(3):
        term = state[k + 1] * normal
        out.append(term + pressure if k == d else term)
    out.append((state[4] + pressure) * normal)
    return out


def side(state, d):
    vel, pressure, sound, _ = primitives(state)
    return flux(state, vel, pressure, d), jnp.abs(vel[d]) + sound


def pack_kernel(u_ref, data_ref, host_ref, count_ref, up_ref, down_ref, keep_ref, face_ref):
    slot = lax.broadcasted_iota(jnp.int32, (1, 64), 1)
    for a, out in ((2, up_ref), (0, down_ref), (1, keep_ref)):
        for b in range(3):
            for c in range(3):
                count = count_ref[a, b : b + 1, c : c + 1]
                host = host_ref[a, b, c : c + 1, :]
                code = jnp.where(slot < count, host + 1, 0).astype(F32)
                out[3 * b + c, :, 0:64] = data_ref[a, b, c]
                out[3 * b + c, :, 64:128] = jnp.broadcast_to(code, (8, 64))
    top = None
    for i in range(4):
        _, _, sound, square = primitives([u_ref[v, i] for v in range(5)])
        speed = jnp.sqrt(square) + sound
        top = speed if top is None else jnp.maximum(top, speed)
    top = jnp.maximum(top[:, :128], top[:, 128:])
    top = jnp.maximum(top[:8], top[8:])
    up_ref[TOP] = top
    down_ref[TOP] = top
    for v in range(5):
        for yh in range(2):
            for zh in range(2):
                tile = FACE + 4 * v + 2 * yh + zh
                ys, zs = slice(8 * yh, 8 * yh + 8), slice(128 * zh, 128 * zh + 128)
                up_ref[tile] = u_ref[v, 3, ys, zs]
                down_ref[tile] = u_ref[v, 0, ys, zs]
        for i in range(4):
            for zh in range(2):
                zs = slice(128 * zh, 128 * zh + 128)
                row = 4 * zh + i
                face_ref[v, row : row + 1, :] = u_ref[v, i, 15:16, zs]
                face_ref[5 + v, row : row + 1, :] = u_ref[v, i, 0:1, zs]
    lane = lax.broadcasted_iota(jnp.int32, (16, 128), 1)
    high = jnp.zeros((16, 128), F32)
    low = jnp.zeros((16, 128), F32)
    for v in range(5):
        for i in range(4):
            here = lane == 4 * v + i
            high = jnp.where(here, u_ref[v, i, :, 255:256], high)
            low = jnp.where(here, u_ref[v, i, :, 0:1], low)
    for yh in range(2):
        face_ref[10 + yh] = high[8 * yh : 8 * yh + 8]
        face_ref[12 + yh] = low[8 * yh : 8 * yh + 8]


def turn_y_kernel(lo_ref, hi_ref, own_ref, face_ref, mine_ref, up_ref, down_ref, keep_ref):
    for a, source in enumerate((lo_ref, own_ref, hi_ref)):
        for c in range(3):
            up_ref[3 * a + c] = source[6 + c]
            down_ref[3 * a + c] = source[c]
            keep_ref[3 * a + c] = source[3 + c]
    top = jnp.maximum(jnp.maximum(lo_ref[TOP], hi_ref[TOP]), mine_ref[TOP])
    up_ref[TOP] = top
    down_ref[TOP] = top
    for v in range(5):
        up_ref[FACE + v] = face_ref[v]
        down_ref[FACE + v] = face_ref[5 + v]


def turn_z_kernel(lo_ref, hi_ref, own_ref, face_ref, mine_ref, up_ref, down_ref, keep_ref):
    for b, source in enumerate((lo_ref, own_ref, hi_ref)):
        for a in range(3):
            up_ref[3 * a + b] = source[3 * a + 2]
            down_ref[3 * a + b] = source[3 * a]
            keep_ref[3 * a + b] = source[3 * a + 1]
    top = jnp.maximum(jnp.maximum(lo_ref[TOP], hi_ref[TOP]), mine_ref[TOP])
    up_ref[TOP] = top
    down_ref[TOP] = top
    for yh in range(2):
        up_ref[FACE + yh] = face_ref[10 + yh]
        down_ref[FACE + yh] = face_ref[12 + yh]


def wall(axis, last, own, received, sign_of):
    at = lax.axis_index(axis) == (lax.axis_size(axis) - 1 if last else 0)
    pick = jnp.full(received[0].shape, at.astype(jnp.int32), jnp.int32) == 1
    return [jnp.where(pick, sign_of(v) * own[v], received[v]) for v in range(5)]


def shift_rate(state, fluxes, speed, low, high, axis, pos, first, last, coef):
    count = state[0].shape[axis]
    low_state, low_flux, low_speed = low
    high_state, high_flux, high_speed = high
    at_low = pos == 0
    ends = at_low | (pos == 3)

    def beside(here, below, above):
        near = jnp.where(at_low, pltpu.roll(here, 1, axis), pltpu.roll(here, count - 1, axis))
        return jnp.where(first, below, jnp.where(last, above, near))

    spread = jnp.maximum(speed, beside(speed, low_speed, high_speed))
    spread = jnp.where(ends, 3.0 * spread, 0.0)
    out = []
    for v in range(5):
        value = fluxes[v]
        above = jnp.where(last, high_flux[v], pltpu.roll(value, count - 1, axis))
        below = jnp.where(first, low_flux[v], pltpu.roll(value, 1, axis))
        total = coef[1] * above + coef[-1] * below
        for d in (-3, -2, 2, 3):
            total = total + coef[d] * pltpu.roll(value, -d % count, axis)
        out.append(spread * (beside(state[v], low_state[v], high_state[v]) - state[v]) - total)
    return out


def rate_kernel(u_ref, xl_ref, xh_ref, yl_ref, yh_ref, zl_ref, zh_ref, face_ref, rate_ref, fx_ref, sx_ref):
    shape = (16, 256)
    row = lax.broadcasted_iota(jnp.int32, shape, 0)
    lane = lax.broadcasted_iota(jnp.int32, shape, 1)
    ypos, zpos = row & 3, lane & 3

    def coefs(pos):
        out = {}
        for d in (-3, -2, -1, 1, 2, 3):
            values = [DERIV[k, k + d] if 0 <= k + d < 4 else 0.0 for k in range(4)]
            if d == 1:
                values[3] = 3.0
            if d == -1:
                values[0] = -3.0
            out[d] = by_pos(pos, values)
        return out

    ycoef, zcoef = coefs(ypos), coefs(zpos)
    yfirst, ylast = row == 0, row == 15
    zfirst, zlast = lane == 0, lane == 255

    yflip = lambda v: -1.0 if v == 2 else 1.0
    ylow = wall("gy", False, [face_ref[5 + v] for v in range(5)], [yl_ref[FACE + v] for v in range(5)], yflip)
    yhigh = wall("gy", True, [face_ref[v] for v in range(5)], [yh_ref[FACE + v] for v in range(5)], yflip)
    ylow_flux, ylow_speed = side(ylow, 1)
    yhigh_flux, yhigh_speed = side(yhigh, 1)

    def columns(first_tile, ref):
        both = jnp.concatenate([ref[first_tile], ref[first_tile + 1]], axis=0)
        return [both if v == 0 else pltpu.roll(both, 128 - 4 * v, 1) for v in range(5)]

    zflip = lambda v: -1.0 if v == 3 else 1.0
    zlow = wall("gz", False, columns(12, face_ref), columns(FACE, zl_ref), zflip)
    zhigh = wall("gz", True, columns(10, face_ref), columns(FACE, zh_ref), zflip)
    zlow_flux, zlow_speed = side(zlow, 2)
    zhigh_flux, zhigh_speed = side(zhigh, 2)

    def pick_row(tile, i):
        return jnp.concatenate([tile[i : i + 1], tile[4 + i : 5 + i]], axis=1)

    for i in range(4):
        state = [u_ref[v, i] for v in range(5)]
        vel, pressure, sound, _ = primitives(state)
        xflux = flux(state, vel, pressure, 0)
        for v in range(5):
            fx_ref[v, i] = xflux[v]
        if i in (0, 3):
            sx_ref[i // 3] = jnp.abs(vel[0]) + sound
        low = ([pick_row(t, i) for t in ylow], [pick_row(t, i) for t in ylow_flux], pick_row(ylow_speed, i))
        high = ([pick_row(t, i) for t in yhigh], [pick_row(t, i) for t in yhigh_flux], pick_row(yhigh_speed, i))
        yrate = shift_rate(
            state, flux(state, vel, pressure, 1), jnp.abs(vel[1]) + sound,
            low, high, 0, ypos, yfirst, ylast, ycoef,
        )
        pick = lambda t: t[:, i : i + 1]
        low = ([pick(t) for t in zlow], [pick(t) for t in zlow_flux], pick(zlow_speed))
        high = ([pick(t) for t in zhigh], [pick(t) for t in zhigh_flux], pick(zhigh_speed))
        zrate = shift_rate(
            state, flux(state, vel, pressure, 2), jnp.abs(vel[2]) + sound,
            low, high, 1, zpos, zfirst, zlast, zcoef,
        )
        for v in range(5):
            rate_ref[v, i] = yrate[v] + zrate[v]

    xflip = lambda v: -1.0 if v == 1 else 1.0
    for half in range(2):
        for part in range(2):
            ys, zs = slice(8 * half, 8 * half + 8), slice(128 * part, 128 * part + 128)
            tile = FACE + 2 * half + part
            ends = []
            for last, i, ref in ((False, 0, xl_ref), (True, 3, xh_ref)):
                own = [u_ref[v, i, ys, zs] for v in range(5)]
                beyond = wall("gx", last, own, [ref[tile + 4 * v] for v in range(5)], xflip)
                far_flux, far_speed = side(beyond, 0)
                spread = 3.0 * jnp.maximum(sx_ref[i // 3, ys, zs], far_speed)
                sign = -3.0 if last else 3.0
                ends.append([sign * far_flux[v] + spread * (beyond[v] - own[v]) for v in range(5)])
            for v in range(5):
                f = [fx_ref[v, i, ys, zs] for i in range(4)]
                for j in range(4):
                    total = rate_ref[v, j, ys, zs]
                    for i in range(4):
                        if i != j:
                            total = total - float(DERIV[j, i]) * f[i]
                    if j == 0:
                        total = total + ends[0][v]
                    if j == 3:
                        total = total + ends[1][v]
                    rate_ref[v, j, ys, zs] = total


def split(value):
    high = value.astype(BF16)
    return high, (value - high.astype(F32)).astype(BF16)


def parcel_kernel(u_ref, zl_ref, zh_ref, own_ref, dep_ref, base_ref, acc_ref, tiles, vel_hi, vel_lo, z_hi, z_lo, a_hi, a_lo, total):
    for c, source in enumerate((zl_ref, own_ref, zh_ref)):
        for ab in range(9):
            tiles[3 * ab + c] = source[ab]
    tiles[27] = jnp.zeros((8, 128), F32)
    for i in range(4):
        inverse = 1.0 / u_ref[0, i]
        for d in range(3):
            high, low = split(u_ref[d + 1, i] * inverse)
            start = 16 * (4 * d + i)
            vel_hi[start : start + 16, :] = high
            vel_lo[start : start + 16, :] = low
    total[...] = jnp.zeros((256, 256), F32)
    left = lax.broadcasted_iota(jnp.int32, (8, 128), 1) < 64
    sub8 = lax.broadcasted_iota(jnp.int32, (8, 256), 0)
    sub16 = lax.broadcasted_iota(jnp.int32, (16, 256), 0)
    pos, block = sub16 & 3, sub16 >> 2
    weight_y = by_pos(pos, 1.0 / WEIGHTS)
    inner = float(NODES[2])

    def chunk(j, carry):
        fields, codes = [], []
        for p in range(2):
            first, second = tiles[4 * j + 2 * p], tiles[4 * j + 2 * p + 1]
            fields.append(jnp.where(left, first, pltpu.roll(second, 64, 1)))
            codes.append(jnp.where(left, pltpu.roll(first, 64, 1), second))
        field = jnp.concatenate(fields, axis=1)
        code = jnp.concatenate(codes, axis=1)
        live = code > 0.5
        host = code.astype(jnp.int32) - 1
        host = jnp.concatenate([host, host], axis=0)
        row_y, col_z = host >> 6, host & 63
        outer = (field + 1.0) * (field - 1.0)
        middle = (field + inner) * (field - inner)
        basis = [
            float(SCALE[0]) * middle * (field - 1.0),
            float(SCALE[1]) * outer * (field - inner),
            float(SCALE[2]) * outer * (field + inner),
            float(SCALE[3]) * middle * (field + 1.0),
        ]

        def spread(r):
            rows = [jnp.broadcast_to(basis[k][r : r + 1], (16, 256)) for k in range(4)]
            return jnp.where(pos == 0, rows[0], jnp.where(pos == 1, rows[1], jnp.where(pos == 2, rows[2], rows[3])))

        in_y = jnp.where(row_y == block, spread(1), 0.0)
        in_z = spread(2)
        in_z_hi = in_z.astype(BF16).astype(F32)
        in_z_lo = in_z - in_z_hi
        offset = col_z - block
        for t in range(16):
            here = offset == 4 * t
            z_hi[16 * t : 16 * t + 16, :] = jnp.where(here, in_z_hi, 0.0).astype(BF16)
            z_lo[16 * t : 16 * t + 16, :] = jnp.where(here, in_z_lo, 0.0).astype(BF16)
        wide = jnp.dot(vel_hi[...], z_hi[...], preferred_element_type=F32)
        wide += jnp.dot(vel_lo[...], z_hi[...], preferred_element_type=F32)
        wide += jnp.dot(vel_hi[...], z_lo[...], preferred_element_type=F32)
        in_xy = [basis[i][0:1] * in_y for i in range(4)]
        seen = []
        for d in range(3):
            mixed = None
            for i in range(4):
                start = 16 * (4 * d + i)
                term = in_xy[i] * wide[start : start + 16]
                mixed = term if mixed is None else mixed + term
            seen.append(jnp.sum(mixed, axis=0, keepdims=True))
        fluid = jnp.where(sub8 == 0, seen[0], jnp.where(sub8 == 1, seen[1], seen[2]))
        speed = pltpu.roll(field, 5, 0)
        keep = live & (sub8 < 3)
        relax = jnp.where(live[0:1], field[6:7], 1.0)
        force = jnp.where(keep, (fluid - speed) / relax, 0.0)
        base = jnp.where(keep, speed, 0.0)
        for p in range(2):
            base_ref[2 * j + p] = base[:, 128 * p : 128 * p + 128]
            acc_ref[2 * j + p] = force[:, 128 * p : 128 * p + 128]
        mass = field[7:8]
        push = -mass * force
        work = -mass * jnp.sum(force * base, axis=0, keepdims=True)
        sources = [push[0:1], push[1:2], push[2:3], work]
        for i in range(4):
            scaled = in_xy[i] * (weight_y * float(1.0 / WEIGHTS[i]))
            for d in range(4):
                high, low = split(sources[d] * scaled)
                start = 16 * (4 * d + i)
                a_hi[start : start + 16, :] = high
                a_lo[start : start + 16, :] = low
        lanes = (((1,), (1,)), ((), ()))
        out = lax.dot_general(a_hi[...], z_hi[...], lanes, preferred_element_type=F32)
        out += lax.dot_general(a_lo[...], z_hi[...], lanes, preferred_element_type=F32)
        out += lax.dot_general(a_hi[...], z_lo[...], lanes, preferred_element_type=F32)
        total[...] += out
        return carry

    lax.fori_loop(0, 7, chunk, 0)
    zpos = lax.broadcasted_iota(jnp.int32, (16, 256), 1) & 3
    weight_z = by_pos(zpos, 1.0 / WEIGHTS)
    for d in range(4):
        for i in range(4):
            start = 16 * (4 * d + i)
            dep_ref[d, i] = total[start : start + 16, :] * weight_z


def finish_kernel(u_ref, rate_ref, dep_ref, top_ref, base_ref, acc_ref, next_ref, vel_ref):
    top = jnp.max(jnp.max(top_ref[...], axis=0, keepdims=True), axis=1, keepdims=True)
    step = 1.0 / (7.0 * jnp.broadcast_to(top, (8, 256)))
    step16 = jnp.concatenate([step, step], axis=0)
    for v in range(5):
        for i in range(4):
            rate = rate_ref[v, i]
            if v > 0:
                rate = rate + dep_ref[v - 1, i]
            next_ref[v, i] = u_ref[v, i] + step16 * rate
    small = step[:, :128]
    for pair in range(14):
        value = base_ref[pair] + small * acc_ref[pair]
        for h in range(2):
            g = 2 * pair + h
            if g < 27:
                vel_ref[g // 9, g // 3 % 3, g % 3] = value[0:3, 64 * h : 64 * h + 64]


def shifted(value, axis, by):
    count = lax.axis_size(axis)
    return lax.ppermute(value, axis, [(i, (i + by) % count) for i in range(count)])


def call(kernel, outs, scratch=(), flops=10**6, nbytes=10**6):
    return pl.pallas_call(
        kernel,
        out_shape=outs,
        scratch_shapes=list(scratch),
        compiler_params=pltpu.CompilerParams(vmem_limit_bytes=VMEM_BYTES),
        cost_estimate=pl.CostEstimate(flops=flops, bytes_accessed=nbytes, transcendentals=0),
    )


def tiles_of(n):
    return jax.ShapeDtypeStruct((n, 8, 128), F32)


def local(fluid_state, parcel_data, host_element, slot_counts):
    x_up, x_down, keep_x, faces = call(pack_kernel, (tiles_of(30), tiles_of(30), tiles_of(9), tiles_of(14)))(
        fluid_state, parcel_data, host_element, slot_counts
    )
    x_low, x_high = shifted(x_up, "gx", 1), shifted(x_down, "gx", -1)
    y_up, y_down, keep_y = call(turn_y_kernel, (tiles_of(15), tiles_of(15), tiles_of(9)))(
        x_low, x_high, keep_x, faces, x_up
    )
    y_low, y_high = shifted(y_up, "gy", 1), shifted(y_down, "gy", -1)
    z_up, z_down, keep_z = call(turn_z_kernel, (tiles_of(12), tiles_of(12), tiles_of(9)))(
        y_low, y_high, keep_y, faces, y_up
    )
    z_low, z_high = shifted(z_up, "gz", 1), shifted(z_down, "gz", -1)
    top = jnp.maximum(jnp.maximum(z_low[TOP], z_high[TOP]), z_up[TOP])
    for axis in AXES:
        top = jnp.maximum(jnp.maximum(shifted(top, axis, 3), shifted(top, axis, -3)), top)
    field = jax.ShapeDtypeStruct((5, 4, 16, 256), F32)
    rate = call(
        rate_kernel, field, [pltpu.VMEM((5, 4, 16, 256), F32), pltpu.VMEM((2, 16, 256), F32)],
    )(fluid_state, x_low, x_high, y_low, y_high, z_low, z_high, faces)
    deposit, base, acc = call(
        parcel_kernel,
        (jax.ShapeDtypeStruct((4, 4, 16, 256), F32), tiles_of(14), tiles_of(14)),
        [
            pltpu.VMEM((28, 8, 128), F32),
            pltpu.VMEM((192, 256), BF16),
            pltpu.VMEM((192, 256), BF16),
            pltpu.VMEM((256, 256), BF16),
            pltpu.VMEM((256, 256), BF16),
            pltpu.VMEM((256, 256), BF16),
            pltpu.VMEM((256, 256), BF16),
            pltpu.VMEM((256, 256), F32),
        ],
    )(fluid_state, z_low, z_high, keep_z)
    return call(finish_kernel, (field, jax.ShapeDtypeStruct((3, 3, 3, 3, 64), F32)))(
        fluid_state, rate, deposit, top, base, acc
    )


def solution(mesh):
    placed = (
        P(None, "gx", "gy", "gz"),
        P("gx", "gy", "gz", None, None),
        P("gx", "gy", "gz", None),
        P("gx", "gy", "gz"),
    )
    return jax.shard_map(
        local,
        mesh=mesh,
        in_specs=placed,
        out_specs=(P(None, "gx", "gy", "gz"), P("gx", "gy", "gz", None, None)),
        check_vma=False,
    )
```

time: 254 us -> 77.7 us (0.31)
  blocking collectives: 106 us -> 0 us
  local copies, waits for them, and re-layouts: 65 us -> 3.28 us
  other arithmetic: 31.9 us -> 0.02 us
  starting transfers between devices: 33 us -> 49.1 us
  waiting for transfers between devices: 2.83 us -> 16.7 us
  matrix products: 10.1 us -> 0 us
  Pallas kernels: 0 us -> 7.31 us
    pmax x1 -> x0, blocking collectives: 106 us -> none  [local(): global_top = lax.pmax(local_top, ('gx', 'gy', 'gz'))]
    reshape x8 -> x0, local copies, waits for them, and re-layouts: 24.8 us -> none  [the longest x2 13.1 us: local(): deposit = deposit.reshape((4, 4, 4, 4, counts_elem[0], counts_elem[1], co...]
    ppermute x12, starting transfers between devices: 33 us -> 49.1 us  [shifted(): lax.ppermute(value, axis, [(i, (i + by) % count) for i in range(count)])]
    ppermute x12, waiting for transfers between devices: 2.83 us -> 16.7 us  [shifted(): lax.ppermute(value, axis, [(i, (i + by) % count) for i in range(count)])]
    unnamed x1 -> x0, other arithmetic: 11.6 us -> none
    slice x15 -> x0, local copies, waits for them, and re-layouts: 11.2 us -> none  [the longest x3 3.75 us: surface_term(): right_side = lax.slice_in_dim(padded, 1, 4 * elem_along + 2, 4, axis_pos)]
    dot_general x4 -> x0, matrix products: 10.1 us -> none  [the longest x3 6.07 us: along_nodes(): jnp.tensordot(field_data.reshape(split_shape), derivative, axes=([axis_po...]
    pallas_call x0 -> x6, Pallas kernels: none -> 7.31 us  [the longest x1 5.01 us: local(): call(parcel_kernel, (jax.ShapeDtypeStruct((4, 4, 16, 256), F32), tiles_of...]
  transfers between devices with their start and end apart: 12 -> 12, of which waited for: 1 -> 5; matrix products, arithmetic and copies ran while one was open for 34% -> 0% of each run, Pallas kernels for 0% -> 8%
where the time goes in v1:
time: 77.7 us; the launch traced here: 77.2 us
  starting transfers between devices  49.1 us (63%)
  waiting for transfers between devices  16.7 us (21%)
  Pallas kernels  7.31 us (9%)
  local copies, waits for them, and re-layouts  3.28 us (4%)
  between operations  0.81 us (1%)
    ppermute x12, starting transfers between devices, shifted(): lax.ppermute(value, axis, [(i, (i + by) % count) for i in range(count)])  49.1 us
    ppermute x12, waiting for transfers between devices, shifted(): lax.ppermute(value, axis, [(i, (i + by) % count) for i in range(count)])  16.7 us
    pallas_call x1, Pallas kernels, local(): call(parcel_kernel, (jax.ShapeDtypeStruct((4, 4, 16, 256), F32), tiles_of...  5.01 us
    unnamed x10, local copies, waits for them, and re-layouts  3.28 us
  transfers between devices with their start and end apart: 12, of which 5 were waited for; matrix products, arithmetic and copies ran while one was open for 0% of the time, Pallas kernels for 8%

profile of v1, /device:TPU:1, one launch (start us, length us, event | category | flops | bytes accessed | tf_op | source)
XLA Modules:
  0.0 77.2 jit_solution(14855454133368470590)
XLA Ops:
  0.6 1.0 %copy-done = f32[5,4,16,256]{3,2,1,0:T(8,128)S(1)} copy-done((f32[5,4,16,256]{3,2,1,0:T(8,128)S(1)}, f32[5,4,16,256]{3,2,1,0:T(8,128)}, u32[]{:S(2)}) %copy-start) | copy-done | bytes 327704
  1.6 0.9 %copy-done.2 = f32[3,3,3,8,64]{4,3,2,1,0:T(8,128)S(1)} copy-done((f32[3,3,3,8,64]{4,3,2,1,0:T(8,128)S(1)}, f32[3,3,3,8,64]{4,3,2,1,0:T(8,128)}, u32[]{:S(2)}) %copy-start.2) | copy-done | bytes 55320
  2.5 0.7 copy-done.3
  3.2 0.7 copy-done.4
  4.2 11.5 %collective-permute-start.1 = (f32[30,8,128]{2,1,0:T(8,128)S(1)}, f32[30,8,128]{2,1,0:T(8,128)S(1)}, u32[]{:S(2)}, u32[]{:S(2)}) collective-permute-start(f32[30,8,128]{2,1,0:T(8,128)S(1)} %get-tuple-element.16), channel_id=1, source_target_pairs={{0,448},{64,0},{128,64},{192,128},{256,192},{320,256},{384,320},{4... | collective-permute-start | bytes 368648 | tf_op jit(solution)/shard_map/ppermute | solution.py:388
  15.7 1.9 %collective-permute-start = (f32[30,8,128]{2,1,0:T(8,128)S(1)}, f32[30,8,128]{2,1,0:T(8,128)S(1)}, u32[]{:S(2)}, u32[]{:S(2)}) collective-permute-start(f32[30,8,128]{2,1,0:T(8,128)S(1)} %get-tuple-element.15.mine_ref), channel_id=1, source_target_pairs={{0,64},{64,128},{128,192},{192,256},{256,320},{320,384},{384,448},... | collective-permute-start | bytes 368648 | tf_op jit(solution)/shard_map/ppermute | solution.py:388
  17.6 4.9 %collective-permute-done.lo_ref.xl_ref = f32[30,8,128]{2,1,0:T(8,128)S(1)} collective-permute-done((f32[30,8,128]{2,1,0:T(8,128)S(1)}, f32[30,8,128]{2,1,0:T(8,128)S(1)}, u32[]{:S(2)}, u32[]{:S(2)}) %collective-permute-start) | collective-permute-done | bytes 122912 | tf_op jit(solution)/shard_map/ppermute | solution.py:388
  22.5 5.2 %collective-permute-start.3 = (f32[15,8,128]{2,1,0:T(8,128)S(1)}, f32[15,8,128]{2,1,0:T(8,128)S(1)}, u32[]{:S(2)}, u32[]{:S(2)}) collective-permute-start(f32[15,8,128]{2,1,0:T(8,128)S(1)} %get-tuple-element.20), channel_id=1, source_target_pairs={{0,56},{8,0},{16,8},{24,16},{32,24},{40,32},{48,40},{56,48},{1,57}... | collective-permute-start | bytes 184328 | tf_op jit(solution)/shard_map/ppermute | solution.py:388
  27.8 1.9 %collective-permute-start.2 = (f32[15,8,128]{2,1,0:T(8,128)S(1)}, f32[15,8,128]{2,1,0:T(8,128)S(1)}, u32[]{:S(2)}, u32[]{:S(2)}) collective-permute-start(f32[15,8,128]{2,1,0:T(8,128)S(1)} %get-tuple-element.19.mine_ref), channel_id=1, source_target_pairs={{0,8},{8,16},{16,24},{24,32},{32,40},{40,48},{48,56},{56,0},{1,9},... | collective-permute-start | bytes 184328 | tf_op jit(solution)/shard_map/ppermute | solution.py:388
  29.7 4.2 %collective-permute-done.2.lo_ref.yl_ref = f32[15,8,128]{2,1,0:T(8,128)S(1)} collective-permute-done((f32[15,8,128]{2,1,0:T(8,128)S(1)}, f32[15,8,128]{2,1,0:T(8,128)S(1)}, u32[]{:S(2)}, u32[]{:S(2)}) %collective-permute-start.2) | collective-permute-done | bytes 61472 | tf_op jit(solution)/shard_map/ppermute | solution.py:388
  34.0 3.5 %collective-permute-start.5 = (f32[12,8,128]{2,1,0:T(8,128)S(1)}, f32[12,8,128]{2,1,0:T(8,128)S(1)}, u32[]{:S(2)}, u32[]{:S(2)}) collective-permute-start(f32[12,8,128]{2,1,0:T(8,128)S(1)} %get-tuple-element.23), channel_id=1, source_target_pairs={{0,7},{1,0},{2,1},{3,2},{4,3},{5,4},{6,5},{7,6},{8,15},{9,8},{10,9... | collective-permute-start | bytes 147464 | tf_op jit(solution)/shard_map/ppermute | solution.py:388
  37.5 1.1 %collective-permute-start.4 = (f32[12,8,128]{2,1,0:T(8,128)S(1)}, f32[12,8,128]{2,1,0:T(8,128)S(1)}, u32[]{:S(2)}, u32[]{:S(2)}) collective-permute-start(f32[12,8,128]{2,1,0:T(8,128)S(1)} %get-tuple-element.22), channel_id=1, source_target_pairs={{0,1},{1,2},{2,3},{3,4},{4,5},{5,6},{6,7},{7,0},{8,9},{9,10},{10,1... | collective-permute-start | bytes 147464 | tf_op jit(solution)/shard_map/ppermute | solution.py:388
  38.6 1.8 %collective-permute-done.5.zh_ref = f32[12,8,128]{2,1,0:T(8,128)S(1)} collective-permute-done((f32[12,8,128]{2,1,0:T(8,128)S(1)}, f32[12,8,128]{2,1,0:T(8,128)S(1)}, u32[]{:S(2)}, u32[]{:S(2)}) %collective-permute-start.5) | collective-permute-done | bytes 49184 | tf_op jit(solution)/shard_map/ppermute | solution.py:388
  40.4 1.9 %collective-permute-start.7 = (f32[8,128]{1,0:T(8,128)S(1)}, f32[8,128]{1,0:T(8,128)S(1)}, u32[]{:S(2)}, u32[]{:S(2)}) collective-permute-start(f32[8,128]{1,0:T(8,128)S(1)} %fusion.1), channel_id=1, source_target_pairs={{0,320},{64,384},{128,448},{192,0},{256,64},{320,128},{384,192},{4... | collective-permute-start | bytes 12296 | tf_op jit(solution)/shard_map/ppermute | solution.py:388
  42.3 5.2 %collective-permute-start.6 = (f32[8,128]{1,0:T(8,128)S(1)}, f32[8,128]{1,0:T(8,128)S(1)}, u32[]{:S(2)}, u32[]{:S(2)}) collective-permute-start(f32[8,128]{1,0:T(8,128)S(1)} %fusion.1), channel_id=1, source_target_pairs={{0,192},{64,256},{128,320},{192,384},{256,448},{320,0},{384,64},{4... | collective-permute-start | bytes 12296 | tf_op jit(solution)/shard_map/ppermute | solution.py:388
  47.5 2.2 %collective-permute-done.6 = f32[8,128]{1,0:T(8,128)S(1)} collective-permute-done((f32[8,128]{1,0:T(8,128)S(1)}, f32[8,128]{1,0:T(8,128)S(1)}, u32[]{:S(2)}, u32[]{:S(2)}) %collective-permute-start.6) | collective-permute-done | bytes 4128 | tf_op jit(solution)/shard_map/ppermute | solution.py:388
  49.7 3.3 %collective-permute-start.9 = (f32[8,128]{1,0:T(8,128)S(1)}, f32[8,128]{1,0:T(8,128)S(1)}, u32[]{:S(2)}, u32[]{:S(2)}) collective-permute-start(f32[8,128]{1,0:T(8,128)S(1)} %maximum_maximum_fusion.2), channel_id=1, source_target_pairs={{0,40},{8,48},{16,56},{24,0},{32,8},{40,16},{48,24},{56,32},{1,41}... | collective-permute-start | bytes 12296 | tf_op jit(solution)/shard_map/ppermute | solution.py:388
  53.0 3.7 %collective-permute-start.8 = (f32[8,128]{1,0:T(8,128)S(1)}, f32[8,128]{1,0:T(8,128)S(1)}, u32[]{:S(2)}, u32[]{:S(2)}) collective-permute-start(f32[8,128]{1,0:T(8,128)S(1)} %maximum_maximum_fusion.2), channel_id=1, source_target_pairs={{0,24},{8,32},{16,40},{24,48},{32,56},{40,0},{48,8},{56,16},{1,25}... | collective-permute-start | bytes 12296 | tf_op jit(solution)/shard_map/ppermute | solution.py:388
  56.8 3.6 %collective-permute-done.8 = f32[8,128]{1,0:T(8,128)S(1)} collective-permute-done((f32[8,128]{1,0:T(8,128)S(1)}, f32[8,128]{1,0:T(8,128)S(1)}, u32[]{:S(2)}, u32[]{:S(2)}) %collective-permute-start.8) | collective-permute-done | bytes 4128 | tf_op jit(solution)/shard_map/ppermute | solution.py:388
  60.4 7.5 %collective-permute-start.11 = (f32[8,128]{1,0:T(8,128)S(1)}, f32[8,128]{1,0:T(8,128)S(1)}, u32[]{:S(2)}, u32[]{:S(2)}) collective-permute-start(f32[8,128]{1,0:T(8,128)S(1)} %maximum_maximum_fusion.1), channel_id=1, source_target_pairs={{0,5},{1,6},{2,7},{3,0},{4,1},{5,2},{6,3},{7,4},{8,13},{9,14},{10,... | collective-permute-start | bytes 12296 | tf_op jit(solution)/shard_map/ppermute | solution.py:388
  67.9 2.2 %collective-permute-start.10 = (f32[8,128]{1,0:T(8,128)S(1)}, f32[8,128]{1,0:T(8,128)S(1)}, u32[]{:S(2)}, u32[]{:S(2)}) collective-permute-start(f32[8,128]{1,0:T(8,128)S(1)} %maximum_maximum_fusion.1), channel_id=1, source_target_pairs={{0,3},{1,4},{2,5},{3,6},{4,7},{5,0},{6,1},{7,2},{8,11},{9,12},{10,... | collective-permute-start | bytes 12296 | tf_op jit(solution)/shard_map/ppermute | solution.py:388
  70.1 1.1 %shard_map.62.rate_ref = f32[5,4,16,256]{3,2,1,0:T(8,128)S(1)} custom-call(f32[5,4,16,256]{3,2,1,0:T(8,128)S(1)} %copy-done.1, f32[30,8,128]{2,1,0:T(8,128)S(1)} %collective-permute-done.lo_ref.xl_ref, f32[30,8,128]{2,1,0:T(8,128)S(1)} %collective-permute-done.1.hi_ref.xh_ref, f32[15,8,128]{2,1,0:T(8,128)S(1)} %collective-permute-done.2.lo_ref.yl_ref, ...), custom_call_target="tpu_custom_call" | custom-call | flops 1000000 | bytes 1000000 | tf_op jit(solution)/shard_map/pallas_call | solution.py:422
  71.2 5.0 %shard_map.63 = (f32[4,4,16,256]{3,2,1,0:T(8,128)S(1)}, f32[14,8,128]{2,1,0:T(8,128)S(1)}, f32[14,8,128]{2,1,0:T(8,128)S(1)}) custom-call(f32[5,4,16,256]{3,2,1,0:T(8,128)S(1)} %copy-done.1, f32[12,8,128]{2,1,0:T(8,128)S(1)} %collective-permute-done.4.zl_ref, f32[12,8,128]{2,1,0:T(8,128)S(1)} %collective-permute-done.5.zh_ref, ...), custom_call_target="tpu_custom_call" | custom-call | flops 1000000 | bytes 1000000 | tf_op jit(solution)/shard_map/pallas_call | solution.py:425
  76.3 0.9 %shard_map.64 = (f32[5,4,16,256]{3,2,1,0:T(8,128)}, f32[3,3,3,3,64]{4,3,2,1,0:T(4,128)}) custom-call(f32[5,4,16,256]{3,2,1,0:T(8,128)S(1)} %copy-done.1, f32[5,4,16,256]{3,2,1,0:T(8,128)S(1)} %shard_map.62.rate_ref, f32[4,4,16,256]{3,2,1,0:T(8,128)S(1)} %get-tuple-element.25.dep_ref, f32[8,128]{1,0:T(8,128)S(1)} %maximum_maximum_fusion.top_ref, ...), custom_call_target="tpu_custom_call" | custom-call | flops 1000000 | bytes 1000000 | tf_op jit(solution)/shard_map/pallas_call | solution.py:439
  (20 shorter events, 0.3 us)
Async XLA Ops:
  0.6 1.0 %copy-start = (f32[5,4,16,256]{3,2,1,0:T(8,128)S(1)}, f32[5,4,16,256]{3,2,1,0:T(8,128)}, u32[]{:S(2)}) copy-start(f32[5,4,16,256]{3,2,1,0:T(8,128)} %u_ref.7) | copy-start | bytes 983044
  1.6 0.9 %copy-start.2 = (f32[3,3,3,8,64]{4,3,2,1,0:T(8,128)S(1)}, f32[3,3,3,8,64]{4,3,2,1,0:T(8,128)}, u32[]{:S(2)}) copy-start(f32[3,3,3,8,64]{4,3,2,1,0:T(8,128)} %data_ref.1) | copy-start | bytes 165892
  2.5 0.7 copy-start.3
  3.2 0.7 copy-start.4
  4.2 13.4 %collective-permute-start.1 = (f32[30,8,128]{2,1,0:T(8,128)S(1)}, f32[30,8,128]{2,1,0:T(8,128)S(1)}, u32[]{:S(2)}, u32[]{:S(2)}) collective-permute-start(f32[30,8,128]{2,1,0:T(8,128)S(1)} %get-tuple-element.16), channel_id=1, source_target_pairs={{0,448},{64,0},{128,64},{192,128},{256,192},{320,256},{384,320},{4... | collective-permute-start | bytes 368648 | tf_op jit(solution)/shard_map/ppermute | solution.py:388
  15.7 6.8 %collective-permute-start = (f32[30,8,128]{2,1,0:T(8,128)S(1)}, f32[30,8,128]{2,1,0:T(8,128)S(1)}, u32[]{:S(2)}, u32[]{:S(2)}) collective-permute-start(f32[30,8,128]{2,1,0:T(8,128)S(1)} %get-tuple-element.15.mine_ref), channel_id=1, source_target_pairs={{0,64},{64,128},{128,192},{192,256},{256,320},{320,384},{384,448},... | collective-permute-start | bytes 368648 | tf_op jit(solution)/shard_map/ppermute | solution.py:388
  22.5 47.6 %copy-start.1 = (f32[5,4,16,256]{3,2,1,0:T(8,128)S(1)}, f32[5,4,16,256]{3,2,1,0:T(8,128)}, u32[]{:S(2)}) copy-start(f32[5,4,16,256]{3,2,1,0:T(8,128)} %u_ref.7) | copy-start | bytes 983044
  22.5 7.2 %collective-permute-start.3 = (f32[15,8,128]{2,1,0:T(8,128)S(1)}, f32[15,8,128]{2,1,0:T(8,128)S(1)}, u32[]{:S(2)}, u32[]{:S(2)}) collective-permute-start(f32[15,8,128]{2,1,0:T(8,128)S(1)} %get-tuple-element.20), channel_id=1, source_target_pairs={{0,56},{8,0},{16,8},{24,16},{32,24},{40,32},{48,40},{56,48},{1,57}... | collective-permute-start | bytes 184328 | tf_op jit(solution)/shard_map/ppermute | solution.py:388
  27.8 6.2 %collective-permute-start.2 = (f32[15,8,128]{2,1,0:T(8,128)S(1)}, f32[15,8,128]{2,1,0:T(8,128)S(1)}, u32[]{:S(2)}, u32[]{:S(2)}) collective-permute-start(f32[15,8,128]{2,1,0:T(8,128)S(1)} %get-tuple-element.19.mine_ref), channel_id=1, source_target_pairs={{0,8},{8,16},{16,24},{24,32},{32,40},{40,48},{48,56},{56,0},{1,9},... | collective-permute-start | bytes 184328 | tf_op jit(solution)/shard_map/ppermute | solution.py:388
  34.0 6.4 %collective-permute-start.5 = (f32[12,8,128]{2,1,0:T(8,128)S(1)}, f32[12,8,128]{2,1,0:T(8,128)S(1)}, u32[]{:S(2)}, u32[]{:S(2)}) collective-permute-start(f32[12,8,128]{2,1,0:T(8,128)S(1)} %get-tuple-element.23), channel_id=1, source_target_pairs={{0,7},{1,0},{2,1},{3,2},{4,3},{5,4},{6,5},{7,6},{8,15},{9,8},{10,9... | collective-permute-start | bytes 147464 | tf_op jit(solution)/shard_map/ppermute | solution.py:388
  37.5 2.9 %collective-permute-start.4 = (f32[12,8,128]{2,1,0:T(8,128)S(1)}, f32[12,8,128]{2,1,0:T(8,128)S(1)}, u32[]{:S(2)}, u32[]{:S(2)}) collective-permute-start(f32[12,8,128]{2,1,0:T(8,128)S(1)} %get-tuple-element.22), channel_id=1, source_target_pairs={{0,1},{1,2},{2,3},{3,4},{4,5},{5,6},{6,7},{7,0},{8,9},{9,10},{10,1... | collective-permute-start | bytes 147464 | tf_op jit(solution)/shard_map/ppermute | solution.py:388
  40.4 7.1 %collective-permute-start.7 = (f32[8,128]{1,0:T(8,128)S(1)}, f32[8,128]{1,0:T(8,128)S(1)}, u32[]{:S(2)}, u32[]{:S(2)}) collective-permute-start(f32[8,128]{1,0:T(8,128)S(1)} %fusion.1), channel_id=1, source_target_pairs={{0,320},{64,384},{128,448},{192,0},{256,64},{320,128},{384,192},{4... | collective-permute-start | bytes 12296 | tf_op jit(solution)/shard_map/ppermute | solution.py:388
  42.3 7.4 %collective-permute-start.6 = (f32[8,128]{1,0:T(8,128)S(1)}, f32[8,128]{1,0:T(8,128)S(1)}, u32[]{:S(2)}, u32[]{:S(2)}) collective-permute-start(f32[8,128]{1,0:T(8,128)S(1)} %fusion.1), channel_id=1, source_target_pairs={{0,192},{64,256},{128,320},{192,384},{256,448},{320,0},{384,64},{4... | collective-permute-start | bytes 12296 | tf_op jit(solution)/shard_map/ppermute | solution.py:388
  49.7 7.1 %collective-permute-start.9 = (f32[8,128]{1,0:T(8,128)S(1)}, f32[8,128]{1,0:T(8,128)S(1)}, u32[]{:S(2)}, u32[]{:S(2)}) collective-permute-start(f32[8,128]{1,0:T(8,128)S(1)} %maximum_maximum_fusion.2), channel_id=1, source_target_pairs={{0,40},{8,48},{16,56},{24,0},{32,8},{40,16},{48,24},{56,32},{1,41}... | collective-permute-start | bytes 12296 | tf_op jit(solution)/shard_map/ppermute | solution.py:388
  53.0 7.4 %collective-permute-start.8 = (f32[8,128]{1,0:T(8,128)S(1)}, f32[8,128]{1,0:T(8,128)S(1)}, u32[]{:S(2)}, u32[]{:S(2)}) collective-permute-start(f32[8,128]{1,0:T(8,128)S(1)} %maximum_maximum_fusion.2), channel_id=1, source_target_pairs={{0,24},{8,32},{16,40},{24,48},{32,56},{40,0},{48,8},{56,16},{1,25}... | collective-permute-start | bytes 12296 | tf_op jit(solution)/shard_map/ppermute | solution.py:388
  60.4 15.9 %collective-permute-start.11 = (f32[8,128]{1,0:T(8,128)S(1)}, f32[8,128]{1,0:T(8,128)S(1)}, u32[]{:S(2)}, u32[]{:S(2)}) collective-permute-start(f32[8,128]{1,0:T(8,128)S(1)} %maximum_maximum_fusion.1), channel_id=1, source_target_pairs={{0,5},{1,6},{2,7},{3,0},{4,1},{5,2},{6,3},{7,4},{8,13},{9,14},{10,... | collective-permute-start | bytes 12296 | tf_op jit(solution)/shard_map/ppermute | solution.py:388
  67.9 8.4 %collective-permute-start.10 = (f32[8,128]{1,0:T(8,128)S(1)}, f32[8,128]{1,0:T(8,128)S(1)}, u32[]{:S(2)}, u32[]{:S(2)}) collective-permute-start(f32[8,128]{1,0:T(8,128)S(1)} %maximum_maximum_fusion.1), channel_id=1, source_target_pairs={{0,3},{1,4},{2,5},{3,6},{4,7},{5,0},{6,1},{7,2},{8,11},{9,12},{10,... | collective-permute-start | bytes 12296 | tf_op jit(solution)/shard_map/ppermute | solution.py:388

commit v2 on v1

v2 whole, which is shorter than its diff:
```python
import jax
import jax.numpy as jnp
import numpy as np
from jax import lax
from jax.experimental import pallas as pl
from jax.experimental.pallas import tpu as pltpu
from jax.sharding import PartitionSpec as P

F32 = jnp.float32
BF16 = jnp.bfloat16
VMEM_BYTES = 24 * 1024 * 1024

NODES = np.array([-1.0, -1.0 / np.sqrt(5.0), 1.0 / np.sqrt(5.0), 1.0])
WEIGHTS = np.array([1.0 / 6.0, 5.0 / 6.0, 5.0 / 6.0, 1.0 / 6.0])


def derivative_table():
    factor = [np.prod([NODES[i] - NODES[j] for j in range(4) if j != i]) for i in range(4)]
    table = np.zeros((4, 4))
    for i in range(4):
        for j in range(4):
            if i != j:
                table[i, j] = factor[i] / (factor[j] * (NODES[i] - NODES[j]))
    return table


DERIV = derivative_table()
SCALE = [1.0 / np.prod([NODES[i] - NODES[j] for j in range(4) if j != i]) for i in range(4)]

FACE = 9


def by_pos(pos, values):
    out = jnp.full(pos.shape, float(values[3]), F32)
    for k in range(3):
        out = jnp.where(pos == k, float(values[k]), out)
    return out


def primitives(state):
    inverse = 1.0 / state[0]
    vel = [state[d + 1] * inverse for d in range(3)]
    square = vel[0] * vel[0] + vel[1] * vel[1] + vel[2] * vel[2]
    pressure = 0.4 * (state[4] - 0.5 * state[0] * square)
    sound = jnp.sqrt(1.4 * pressure * inverse)
    return vel, pressure, sound, square


def flux(state, vel, pressure, d):
    normal = vel[d]
    out = [state[d + 1]]
    for k in range(3):
        term = state[k + 1] * normal
        out.append(term + pressure if k == d else term)
    out.append((state[4] + pressure) * normal)
    return out


def side(state, d):
    vel, pressure, sound, _ = primitives(state)
    return flux(state, vel, pressure, d), jnp.abs(vel[d]) + sound


def parity(axis):
    return lax.axis_index(axis) & 1


def lows_highs(axis, first_ref, second_ref):
    odd = jnp.full((8, 128), parity(axis), jnp.int32) == 1

    def low(tile):
        return jnp.where(odd, first_ref[tile], second_ref[tile])

    def high(tile):
        return jnp.where(odd, second_ref[tile], first_ref[tile])

    return low, high


def pack_kernel(u_hbm, data_hbm, host_hbm, count_hbm, first_ref, second_ref, keep_ref, face_ref, top_ref, u_ref, data_ref, host_ref, count_ref, sems):
    copies = [
        pltpu.make_async_copy(source, target, sems.at[k])
        for k, (source, target) in enumerate(
            ((u_hbm, u_ref), (data_hbm, data_ref), (host_hbm, host_ref), (count_hbm, count_ref))
        )
    ]
    for copy in copies:
        copy.start()
    for copy in copies:
        copy.wait()
    top = None
    for i in range(4):
        _, _, sound, square = primitives([u_ref[v, i] for v in range(5)])
        speed = jnp.sqrt(square) + sound
        top = speed if top is None else jnp.maximum(top, speed)
    top = jnp.maximum(top[:, :128], top[:, 128:])
    top_ref[...] = jnp.broadcast_to(jnp.max(top, axis=0, keepdims=True), (8, 128))
    slot = lax.broadcasted_iota(jnp.int32, (1, 64), 1)
    odd = parity("gx")
    for a, out in ((2 - 2 * odd, first_ref), (2 * odd, second_ref), (1, keep_ref)):
        for b in range(3):
            for c in range(3):
                count = count_ref[a, b : b + 1, c : c + 1]
                host = host_ref[a, b, c : c + 1, :]
                code = jnp.where(slot < count, host + 1, 0).astype(F32)
                out[3 * b + c, :, 0:64] = data_ref[a, b, c]
                out[3 * b + c, :, 64:128] = jnp.broadcast_to(code, (8, 64))
    for v in range(5):
        for yh in range(2):
            for zh in range(2):
                tile = FACE + 4 * v + 2 * yh + zh
                ys, zs = slice(8 * yh, 8 * yh + 8), slice(128 * zh, 128 * zh + 128)
                first_ref[tile] = u_ref[v, 3 - 3 * odd, ys, zs]
                second_ref[tile] = u_ref[v, 3 * odd, ys, zs]
        for i in range(4):
            for zh in range(2):
                zs = slice(128 * zh, 128 * zh + 128)
                row = 4 * zh + i
                face_ref[v, row : row + 1, :] = u_ref[v, i, 15:16, zs]
                face_ref[5 + v, row : row + 1, :] = u_ref[v, i, 0:1, zs]
    lane = lax.broadcasted_iota(jnp.int32, (16, 128), 1)
    high = jnp.zeros((16, 128), F32)
    low = jnp.zeros((16, 128), F32)
    for v in range(5):
        for i in range(4):
            here = lane == 4 * v + i
            high = jnp.where(here, u_ref[v, i, :, 255:256], high)
            low = jnp.where(here, u_ref[v, i, :, 0:1], low)
    for yh in range(2):
        face_ref[10 + yh] = high[8 * yh : 8 * yh + 8]
        face_ref[12 + yh] = low[8 * yh : 8 * yh + 8]


def turn_y_kernel(x1_ref, x2_ref, own_ref, face_ref, tops_ref, first_ref, second_ref, keep_ref, top_ref):
    top_ref[...] = jnp.max(tops_ref[...], axis=0, keepdims=True)
    low, high = lows_highs("gx", x1_ref, x2_ref)
    odd = parity("gy")
    for a, source in enumerate((low, lambda t: own_ref[t], high)):
        for c in range(3):
            first_ref[3 * a + c] = source(6 - 6 * odd + c)
            second_ref[3 * a + c] = source(6 * odd + c)
            keep_ref[3 * a + c] = source(3 + c)
    for v in range(5):
        first_ref[FACE + v] = face_ref[v + 5 * odd]
        second_ref[FACE + v] = face_ref[v + 5 - 5 * odd]


def turn_z_kernel(y1_ref, y2_ref, own_ref, face_ref, tops_ref, first_ref, second_ref, keep_ref, top_ref):
    top_ref[...] = jnp.max(tops_ref[...], axis=0, keepdims=True)
    low, high = lows_highs("gy", y1_ref, y2_ref)
    odd = parity("gz")
    for b, source in enumerate((low, lambda t: own_ref[t], high)):
        for a in range(3):
            first_ref[3 * a + b] = source(3 * a + 2 - 2 * odd)
            second_ref[3 * a + b] = source(3 * a + 2 * odd)
            keep_ref[3 * a + b] = source(3 * a + 1)
    for yh in range(2):
        first_ref[FACE + yh] = face_ref[10 + 2 * odd + yh]
        second_ref[FACE + yh] = face_ref[12 - 2 * odd + yh]


def wall(axis, last, own, received, sign_of):
    at = lax.axis_index(axis) == (lax.axis_size(axis) - 1 if last else 0)
    pick = jnp.full(received[0].shape, at.astype(jnp.int32), jnp.int32) == 1
    return [jnp.where(pick, sign_of(v) * own[v], received[v]) for v in range(5)]


def shift_rate(state, fluxes, speed, low, high, axis, pos, first, last, coef):
    count = state[0].shape[axis]
    low_state, low_flux, low_speed = low
    high_state, high_flux, high_speed = high
    at_low = pos == 0
    ends = at_low | (pos == 3)

    def beside(here, below, above):
        near = jnp.where(at_low, pltpu.roll(here, 1, axis), pltpu.roll(here, count - 1, axis))
        return jnp.where(first, below, jnp.where(last, above, near))

    spread = jnp.maximum(speed, beside(speed, low_speed, high_speed))
    spread = jnp.where(ends, 3.0 * spread, 0.0)
    out = []
    for v in range(5):
        value = fluxes[v]
        above = jnp.where(last, high_flux[v], pltpu.roll(value, count - 1, axis))
        below = jnp.where(first, low_flux[v], pltpu.roll(value, 1, axis))
        total = coef[1] * above + coef[-1] * below
        for d in (-3, -2, 2, 3):
            total = total + coef[d] * pltpu.roll(value, -d % count, axis)
        out.append(spread * (beside(state[v], low_state[v], high_state[v]) - state[v]) - total)
    return out


def rate_kernel(u_ref, x1_ref, x2_ref, y1_ref, y2_ref, z1_ref, z2_ref, face_ref, rate_ref, fx_ref, sx_ref):
    x_side = lows_highs("gx", x1_ref, x2_ref)
    y_side = lows_highs("gy", y1_ref, y2_ref)
    z_side = lows_highs("gz", z1_ref, z2_ref)
    shape = (16, 256)
    row = lax.broadcasted_iota(jnp.int32, shape, 0)
    lane = lax.broadcasted_iota(jnp.int32, shape, 1)
    ypos, zpos = row & 3, lane & 3

    def coefs(pos):
        out = {}
        for d in (-3, -2, -1, 1, 2, 3):
            values = [DERIV[k, k + d] if 0 <= k + d < 4 else 0.0 for k in range(4)]
            if d == 1:
                values[3] = 3.0
            if d == -1:
                values[0] = -3.0
            out[d] = by_pos(pos, values)
        return out

    ycoef, zcoef = coefs(ypos), coefs(zpos)
    yfirst, ylast = row == 0, row == 15
    zfirst, zlast = lane == 0, lane == 255

    yflip = lambda v: -1.0 if v == 2 else 1.0
    ylow = wall("gy", False, [face_ref[5 + v] for v in range(5)], [y_side[0](FACE + v) for v in range(5)], yflip)
    yhigh = wall("gy", True, [face_ref[v] for v in range(5)], [y_side[1](FACE + v) for v in range(5)], yflip)
    ylow_flux, ylow_speed = side(ylow, 1)
    yhigh_flux, yhigh_speed = side(yhigh, 1)

    def columns(first_tile, source):
        both = jnp.concatenate([source(first_tile), source(first_tile + 1)], axis=0)
        return [both if v == 0 else pltpu.roll(both, 128 - 4 * v, 1) for v in range(5)]

    own = lambda t: face_ref[t]
    zflip = lambda v: -1.0 if v == 3 else 1.0
    zlow = wall("gz", False, columns(12, own), columns(FACE, z_side[0]), zflip)
    zhigh = wall("gz", True, columns(10, own), columns(FACE, z_side[1]), zflip)
    zlow_flux, zlow_speed = side(zlow, 2)
    zhigh_flux, zhigh_speed = side(zhigh, 2)

    def pick_row(tile, i):
        return jnp.concatenate([tile[i : i + 1], tile[4 + i : 5 + i]], axis=1)

    for i in range(4):
        state = [u_ref[v, i] for v in range(5)]
        vel, pressure, sound, _ = primitives(state)
        xflux = flux(state, vel, pressure, 0)
        for v in range(5):
            fx_ref[v, i] = xflux[v]
        if i in (0, 3):
            sx_ref[i // 3] = jnp.abs(vel[0]) + sound
        low = ([pick_row(t, i) for t in ylow], [pick_row(t, i) for t in ylow_flux], pick_row(ylow_speed, i))
        high = ([pick_row(t, i) for t in yhigh], [pick_row(t, i) for t in yhigh_flux], pick_row(yhigh_speed, i))
        yrate = shift_rate(
            state, flux(state, vel, pressure, 1), jnp.abs(vel[1]) + sound,
            low, high, 0, ypos, yfirst, ylast, ycoef,
        )
        pick = lambda t: t[:, i : i + 1]
        low = ([pick(t) for t in zlow], [pick(t) for t in zlow_flux], pick(zlow_speed))
        high = ([pick(t) for t in zhigh], [pick(t) for t in zhigh_flux], pick(zhigh_speed))
        zrate = shift_rate(
            state, flux(state, vel, pressure, 2), jnp.abs(vel[2]) + sound,
            low, high, 1, zpos, zfirst, zlast, zcoef,
        )
        for v in range(5):
            rate_ref[v, i] = yrate[v] + zrate[v]

    xflip = lambda v: -1.0 if v == 1 else 1.0
    for half in range(2):
        for part in range(2):
            ys, zs = slice(8 * half, 8 * half + 8), slice(128 * part, 128 * part + 128)
            tile = FACE + 2 * half + part
            ends = []
            for last, i, source in ((False, 0, x_side[0]), (True, 3, x_side[1])):
                mine = [u_ref[v, i, ys, zs] for v in range(5)]
                beyond = wall("gx", last, mine, [source(tile + 4 * v) for v in range(5)], xflip)
                far_flux, far_speed = side(beyond, 0)
                spread = 3.0 * jnp.maximum(sx_ref[i // 3, ys, zs], far_speed)
                sign = -3.0 if last else 3.0
                ends.append([sign * far_flux[v] + spread * (beyond[v] - mine[v]) for v in range(5)])
            for v in range(5):
                f = [fx_ref[v, i, ys, zs] for i in range(4)]
                for j in range(4):
                    total = rate_ref[v, j, ys, zs]
                    for i in range(4):
                        if i != j:
                            total = total - float(DERIV[j, i]) * f[i]
                    if j == 0:
                        total = total + ends[0][v]
                    if j == 3:
                        total = total + ends[1][v]
                    rate_ref[v, j, ys, zs] = total


def split(value):
    high = value.astype(BF16)
    return high, (value - high.astype(F32)).astype(BF16)


def parcel_kernel(u_ref, z1_ref, z2_ref, own_ref, dep_ref, base_ref, acc_ref, vel_hi, vel_lo, z_hi, z_lo, a_hi, a_lo):
    low, high = lows_highs("gz", z1_ref, z2_ref)
    sides = (low, lambda t: own_ref[t], high)
    tiles = [sides[g % 3](g // 3) for g in range(27)] + [jnp.zeros((8, 128), F32)]
    for i in range(4):
        inverse = 1.0 / u_ref[0, i]
        for d in range(3):
            hi, lo = split(u_ref[d + 1, i] * inverse)
            start = 16 * (4 * d + i)
            vel_hi[start : start + 16, :] = hi
            vel_lo[start : start + 16, :] = lo
    left = lax.broadcasted_iota(jnp.int32, (8, 128), 1) < 64
    sub8 = lax.broadcasted_iota(jnp.int32, (8, 128), 0)
    sub16 = lax.broadcasted_iota(jnp.int32, (16, 128), 0)
    pos, block = sub16 & 3, sub16 >> 2
    weight_y = by_pos(pos, 1.0 / WEIGHTS)
    weight_xy = [weight_y * float(1.0 / WEIGHTS[i]) for i in range(4)]
    inner = float(NODES[2])
    kept = []
    for p in range(14):
        first, second = tiles[2 * p], tiles[2 * p + 1]
        field = jnp.where(left, first, pltpu.roll(second, 64, 1))
        code = jnp.where(left, pltpu.roll(first, 64, 1), second)
        host = code.astype(jnp.int32) - 1
        host = jnp.concatenate([host, host], axis=0)
        outer = (field + 1.0) * (field - 1.0)
        middle = (field + inner) * (field - inner)
        basis = [
            float(SCALE[0]) * middle * (field - 1.0),
            float(SCALE[1]) * outer * (field - inner),
            float(SCALE[2]) * outer * (field + inner),
            float(SCALE[3]) * middle * (field + 1.0),
        ]

        def spread(r):
            rows = [jnp.broadcast_to(basis[k][r : r + 1], (16, 128)) for k in range(4)]
            return jnp.where(pos == 0, rows[0], jnp.where(pos == 1, rows[1], jnp.where(pos == 2, rows[2], rows[3])))

        in_y = jnp.where((host >> 6) == block, spread(1), 0.0)
        in_z = spread(2)
        in_z_hi = in_z.astype(BF16).astype(F32)
        in_z_lo = in_z - in_z_hi
        offset = (host & 63) - block
        cols = slice(128 * p, 128 * p + 128)
        for t in range(16):
            here = offset == 4 * t
            z_hi[16 * t : 16 * t + 16, cols] = jnp.where(here, in_z_hi, 0.0).astype(BF16)
            z_lo[16 * t : 16 * t + 16, cols] = jnp.where(here, in_z_lo, 0.0).astype(BF16)
        kept.append((field, code, [basis[i][0:1] for i in range(4)], in_y))
    wide = jnp.dot(vel_hi[...], z_hi[...], preferred_element_type=F32)
    wide += jnp.dot(vel_lo[...], z_hi[...], preferred_element_type=F32)
    wide += jnp.dot(vel_hi[...], z_lo[...], preferred_element_type=F32)
    for p in range(14):
        field, code, in_x, in_y = kept[p]
        cols = slice(128 * p, 128 * p + 128)
        live = code > 0.5
        in_xy = [in_x[i] * in_y for i in range(4)]
        seen = []
        for d in range(3):
            mixed = None
            for i in range(4):
                start = 16 * (4 * d + i)
                term = in_xy[i] * wide[start : start + 16, cols]
                mixed = term if mixed is None else mixed + term
            seen.append(jnp.sum(mixed, axis=0, keepdims=True))
        fluid = jnp.where(sub8 == 0, seen[0], jnp.where(sub8 == 1, seen[1], seen[2]))
        speed = pltpu.roll(field, 5, 0)
        keep = live & (sub8 < 3)
        relax = jnp.where(live[0:1], field[6:7], 1.0)
        force = jnp.where(keep, (fluid - speed) / relax, 0.0)
        base = jnp.where(keep, speed, 0.0)
        base_ref[p] = base
        acc_ref[p] = force
        mass = field[7:8]
        push = -mass * force
        work = -mass * jnp.sum(force * base, axis=0, keepdims=True)
        sources = [push[0:1], push[1:2], push[2:3], work]
        for i in range(4):
            scaled = in_xy[i] * weight_xy[i]
            for d in range(4):
                hi, lo = split(sources[d] * scaled)
                start = 16 * (4 * d + i)
                a_hi[start : start + 16, cols] = hi
                a_lo[start : start + 16, cols] = lo
    lanes = (((1,), (1,)), ((), ()))
    total = lax.dot_general(a_hi[...], z_hi[...], lanes, preferred_element_type=F32)
    total += lax.dot_general(a_lo[...], z_hi[...], lanes, preferred_element_type=F32)
    total += lax.dot_general(a_hi[...], z_lo[...], lanes, preferred_element_type=F32)
    zpos = lax.broadcasted_iota(jnp.int32, (16, 256), 1) & 3
    weight_z = by_pos(zpos, 1.0 / WEIGHTS)
    for d in range(4):
        for i in range(4):
            start = 16 * (4 * d + i)
            dep_ref[d, i] = total[start : start + 16, :] * weight_z


def finish_kernel(u_ref, rate_ref, dep_ref, top_ref, base_ref, acc_ref, next_ref, vel_ref):
    top = jnp.max(jnp.max(top_ref[...], axis=0, keepdims=True), axis=1, keepdims=True)
    step = 1.0 / (7.0 * jnp.broadcast_to(top, (8, 256)))
    step16 = jnp.concatenate([step, step], axis=0)
    for v in range(5):
        for i in range(4):
            rate = rate_ref[v, i]
            if v > 0:
                rate = rate + dep_ref[v - 1, i]
            next_ref[v, i] = u_ref[v, i] + step16 * rate
    small = step[:, :128]
    for pair in range(14):
        value = base_ref[pair] + small * acc_ref[pair]
        for h in range(2):
            g = 2 * pair + h
            if g < 27:
                vel_ref[g // 9, g // 3 % 3, g % 3] = value[0:3, 64 * h : 64 * h + 64]


def exchanged(first, second, axis):
    count = lax.axis_size(axis)
    out = []
    for start, value in ((0, first), (1, second)):
        pairs = [(i, i + 1) for i in range(start, count - 1, 2)]
        pairs = pairs + [(j, i) for i, j in pairs]
        out.append(lax.ppermute(value, axis, pairs) if pairs else jnp.zeros_like(value))
    return out


def call(kernel, outs, scratch=(), inputs=None):
    return pl.pallas_call(
        kernel,
        out_shape=outs,
        scratch_shapes=list(scratch),
        compiler_params=pltpu.CompilerParams(vmem_limit_bytes=VMEM_BYTES),
        **({} if inputs is None else {"in_specs": inputs}),
    )


def tiles_of(n):
    return jax.ShapeDtypeStruct((n, 8, 128), F32)


def local(fluid_state, parcel_data, host_element, slot_counts):
    tile = jax.ShapeDtypeStruct((8, 128), F32)
    row = jax.ShapeDtypeStruct((1, 128), F32)
    args = (fluid_state, parcel_data, host_element, slot_counts)
    x_first, x_second, keep_x, faces, top = call(
        pack_kernel,
        (tiles_of(29), tiles_of(29), tiles_of(9), tiles_of(14), tile),
        [pltpu.VMEM(arg.shape, arg.dtype) for arg in args] + [pltpu.SemaphoreType.DMA((4,))],
        [pl.BlockSpec(memory_space=pltpu.HBM)] * 4,
    )(*args)
    top = lax.all_to_all(top, "gx", 0, 0, tiled=True)
    x1, x2 = exchanged(x_first, x_second, "gx")
    y_first, y_second, keep_y, top = call(turn_y_kernel, (tiles_of(14), tiles_of(14), tiles_of(9), row))(
        x1, x2, keep_x, faces, top
    )
    top = lax.pmax(top, "gy")
    y1, y2 = exchanged(y_first, y_second, "gy")
    z_first, z_second, keep_z, top = call(turn_z_kernel, (tiles_of(11), tiles_of(11), tiles_of(9), row))(
        y1, y2, keep_y, faces, top
    )
    top = lax.all_gather(top, "gz", axis=0, tiled=True)
    z1, z2 = exchanged(z_first, z_second, "gz")
    field = jax.ShapeDtypeStruct((5, 4, 16, 256), F32)
    rate = call(
        rate_kernel, field, [pltpu.VMEM((5, 4, 16, 256), F32), pltpu.VMEM((2, 16, 256), F32)],
    )(fluid_state, x1, x2, y1, y2, z1, z2, faces)
    deposit, base, acc = call(
        parcel_kernel,
        (jax.ShapeDtypeStruct((4, 4, 16, 256), F32), tiles_of(14), tiles_of(14)),
        [
            pltpu.VMEM((192, 256), BF16),
            pltpu.VMEM((192, 256), BF16),
            pltpu.VMEM((256, 1792), BF16),
            pltpu.VMEM((256, 1792), BF16),
            pltpu.VMEM((256, 1792), BF16),
            pltpu.VMEM((256, 1792), BF16),
        ],
    )(fluid_state, z1, z2, keep_z)
    return call(finish_kernel, (field, jax.ShapeDtypeStruct((3, 3, 3, 3, 64), F32)))(
        fluid_state, rate, deposit, top, base, acc
    )


def solution(mesh):
    placed = (
        P(None, "gx", "gy", "gz"),
        P("gx", "gy", "gz", None, None),
        P("gx", "gy", "gz", None),
        P("gx", "gy", "gz"),
    )
    return jax.shard_map(
        local,
        mesh=mesh,
        in_specs=placed,
        out_specs=(P(None, "gx", "gy", "gz"), P("gx", "gy", "gz", None, None)),
        check_vma=False,
    )
```

time: 77.7 us -> 73.5 us (0.946)
  blocking collectives: 0 us -> 42.7 us
  starting transfers between devices: 49.1 us -> 21.4 us
  waiting for transfers between devices: 16.7 us -> 0.02 us
  Pallas kernels: 7.31 us -> 4.81 us
    ppermute x12 -> x6, starting transfers between devices: 49.1 us -> 21.4 us  [exchanged(): lax.ppermute(value, axis, pairs)]
    all_to_all x0 -> x1, blocking collectives: none -> 17.9 us  [local(): top = lax.all_to_all(top, 'gx', 0, 0, tiled=True)]
    ppermute x12 -> x6, waiting for transfers between devices: 16.7 us -> 0.02 us  [exchanged(): lax.ppermute(value, axis, pairs)]
    pmax x0 -> x1, blocking collectives: none -> 14.7 us  [local(): top = lax.pmax(top, 'gy')]
    all_gather x0 -> x1, blocking collectives: none -> 10.1 us  [local(): top = lax.all_gather(top, 'gz', axis=0, tiled=True)]
    pallas_call x1, Pallas kernels: 5.01 us -> 2.11 us  [local(): call(parcel_kernel, (jax.ShapeDtypeStruct((4, 4, 16, 256), F32), tiles_of...]
  transfers between devices with their start and end apart: 12 -> 6, of which waited for: 5 -> 0; matrix products, arithmetic and copies ran while one was open for 0% -> 0% of each run, Pallas kernels for 8% -> 0%
where the time goes in v2:
time: 73.5 us; the launch traced here: 73 us
  blocking collectives  42.7 us (58%)
  starting transfers between devices  21.4 us (29%)
  Pallas kernels  4.81 us (7%)
  local copies, waits for them, and re-layouts  3.28 us (4%)
  between operations  0.74 us (1%)
    ppermute x6, starting transfers between devices, exchanged(): lax.ppermute(value, axis, pairs)  21.4 us
    all_to_all x1, blocking collectives, local(): top = lax.all_to_all(top, 'gx', 0, 0, tiled=True)  17.9 us
    pmax x1, blocking collectives, local(): top = lax.pmax(top, 'gy')  14.7 us
    all_gather x1, blocking collectives, local(): top = lax.all_gather(top, 'gz', axis=0, tiled=True)  10.1 us
    unnamed x10, local copies, waits for them, and re-layouts  3.28 us
    pallas_call x1, Pallas kernels, local(): call(parcel_kernel, (jax.ShapeDtypeStruct((4, 4, 16, 256), F32), tiles_of...  2.11 us
  transfers between devices with their start and end apart: 6, of which 0 were waited for; matrix products, arithmetic and copies ran while one was open for 0% of the time, Pallas kernels for 0%

profile of v2, /device:TPU:1, one launch (start us, length us, event | category | flops | bytes accessed | tf_op | source)
XLA Modules:
  0.0 73.0 jit_solution(2157882561008257950)
XLA Ops:
  0.6 0.0 copy-start
  0.6 1.0 %copy-done = f32[5,4,16,256]{3,2,1,0:T(8,128)S(1)} copy-done((f32[5,4,16,256]{3,2,1,0:T(8,128)S(1)}, f32[5,4,16,256]{3,2,1,0:T(8,128)}, u32[]{:S(2)}) %copy-start) | copy-done | bytes 327704
  1.6 0.9 %copy-done.2 = f32[3,3,3,8,64]{4,3,2,1,0:T(8,128)S(1)} copy-done((f32[3,3,3,8,64]{4,3,2,1,0:T(8,128)S(1)}, f32[3,3,3,8,64]{4,3,2,1,0:T(8,128)}, u32[]{:S(2)}) %copy-start.2) | copy-done | bytes 55320
  2.5 0.7 copy-done.3
  3.2 0.7 copy-done.4
  3.9 0.6 shard_map.59
  4.6 0.0 copy-start.1
  4.6 5.0 %collective-permute-start = (f32[29,8,128]{2,1,0:T(8,128)S(1)}, f32[29,8,128]{2,1,0:T(8,128)S(1)}, u32[]{:S(2)}, u32[]{:S(2)}) collective-permute-start(f32[29,8,128]{2,1,0:T(8,128)S(1)} %get-tuple-element.18), channel_id=1, source_target_pairs={{0,64},{128,192},{256,320},{384,448},{64,0},{192,128},{320,256},{4... | collective-permute-start | bytes 356360 | tf_op jit(solution)/shard_map/ppermute | solution.py:414
  9.5 0.7 collective-permute-start.1
  10.2 17.9 %all_to_all.11 = f32[8,1,128]{2,1,0:T(1,128)S(1)} all-to-all(f32[8,1,128]{2,1,0:T(1,128)S(1)} %bitcast.8), channel_id=1, replica_groups=mesh['gx'=8,'gy'=8,'gz'=8] {'gx'}, dimensions={0} | all-to-all | bytes 8192 | tf_op jit(solution)/shard_map/all_to_all | solution.py:442
  28.1 0.0 collective-permute-done.x1_ref
  28.1 0.0 collective-permute-done.1.x2_ref
  28.1 3.2 %collective-permute-start.2 = (f32[14,8,128]{2,1,0:T(8,128)S(1)}, f32[14,8,128]{2,1,0:T(8,128)S(1)}, u32[]{:S(2)}, u32[]{:S(2)}) collective-permute-start(f32[14,8,128]{2,1,0:T(8,128)S(1)} %get-tuple-element.23), channel_id=1, source_target_pairs={{0,8},{16,24},{32,40},{48,56},{8,0},{24,16},{40,32},{56,48},{1,9},... | collective-permute-start | bytes 172040 | tf_op jit(solution)/shard_map/ppermute | solution.py:414
  31.3 0.7 collective-permute-start.3
  32.0 14.7 %pmax.7.tops_ref = f32[1,128]{1,0:T(1,128)S(1)} all-reduce(f32[1,128]{1,0:T(1,128)S(1)} %get-tuple-element.26), channel_id=1, replica_groups=mesh['gx'=8,'gy'=8,'gz'=8] {'gy'}, use_global_device_ids=true, to_apply=%region_0.0 | all-reduce | flops 128 | bytes 1024 | tf_op jit(solution)/shard_map/pmax | solution.py:447
  46.8 0.0 collective-permute-done.2.y1_ref
  46.8 8.9 %collective-permute-start.4 = (f32[11,8,128]{2,1,0:T(8,128)S(1)}, f32[11,8,128]{2,1,0:T(8,128)S(1)}, u32[]{:S(2)}, u32[]{:S(2)}) collective-permute-start(f32[11,8,128]{2,1,0:T(8,128)S(1)} %get-tuple-element.27), channel_id=1, source_target_pairs={{0,1},{2,3},{4,5},{6,7},{1,0},{3,2},{5,4},{7,6},{8,9},{10,11},{12,... | collective-permute-start | bytes 135176 | tf_op jit(solution)/shard_map/ppermute | solution.py:414
  55.7 3.0 %collective-permute-start.5 = (f32[11,8,128]{2,1,0:T(8,128)S(1)}, f32[11,8,128]{2,1,0:T(8,128)S(1)}, u32[]{:S(2)}, u32[]{:S(2)}) collective-permute-start(f32[11,8,128]{2,1,0:T(8,128)S(1)} %get-tuple-element.28), channel_id=1, source_target_pairs={{1,2},{3,4},{5,6},{2,1},{4,3},{6,5},{9,10},{11,12},{13,14},{10,9},... | collective-permute-start | bytes 135176 | tf_op jit(solution)/shard_map/ppermute | solution.py:414
  58.7 10.1 %all-gather = f32[8,1,128]{2,1,0:T(1,128)S(1)} all-gather(f32[1,1,128]{2,1,0:T(1,128)S(1)} %bitcast.9), channel_id=1, replica_groups=mesh['gx'=8,'gy'=8,'gz'=8] {'gz'}, dimensions={0}, use_global_device_ids=true | all-gather | bytes 4608 | tf_op jit(solution)/shard_map/all_gather | solution.py:452
  68.8 0.0 collective-permute-done.4.z1_ref
  68.8 0.0 collective-permute-done.5.z2_ref
  68.8 1.2 %shard_map.62.rate_ref = f32[5,4,16,256]{3,2,1,0:T(8,128)S(1)} custom-call(f32[5,4,16,256]{3,2,1,0:T(8,128)S(1)} %copy-done.1, f32[29,8,128]{2,1,0:T(8,128)S(1)} %collective-permute-done.x1_ref, f32[29,8,128]{2,1,0:T(8,128)S(1)} %collective-permute-done.1.x2_ref, f32[14,8,128]{2,1,0:T(8,128)S(1)} %collective-permute-done.2.y1_ref, ...), custom_call_target="tpu_custom_call" | custom-call | tf_op jit(solution)/shard_map/pallas_call | solution.py:455
  70.0 2.1 %shard_map.63 = (f32[4,4,16,256]{3,2,1,0:T(8,128)S(1)}, f32[14,8,128]{2,1,0:T(8,128)S(1)}, f32[14,8,128]{2,1,0:T(8,128)S(1)}) custom-call(f32[5,4,16,256]{3,2,1,0:T(8,128)S(1)} %copy-done.1, f32[11,8,128]{2,1,0:T(8,128)S(1)} %collective-permute-done.4.z1_ref, f32[11,8,128]{2,1,0:T(8,128)S(1)} %collective-permute-done.5.z2_ref, ...), custom_call_target="tpu_custom_call" | custom-call | tf_op jit(solution)/shard_map/pallas_call | solution.py:458
  72.1 0.9 %shard_map.64 = (f32[5,4,16,256]{3,2,1,0:T(8,128)}, f32[3,3,3,3,64]{4,3,2,1,0:T(4,128)}) custom-call(f32[5,4,16,256]{3,2,1,0:T(8,128)S(1)} %copy-done.1, f32[5,4,16,256]{3,2,1,0:T(8,128)S(1)} %shard_map.62.rate_ref, f32[4,4,16,256]{3,2,1,0:T(8,128)S(1)} %get-tuple-element.30.dep_ref, f32[8,128]{1,0:T(8,128)S(1)} %bitcast.6, ...), custom_call_target="tpu_custom_call" | custom-call | tf_op jit(solution)/shard_map/pallas_call | solution.py:470
  (7 shorter events, 0.1 us)
Async XLA Ops:
  0.6 1.0 %copy-start = (f32[5,4,16,256]{3,2,1,0:T(8,128)S(1)}, f32[5,4,16,256]{3,2,1,0:T(8,128)}, u32[]{:S(2)}) copy-start(f32[5,4,16,256]{3,2,1,0:T(8,128)} %u_ref.5) | copy-start | bytes 983044
  1.6 0.9 %copy-start.2 = (f32[3,3,3,8,64]{4,3,2,1,0:T(8,128)S(1)}, f32[3,3,3,8,64]{4,3,2,1,0:T(8,128)}, u32[]{:S(2)}) copy-start(f32[3,3,3,8,64]{4,3,2,1,0:T(8,128)} %data_hbm.1) | copy-start | bytes 165892
  2.5 0.7 copy-start.3
  3.2 0.7 copy-start.4
  4.6 64.3 %copy-start.1 = (f32[5,4,16,256]{3,2,1,0:T(8,128)S(1)}, f32[5,4,16,256]{3,2,1,0:T(8,128)}, u32[]{:S(2)}) copy-start(f32[5,4,16,256]{3,2,1,0:T(8,128)} %u_ref.5) | copy-start | bytes 983044
  4.6 23.5 %collective-permute-start = (f32[29,8,128]{2,1,0:T(8,128)S(1)}, f32[29,8,128]{2,1,0:T(8,128)S(1)}, u32[]{:S(2)}, u32[]{:S(2)}) collective-permute-start(f32[29,8,128]{2,1,0:T(8,128)S(1)} %get-tuple-element.18), channel_id=1, source_target_pairs={{0,64},{128,192},{256,320},{384,448},{64,0},{192,128},{320,256},{4... | collective-permute-start | bytes 356360 | tf_op jit(solution)/shard_map/ppermute | solution.py:414
  9.5 18.6 %collective-permute-start.1 = (f32[29,8,128]{2,1,0:T(8,128)S(1)}, f32[29,8,128]{2,1,0:T(8,128)S(1)}, u32[]{:S(2)}, u32[]{:S(2)}) collective-permute-start(f32[29,8,128]{2,1,0:T(8,128)S(1)} %get-tuple-element.19), channel_id=1, source_target_pairs={{64,128},{192,256},{320,384},{128,64},{256,192},{384,320},{65,129}... | collective-permute-start | bytes 356360 | tf_op jit(solution)/shard_map/ppermute | solution.py:414
  28.1 18.6 %collective-permute-start.2 = (f32[14,8,128]{2,1,0:T(8,128)S(1)}, f32[14,8,128]{2,1,0:T(8,128)S(1)}, u32[]{:S(2)}, u32[]{:S(2)}) collective-permute-start(f32[14,8,128]{2,1,0:T(8,128)S(1)} %get-tuple-element.23), channel_id=1, source_target_pairs={{0,8},{16,24},{32,40},{48,56},{8,0},{24,16},{40,32},{56,48},{1,9},... | collective-permute-start | bytes 172040 | tf_op jit(solution)/shard_map/ppermute | solution.py:414
  31.3 15.4 %collective-permute-start.3 = (f32[14,8,128]{2,1,0:T(8,128)S(1)}, f32[14,8,128]{2,1,0:T(8,128)S(1)}, u32[]{:S(2)}, u32[]{:S(2)}) collective-permute-start(f32[14,8,128]{2,1,0:T(8,128)S(1)} %get-tuple-element.24), channel_id=1, source_target_pairs={{8,16},{24,32},{40,48},{16,8},{32,24},{48,40},{9,17},{25,33},{41,4... | collective-permute-start | bytes 172040 | tf_op jit(solution)/shard_map/ppermute | solution.py:414
  46.8 22.1 %collective-permute-start.4 = (f32[11,8,128]{2,1,0:T(8,128)S(1)}, f32[11,8,128]{2,1,0:T(8,128)S(1)}, u32[]{:S(2)}, u32[]{:S(2)}) collective-permute-start(f32[11,8,128]{2,1,0:T(8,128)S(1)} %get-tuple-element.27), channel_id=1, source_target_pairs={{0,1},{2,3},{4,5},{6,7},{1,0},{3,2},{5,4},{7,6},{8,9},{10,11},{12,... | collective-permute-start | bytes 135176 | tf_op jit(solution)/shard_map/ppermute | solution.py:414
  55.7 13.2 %collective-permute-start.5 = (f32[11,8,128]{2,1,0:T(8,128)S(1)}, f32[11,8,128]{2,1,0:T(8,128)S(1)}, u32[]{:S(2)}, u32[]{:S(2)}) collective-permute-start(f32[11,8,128]{2,1,0:T(8,128)S(1)} %get-tuple-element.28), channel_id=1, source_target_pairs={{1,2},{3,4},{5,6},{2,1},{4,3},{6,5},{9,10},{11,12},{13,14},{10,9},... | collective-permute-start | bytes 135176 | tf_op jit(solution)/shard_map/ppermute | solution.py:414

commit v3 on v2

--- a/solution.py
+++ b/solution.py
@@ -28,6 +28,8 @@
 SCALE = [1.0 / np.prod([NODES[i] - NODES[j] for j in range(4) if j != i]) for i in range(4)]
 
 FACE = 9
+
+PIECES = (8, 32, 2)
 
 
 def by_pos(pos, values):
@@ -94,7 +96,9 @@
         speed = jnp.sqrt(square) + sound
         top = speed if top is None else jnp.maximum(top, speed)
     top = jnp.maximum(top[:, :128], top[:, 128:])
-    top_ref[...] = jnp.broadcast_to(jnp.max(top, axis=0, keepdims=True), (8, 128))
+    top = jnp.broadcast_to(jnp.max(top, axis=0, keepdims=True), (8, 128))
+    for t in range(PIECES[0]):
+        top_ref[t] = top
     slot = lax.broadcasted_iota(jnp.int32, (1, 64), 1)
     odd = parity("gx")
     for a, out in ((2 - 2 * odd, first_ref), (2 * odd, second_ref), (1, keep_ref)):
@@ -131,8 +135,21 @@
         face_ref[12 + yh] = low[8 * yh : 8 * yh + 8]
 
 
+def folded(tops_ref, pieces):
+    top = tops_ref[0]
+    for t in range(pieces, tops_ref.shape[0], pieces):
+        top = jnp.maximum(top, tops_ref[t])
+    return top
+
+
+def fold(tops_ref, top_ref, pieces):
+    top = folded(tops_ref, pieces)
+    for t in range(top_ref.shape[0]):
+        top_ref[t] = top
+
+
 def turn_y_kernel(x1_ref, x2_ref, own_ref, face_ref, tops_ref, first_ref, second_ref, keep_ref, top_ref):
-    top_ref[...] = jnp.max(tops_ref[...], axis=0, keepdims=True)
+    fold(tops_ref, top_ref, PIECES[0])
     low, high = lows_highs("gx", x1_ref, x2_ref)
     odd = parity("gy")
     for a, source in enumerate((low, lambda t: own_ref[t], high)):
@@ -146,7 +163,7 @@
 
 
 def turn_z_kernel(y1_ref, y2_ref, own_ref, face_ref, tops_ref, first_ref, second_ref, keep_ref, top_ref):
-    top_ref[...] = jnp.max(tops_ref[...], axis=0, keepdims=True)
+    fold(tops_ref, top_ref, PIECES[1])
     low, high = lows_highs("gy", y1_ref, y2_ref)
     odd = parity("gz")
     for b, source in enumerate((low, lambda t: own_ref[t], high)):
@@ -387,7 +404,7 @@
 
 
 def finish_kernel(u_ref, rate_ref, dep_ref, top_ref, base_ref, acc_ref, next_ref, vel_ref):
-    top = jnp.max(jnp.max(top_ref[...], axis=0, keepdims=True), axis=1, keepdims=True)
+    top = jnp.max(jnp.max(folded(top_ref, PIECES[2]), axis=0, keepdims=True), axis=1, keepdims=True)
     step = 1.0 / (7.0 * jnp.broadcast_to(top, (8, 256)))
     step16 = jnp.concatenate([step, step], axis=0)
     for v in range(5):
@@ -430,23 +447,21 @@
 
 
 def local(fluid_state, parcel_data, host_element, slot_counts):
-    tile = jax.ShapeDtypeStruct((8, 128), F32)
-    row = jax.ShapeDtypeStruct((1, 128), F32)
     args = (fluid_state, parcel_data, host_element, slot_counts)
     x_first, x_second, keep_x, faces, top = call(
         pack_kernel,
-        (tiles_of(29), tiles_of(29), tiles_of(9), tiles_of(14), tile),
+        (tiles_of(29), tiles_of(29), tiles_of(9), tiles_of(14), tiles_of(PIECES[0])),
         [pltpu.VMEM(arg.shape, arg.dtype) for arg in args] + [pltpu.SemaphoreType.DMA((4,))],
         [pl.BlockSpec(memory_space=pltpu.HBM)] * 4,
     )(*args)
-    top = lax.all_to_all(top, "gx", 0, 0, tiled=True)
+    top = lax.all_gather(top, "gx", axis=0, tiled=True)
     x1, x2 = exchanged(x_first, x_second, "gx")
-    y_first, y_second, keep_y, top = call(turn_y_kernel, (tiles_of(14), tiles_of(14), tiles_of(9), row))(
+    y_first, y_second, keep_y, top = call(turn_y_kernel, (tiles_of(14), tiles_of(14), tiles_of(9), tiles_of(PIECES[1])))(
         x1, x2, keep_x, faces, top
     )
-    top = lax.pmax(top, "gy")
+    top = lax.all_gather(top, "gy", axis=0, tiled=True)
     y1, y2 = exchanged(y_first, y_second, "gy")
-    z_first, z_second, keep_z, top = call(turn_z_kernel, (tiles_of(11), tiles_of(11), tiles_of(9), row))(
+    z_first, z_second, keep_z, top = call(turn_z_kernel, (tiles_of(11), tiles_of(11), tiles_of(9), tiles_of(PIECES[2])))(
         y1, y2, keep_y, faces, top
     )
     top = lax.all_gather(top, "gz", axis=0, tiled=True)

time: 73.5 us -> 120 us (1.63)
  waiting for transfers between devices: 0.02 us -> 38.1 us
  between operations: 0.74 us -> 14.1 us
  blocking collectives: 42.7 us -> 37.6 us
  starting transfers between devices: 21.4 us -> 19.9 us
  local copies, waits for them, and re-layouts: 3.28 us -> 4.5 us
    all_gather x0 -> x1, waiting for transfers between devices: none -> 37 us  [local(): top = lax.all_gather(top, 'gy', axis=0, tiled=True)]
    all_gather x0 -> x1, blocking collectives: none -> 25.1 us  [local(): top = lax.all_gather(top, 'gx', axis=0, tiled=True)]
    all_to_all x1 -> x0, blocking collectives: 17.9 us -> none  [local(): top = lax.all_to_all(top, 'gx', 0, 0, tiled=True)]
    pmax x1 -> x0, blocking collectives: 14.7 us -> none  [local(): top = lax.pmax(top, 'gy')]
    all_gather x1, blocking collectives: 10.1 us -> 12.5 us  [local(): top = lax.all_gather(top, 'gz', axis=0, tiled=True)]
    ppermute x6, starting transfers between devices: 21.4 us -> 19.8 us  [exchanged(): lax.ppermute(value, axis, pairs)]
    unnamed x10 -> x12, local copies, waits for them, and re-layouts: 3.28 us -> 4.5 us
  transfers between devices with their start and end apart: 6 -> 7, of which waited for: 0 -> 2; matrix products, arithmetic and copies ran while one was open for 0% -> 0% of each run, Pallas kernels for 0% -> 0%
where the time goes in v3:
time: 120 us
  waiting for transfers between devices  38.1 us (32%)
  blocking collectives  37.6 us (31%)
  starting transfers between devices  19.9 us (17%)
  between operations  14.1 us (12%)
  Pallas kernels  5.48 us (5%)
  local copies, waits for them, and re-layouts  4.5 us (4%)
    all_gather x1, waiting for transfers between devices, local(): top = lax.all_gather(top, 'gy', axis=0, tiled=True)  37 us
    all_gather x1, blocking collectives, local(): top = lax.all_gather(top, 'gx', axis=0, tiled=True)  25.1 us
    ppermute x6, starting transfers between devices, exchanged(): lax.ppermute(value, axis, pairs)  19.8 us
    all_gather x1, blocking collectives, local(): top = lax.all_gather(top, 'gz', axis=0, tiled=True)  12.5 us
    unnamed x12, local copies, waits for them, and re-layouts  4.5 us
  transfers between devices with their start and end apart: 7, of which 2 were waited for; matrix products, arithmetic and copies ran while one was open for 0% of the time, Pallas kernels for 0%

profile of v3, /device:TPU:1, one launch (start us, length us, event | category | flops | bytes accessed | tf_op | source)
XLA Modules:
  0.0 119.7 jit_solution(9593484712261017875)
XLA Ops:
  7.2 0.0 all-gather.2.cloned.1.call-start
  7.2 0.0 copy-start
  7.2 1.0 copy-done
  8.2 0.9 copy-done.3
  9.1 0.7 copy-done.4
  9.8 0.7 copy-done.5
  10.5 0.6 shard_map.59
  11.1 4.8 %collective-permute-start = (f32[29,8,128]{2,1,0:T(8,128)S(1)}, f32[29,8,128]{2,1,0:T(8,128)S(1)}, u32[]{:S(2)}, u32[]{:S(2)}) collective-permute-start(f32[29,8,128]{2,1,0:T(8,128)S(1)} %get-tuple-element.18), channel_id=1, source_target_pairs={{0,64},{128,192},{256,320},{384,448},{64,0},{192,128},{320,256},{4... | collective-permute-start | bytes 356360 | tf_op jit(solution)/shard_map/ppermute | solution.py:431
  16.0 0.7 collective-permute-start.1
  16.6 25.1 %all_gather.9.tops_ref = f32[64,8,128]{2,1,0:T(8,128)S(1)} all-gather(f32[8,8,128]{2,1,0:T(8,128)S(1)} %get-tuple-element.22), channel_id=1, replica_groups=mesh['gx'=8,'gy'=8,'gz'=8] {'gx'}, dimensions={0}, use_global_device_ids=true | all-gather | bytes 294912 | tf_op jit(solution)/shard_map/all_gather | solution.py:457
  41.8 0.0 collective-permute-done.x1_ref
  41.8 0.7 shard_map.60
  42.5 0.0 all-gather.2.cloned.1.call-update
  42.5 3.2 %collective-permute-start.2 = (f32[14,8,128]{2,1,0:T(8,128)S(1)}, f32[14,8,128]{2,1,0:T(8,128)S(1)}, u32[]{:S(2)}, u32[]{:S(2)}) collective-permute-start(f32[14,8,128]{2,1,0:T(8,128)S(1)} %get-tuple-element.23), channel_id=1, source_target_pairs={{0,8},{16,24},{32,40},{48,56},{8,0},{24,16},{40,32},{56,48},{1,9},... | collective-permute-start | bytes 172040 | tf_op jit(solution)/shard_map/ppermute | solution.py:431
  45.7 0.7 collective-permute-start.3
  46.4 1.1 collective-permute-done.2.y1_ref
  47.5 37.0 %all-gather.2.cloned.1.call-done.tops_ref = f32[256,8,128]{2,1,0:T(8,128)} async-done(((f32[32,8,128]{2,1,0:T(8,128)}), f32[256,8,128]{2,1,0:T(8,128)}) %all-gather.2.cloned.1.call-update) | async-done | bytes 1048592 | tf_op jit(solution)/shard_map/all_gather | solution.py:462
  84.5 1.2 %copy-done.2 = f32[256,8,128]{2,1,0:T(8,128)S(1)} copy-done((f32[256,8,128]{2,1,0:T(8,128)S(1)}, f32[256,8,128]{2,1,0:T(8,128)}, u32[]{:S(2)}) %copy-start.2) | copy-done | bytes 1048600
  85.7 7.5 %collective-permute-start.4 = (f32[11,8,128]{2,1,0:T(8,128)S(1)}, f32[11,8,128]{2,1,0:T(8,128)S(1)}, u32[]{:S(2)}, u32[]{:S(2)}) collective-permute-start(f32[11,8,128]{2,1,0:T(8,128)S(1)} %get-tuple-element.27), channel_id=1, source_target_pairs={{0,1},{2,3},{4,5},{6,7},{1,0},{3,2},{5,4},{7,6},{8,9},{10,11},{12,... | collective-permute-start | bytes 135176 | tf_op jit(solution)/shard_map/ppermute | solution.py:431
  93.2 3.0 %collective-permute-start.5 = (f32[11,8,128]{2,1,0:T(8,128)S(1)}, f32[11,8,128]{2,1,0:T(8,128)S(1)}, u32[]{:S(2)}, u32[]{:S(2)}) collective-permute-start(f32[11,8,128]{2,1,0:T(8,128)S(1)} %get-tuple-element.28), channel_id=1, source_target_pairs={{1,2},{3,4},{5,6},{2,1},{4,3},{6,5},{9,10},{11,12},{13,14},{10,9},... | collective-permute-start | bytes 135176 | tf_op jit(solution)/shard_map/ppermute | solution.py:431
  96.2 12.5 %all_gather.11.top_ref = f32[16,8,128]{2,1,0:T(8,128)S(1)} all-gather(f32[2,8,128]{2,1,0:T(8,128)S(1)} %get-tuple-element.31), channel_id=1, replica_groups=mesh['gx'=8,'gy'=8,'gz'=8] {'gz'}, dimensions={0}, use_global_device_ids=true | all-gather | bytes 73728 | tf_op jit(solution)/shard_map/all_gather | solution.py:467
  108.6 1.2 shard_map.62.rate_ref
  109.8 2.1 %shard_map.63 = (f32[4,4,16,256]{3,2,1,0:T(8,128)S(1)}, f32[14,8,128]{2,1,0:T(8,128)S(1)}, f32[14,8,128]{2,1,0:T(8,128)S(1)}) custom-call(f32[5,4,16,256]{3,2,1,0:T(8,128)S(1)} %copy-done.1, f32[11,8,128]{2,1,0:T(8,128)S(1)} %collective-permute-done.4.z1_ref, f32[11,8,128]{2,1,0:T(8,128)S(1)} %collective-permute-done.5.z2_ref, ...), custom_call_target="tpu_custom_call" | custom-call | tf_op jit(solution)/shard_map/pallas_call | solution.py:473
  111.9 0.9 shard_map.64
  (11 shorter events, 0.0 us)
Async XLA Ops:
  7.2 77.3 %all-gather.2.cloned.1.call-start = ((), (), s32[]{:S(2)}) async-start(), calls=%async_computation | async-start | bytes 1179648 | tf_op jit(solution)/shard_map/all_gather | solution.py:462
  7.2 1.0 copy-start
  8.2 0.9 copy-start.3
  9.1 0.7 copy-start.4
  9.8 0.7 copy-start.5
  11.1 30.7 %collective-permute-start = (f32[29,8,128]{2,1,0:T(8,128)S(1)}, f32[29,8,128]{2,1,0:T(8,128)S(1)}, u32[]{:S(2)}, u32[]{:S(2)}) collective-permute-start(f32[29,8,128]{2,1,0:T(8,128)S(1)} %get-tuple-element.18), channel_id=1, source_target_pairs={{0,64},{128,192},{256,320},{384,448},{64,0},{192,128},{320,256},{4... | collective-permute-start | bytes 356360 | tf_op jit(solution)/shard_map/ppermute | solution.py:431
  16.0 25.8 %collective-permute-start.1 = (f32[29,8,128]{2,1,0:T(8,128)S(1)}, f32[29,8,128]{2,1,0:T(8,128)S(1)}, u32[]{:S(2)}, u32[]{:S(2)}) collective-permute-start(f32[29,8,128]{2,1,0:T(8,128)S(1)} %get-tuple-element.19), channel_id=1, source_target_pairs={{64,128},{192,256},{320,384},{128,64},{256,192},{384,320},{65,129}... | collective-permute-start | bytes 356360 | tf_op jit(solution)/shard_map/ppermute | solution.py:431
  42.5 5.0 %collective-permute-start.2 = (f32[14,8,128]{2,1,0:T(8,128)S(1)}, f32[14,8,128]{2,1,0:T(8,128)S(1)}, u32[]{:S(2)}, u32[]{:S(2)}) collective-permute-start(f32[14,8,128]{2,1,0:T(8,128)S(1)} %get-tuple-element.23), channel_id=1, source_target_pairs={{0,8},{16,24},{32,40},{48,56},{8,0},{24,16},{40,32},{56,48},{1,9},... | collective-permute-start | bytes 172040 | tf_op jit(solution)/shard_map/ppermute | solution.py:431
  45.7 1.8 %collective-permute-start.3 = (f32[14,8,128]{2,1,0:T(8,128)S(1)}, f32[14,8,128]{2,1,0:T(8,128)S(1)}, u32[]{:S(2)}, u32[]{:S(2)}) collective-permute-start(f32[14,8,128]{2,1,0:T(8,128)S(1)} %get-tuple-element.24), channel_id=1, source_target_pairs={{8,16},{24,32},{40,48},{16,8},{32,24},{48,40},{9,17},{25,33},{41,4... | collective-permute-start | bytes 172040 | tf_op jit(solution)/shard_map/ppermute | solution.py:431
  84.5 1.2 %copy-start.2 = (f32[256,8,128]{2,1,0:T(8,128)S(1)}, f32[256,8,128]{2,1,0:T(8,128)}, u32[]{:S(2)}) copy-start(f32[256,8,128]{2,1,0:T(8,128)} %all-gather.2.cloned.1.call-done.tops_ref) | copy-start | bytes 3145732
  85.7 23.0 %copy-start.1 = (f32[5,4,16,256]{3,2,1,0:T(8,128)S(1)}, f32[5,4,16,256]{3,2,1,0:T(8,128)}, u32[]{:S(2)}) copy-start(f32[5,4,16,256]{3,2,1,0:T(8,128)} %u_ref.5) | copy-start | bytes 983044
  85.7 22.9 %collective-permute-start.4 = (f32[11,8,128]{2,1,0:T(8,128)S(1)}, f32[11,8,128]{2,1,0:T(8,128)S(1)}, u32[]{:S(2)}, u32[]{:S(2)}) collective-permute-start(f32[11,8,128]{2,1,0:T(8,128)S(1)} %get-tuple-element.27), channel_id=1, source_target_pairs={{0,1},{2,3},{4,5},{6,7},{1,0},{3,2},{5,4},{7,6},{8,9},{10,11},{12,... | collective-permute-start | bytes 135176 | tf_op jit(solution)/shard_map/ppermute | solution.py:431
  93.2 15.5 %collective-permute-start.5 = (f32[11,8,128]{2,1,0:T(8,128)S(1)}, f32[11,8,128]{2,1,0:T(8,128)S(1)}, u32[]{:S(2)}, u32[]{:S(2)}) collective-permute-start(f32[11,8,128]{2,1,0:T(8,128)S(1)} %get-tuple-element.28), channel_id=1, source_target_pairs={{1,2},{3,4},{5,6},{2,1},{4,3},{6,5},{9,10},{11,12},{13,14},{10,9},... | collective-permute-start | bytes 135176 | tf_op jit(solution)/shard_map/ppermute | solution.py:431
Sparse Core Ops, SparseCore 0:
  42.6 41.8 all-gather.1

commit v4 on v2

--- a/solution.py
+++ b/solution.py
@@ -27,7 +27,7 @@
 DERIV = derivative_table()
 SCALE = [1.0 / np.prod([NODES[i] - NODES[j] for j in range(4) if j != i]) for i in range(4)]
 
-FACE = 9
+TOP, FACE = 9, 10
 
 
 def by_pos(pos, values):
@@ -61,57 +61,27 @@
     return flux(state, vel, pressure, d), jnp.abs(vel[d]) + sound
 
 
-def parity(axis):
-    return lax.axis_index(axis) & 1
-
-
-def lows_highs(axis, first_ref, second_ref):
-    odd = jnp.full((8, 128), parity(axis), jnp.int32) == 1
-
-    def low(tile):
-        return jnp.where(odd, first_ref[tile], second_ref[tile])
-
-    def high(tile):
-        return jnp.where(odd, second_ref[tile], first_ref[tile])
-
-    return low, high
-
-
-def pack_kernel(u_hbm, data_hbm, host_hbm, count_hbm, first_ref, second_ref, keep_ref, face_ref, top_ref, u_ref, data_ref, host_ref, count_ref, sems):
-    copies = [
-        pltpu.make_async_copy(source, target, sems.at[k])
-        for k, (source, target) in enumerate(
-            ((u_hbm, u_ref), (data_hbm, data_ref), (host_hbm, host_ref), (count_hbm, count_ref))
-        )
-    ]
-    for copy in copies:
-        copy.start()
-    for copy in copies:
-        copy.wait()
+def tile_of(ref):
+    return lambda tile: ref[tile]
+
+
+def face_kernel(u_ref, up_ref, down_ref, face_ref):
     top = None
     for i in range(4):
         _, _, sound, square = primitives([u_ref[v, i] for v in range(5)])
         speed = jnp.sqrt(square) + sound
         top = speed if top is None else jnp.maximum(top, speed)
     top = jnp.maximum(top[:, :128], top[:, 128:])
-    top_ref[...] = jnp.broadcast_to(jnp.max(top, axis=0, keepdims=True), (8, 128))
-    slot = lax.broadcasted_iota(jnp.int32, (1, 64), 1)
-    odd = parity("gx")
-    for a, out in ((2 - 2 * odd, first_ref), (2 * odd, second_ref), (1, keep_ref)):
-        for b in range(3):
-            for c in range(3):
-                count = count_ref[a, b : b + 1, c : c + 1]
-                host = host_ref[a, b, c : c + 1, :]
-                code = jnp.where(slot < count, host + 1, 0).astype(F32)
-                out[3 * b + c, :, 0:64] = data_ref[a, b, c]
-                out[3 * b + c, :, 64:128] = jnp.broadcast_to(code, (8, 64))
+    top = jnp.maximum(top[:8], top[8:])
+    up_ref[0] = top
+    down_ref[0] = top
     for v in range(5):
         for yh in range(2):
             for zh in range(2):
-                tile = FACE + 4 * v + 2 * yh + zh
+                tile = 1 + 4 * v + 2 * yh + zh
                 ys, zs = slice(8 * yh, 8 * yh + 8), slice(128 * zh, 128 * zh + 128)
-                first_ref[tile] = u_ref[v, 3 - 3 * odd, ys, zs]
-                second_ref[tile] = u_ref[v, 3 * odd, ys, zs]
+                up_ref[tile] = u_ref[v, 3, ys, zs]
+                down_ref[tile] = u_ref[v, 0, ys, zs]
         for i in range(4):
             for zh in range(2):
                 zs = slice(128 * zh, 128 * zh + 128)
@@ -131,32 +101,56 @@
         face_ref[12 + yh] = low[8 * yh : 8 * yh + 8]
 
 
-def turn_y_kernel(x1_ref, x2_ref, own_ref, face_ref, tops_ref, first_ref, second_ref, keep_ref, top_ref):
-    top_ref[...] = jnp.max(tops_ref[...], axis=0, keepdims=True)
-    low, high = lows_highs("gx", x1_ref, x2_ref)
-    odd = parity("gy")
-    for a, source in enumerate((low, lambda t: own_ref[t], high)):
+def pack_kernel(data_ref, host_ref, count_ref, face_up_ref, face_down_ref, up_ref, down_ref, keep_ref):
+    slot = lax.broadcasted_iota(jnp.int32, (1, 64), 1)
+    for a, out in ((2, up_ref), (0, down_ref), (1, keep_ref)):
+        for b in range(3):
+            for c in range(3):
+                count = count_ref[a, b : b + 1, c : c + 1]
+                host = host_ref[a, b, c : c + 1, :]
+                code = jnp.where(slot < count, host + 1, 0).astype(F32)
+                out[3 * b + c, :, 0:64] = data_ref[a, b, c]
+                out[3 * b + c, :, 64:128] = jnp.broadcast_to(code, (8, 64))
+    for t in range(21):
+        up_ref[TOP + t] = face_up_ref[t]
+        down_ref[TOP + t] = face_down_ref[t]
+
+
+def turn_y_kernel(low_ref, high_ref, own_ref, face_ref, mine_ref, up_ref, down_ref, keep_ref):
+    for a, source in enumerate((low_ref, own_ref, high_ref)):
         for c in range(3):
-            first_ref[3 * a + c] = source(6 - 6 * odd + c)
-            second_ref[3 * a + c] = source(6 * odd + c)
-            keep_ref[3 * a + c] = source(3 + c)
+            up_ref[3 * a + c] = source[6 + c]
+            down_ref[3 * a + c] = source[c]
+            keep_ref[3 * a + c] = source[3 + c]
+    top = jnp.maximum(jnp.maximum(low_ref[TOP], high_ref[TOP]), mine_ref[TOP])
+    up_ref[TOP] = top
+    down_ref[TOP] = top
     for v in range(5):
-        first_ref[FACE + v] = face_ref[v + 5 * odd]
-        second_ref[FACE + v] = face_ref[v + 5 - 5 * odd]
-
-
-def turn_z_kernel(y1_ref, y2_ref, own_ref, face_ref, tops_ref, first_ref, second_ref, keep_ref, top_ref):
-    top_ref[...] = jnp.max(tops_ref[...], axis=0, keepdims=True)
-    low, high = lows_highs("gy", y1_ref, y2_ref)
-    odd = parity("gz")
-    for b, source in enumerate((low, lambda t: own_ref[t], high)):
+        up_ref[FACE + v] = face_ref[v]
+        down_ref[FACE + v] = face_ref[5 + v]
+
+
+def turn_z_kernel(low_ref, high_ref, own_ref, face_ref, mine_ref, up_ref, down_ref, keep_ref):
+    for b, source in enumerate((low_ref, own_ref, high_ref)):
         for a in range(3):
-            first_ref[3 * a + b] = source(3 * a + 2 - 2 * odd)
-            second_ref[3 * a + b] = source(3 * a + 2 * odd)
-            keep_ref[3 * a + b] = source(3 * a + 1)
+            up_ref[3 * a + b] = source[3 * a + 2]
+            down_ref[3 * a + b] = source[3 * a]
+            keep_ref[3 * a + b] = source[3 * a + 1]
+    top = jnp.maximum(jnp.maximum(low_ref[TOP], high_ref[TOP]), mine_ref[TOP])
+    up_ref[TOP] = top
+    down_ref[TOP] = top
     for yh in range(2):
-        first_ref[FACE + yh] = face_ref[10 + 2 * odd + yh]
-        second_ref[FACE + yh] = face_ref[12 - 2 * odd + yh]
+        up_ref[FACE + yh] = face_ref[10 + yh]
+        down_ref[FACE + yh] = face_ref[12 + yh]
+
+
+def top_kernel(low_ref, high_ref, mine_ref, top_ref):
+    top = jnp.maximum(jnp.maximum(low_ref[TOP], high_ref[TOP]), mine_ref[TOP])
+    top_ref[...] = jnp.broadcast_to(jnp.max(top, axis=0, keepdims=True), top_ref.shape)
+
+
+def fold_kernel(tops_ref, top_ref):
+    top_ref[...] = jnp.broadcast_to(jnp.max(tops_ref[...], axis=0, keepdims=True), top_ref.shape)
 
 
 def wall(axis, last, own, received, sign_of):
@@ -191,9 +185,9 @@
 
 
 def rate_kernel(u_ref, x1_ref, x2_ref, y1_ref, y2_ref, z1_ref, z2_ref, face_ref, rate_ref, fx_ref, sx_ref):
-    x_side = lows_highs("gx", x1_ref, x2_ref)
-    y_side = lows_highs("gy", y1_ref, y2_ref)
-    z_side = lows_highs("gz", z1_ref, z2_ref)
+    x_side = tile_of(x1_ref), tile_of(x2_ref)
+    y_side = tile_of(y1_ref), tile_of(y2_ref)
+    z_side = tile_of(z1_ref), tile_of(z2_ref)
     shape = (16, 256)
     row = lax.broadcasted_iota(jnp.int32, shape, 0)
     lane = lax.broadcasted_iota(jnp.int32, shape, 1)
@@ -224,7 +218,7 @@
         both = jnp.concatenate([source(first_tile), source(first_tile + 1)], axis=0)
         return [both if v == 0 else pltpu.roll(both, 128 - 4 * v, 1) for v in range(5)]
 
-    own = lambda t: face_ref[t]
+    own = tile_of(face_ref)
     zflip = lambda v: -1.0 if v == 3 else 1.0
     zlow = wall("gz", False, columns(12, own), columns(FACE, z_side[0]), zflip)
     zhigh = wall("gz", True, columns(10, own), columns(FACE, z_side[1]), zflip)
@@ -291,9 +285,8 @@
 
 
 def parcel_kernel(u_ref, z1_ref, z2_ref, own_ref, dep_ref, base_ref, acc_ref, vel_hi, vel_lo, z_hi, z_lo, a_hi, a_lo):
-    low, high = lows_highs("gz", z1_ref, z2_ref)
-    sides = (low, lambda t: own_ref[t], high)
-    tiles = [sides[g % 3](g // 3) for g in range(27)] + [jnp.zeros((8, 128), F32)]
+    sides = (z1_ref, own_ref, z2_ref)
+    tiles = [sides[g % 3][g // 3] for g in range(27)] + [jnp.zeros((8, 128), F32)]
     for i in range(4):
         inverse = 1.0 / u_ref[0, i]
         for d in range(3):
@@ -405,23 +398,26 @@
                 vel_ref[g // 9, g // 3 % 3, g % 3] = value[0:3, 64 * h : 64 * h + 64]
 
 
-def exchanged(first, second, axis):
+def exchanged(up, down, axis):
     count = lax.axis_size(axis)
-    out = []
-    for start, value in ((0, first), (1, second)):
-        pairs = [(i, i + 1) for i in range(start, count - 1, 2)]
-        pairs = pairs + [(j, i) for i, j in pairs]
-        out.append(lax.ppermute(value, axis, pairs) if pairs else jnp.zeros_like(value))
-    return out
-
-
-def call(kernel, outs, scratch=(), inputs=None):
+    return (
+        lax.ppermute(up, axis, [(i, (i + 1) % count) for i in range(count)]),
+        lax.ppermute(down, axis, [((i + 1) % count, i) for i in range(count)]),
+    )
+
+
+def spread_top(top, axis):
+    count = lax.axis_size(axis)
+    groups = [list(range(0, count, 2)), list(range(1, count, 2))]
+    return lax.all_to_all(top, axis, 0, 0, axis_index_groups=groups, tiled=True)
+
+
+def call(kernel, outs, scratch=()):
     return pl.pallas_call(
         kernel,
         out_shape=outs,
         scratch_shapes=list(scratch),
         compiler_params=pltpu.CompilerParams(vmem_limit_bytes=VMEM_BYTES),
-        **({} if inputs is None else {"in_specs": inputs}),
     )
 
 
@@ -430,27 +426,19 @@
 
 
 def local(fluid_state, parcel_data, host_element, slot_counts):
-    tile = jax.ShapeDtypeStruct((8, 128), F32)
-    row = jax.ShapeDtypeStruct((1, 128), F32)
-    args = (fluid_state, parcel_data, host_element, slot_counts)
-    x_first, x_second, keep_x, faces, top = call(
-        pack_kernel,
-        (tiles_of(29), tiles_of(29), tiles_of(9), tiles_of(14), tile),
-        [pltpu.VMEM(arg.shape, arg.dtype) for arg in args] + [pltpu.SemaphoreType.DMA((4,))],
-        [pl.BlockSpec(memory_space=pltpu.HBM)] * 4,
-    )(*args)
-    top = lax.all_to_all(top, "gx", 0, 0, tiled=True)
-    x1, x2 = exchanged(x_first, x_second, "gx")
-    y_first, y_second, keep_y, top = call(turn_y_kernel, (tiles_of(14), tiles_of(14), tiles_of(9), row))(
-        x1, x2, keep_x, faces, top
-    )
-    top = lax.pmax(top, "gy")
-    y1, y2 = exchanged(y_first, y_second, "gy")
-    z_first, z_second, keep_z, top = call(turn_z_kernel, (tiles_of(11), tiles_of(11), tiles_of(9), row))(
-        y1, y2, keep_y, faces, top
-    )
-    top = lax.all_gather(top, "gz", axis=0, tiled=True)
-    z1, z2 = exchanged(z_first, z_second, "gz")
+    face_up, face_down, faces = call(face_kernel, (tiles_of(21), tiles_of(21), tiles_of(14)))(fluid_state)
+    x_up, x_down, keep_x = call(pack_kernel, (tiles_of(30), tiles_of(30), tiles_of(9)))(
+        parcel_data, host_element, slot_counts, face_up, face_down
+    )
+    x1, x2 = exchanged(x_up, x_down, "gx")
+    y_up, y_down, keep_y = call(turn_y_kernel, (tiles_of(15), tiles_of(15), tiles_of(9)))(x1, x2, keep_x, faces, x_up)
+    y1, y2 = exchanged(y_up, y_down, "gy")
+    z_up, z_down, keep_z = call(turn_z_kernel, (tiles_of(12), tiles_of(12), tiles_of(9)))(y1, y2, keep_y, faces, y_up)
+    z1, z2 = exchanged(z_up, z_down, "gz")
+    rows = [jax.ShapeDtypeStruct((max(1, lax.axis_size(axis) // 2), 128), F32) for axis in ("gx", "gy", "gz")]
+    top = spread_top(call(top_kernel, rows[0])(z1, z2, z_up), "gx")
+    top = spread_top(call(fold_kernel, rows[1])(top), "gy")
+    top = spread_top(call(fold_kernel, rows[2])(top), "gz")
     field = jax.ShapeDtypeStruct((5, 4, 16, 256), F32)
     rate = call(
         rate_kernel, field, [pltpu.VMEM((5, 4, 16, 256), F32), pltpu.VMEM((2, 16, 256), F32)],

time: 73.5 us -> 70.1 us (0.954)
  the two profiles are of different devices: /device:TPU:1 before, /device:TPU:2 now
where the time goes in v4:
time: 70.1 us; the launch traced here: 69.7 us
  starting transfers between devices  25.7 us (37%)
  blocking collectives  21.5 us (31%)
  waiting for transfers between devices  14.9 us (21%)
  Pallas kernels  5.1 us (7%)
  local copies, waits for them, and re-layouts  1.67 us (2%)
  between operations  0.73 us (1%)
    all_to_all x2, blocking collectives, spread_top(): return lax.all_to_all(top, axis, 0, 0, axis_index_groups=groups, tiled=True)  21.5 us
    ppermute x3, starting transfers between devices, exchanged(): lax.ppermute(down, axis, [((i + 1) % count, i) for i in range(count)])  16.5 us
    ppermute x3, waiting for transfers between devices, exchanged(): lax.ppermute(up, axis, [(i, (i + 1) % count) for i in range(count)])  12.6 us
    all_to_all x1, starting transfers between devices, spread_top(): return lax.all_to_all(top, axis, 0, 0, axis_index_groups=groups, tiled=True)  4.93 us
    ppermute x3, starting transfers between devices, exchanged(): lax.ppermute(up, axis, [(i, (i + 1) % count) for i in range(count)])  4.34 us
    pallas_call x1, Pallas kernels, local(): call(parcel_kernel, (jax.ShapeDtypeStruct((4, 4, 16, 256), F32), tiles_of...  2.1 us
    ppermute x3, waiting for transfers between devices, exchanged(): lax.ppermute(down, axis, [((i + 1) % count, i) for i in range(count)])  1.88 us
    unnamed x10, local copies, waits for them, and re-layouts  1.67 us
  transfers between devices with their start and end apart: 7, of which 6 were waited for; matrix products, arithmetic and copies ran while one was open for 0% of the time, Pallas kernels for 5%

profile of v4, /device:TPU:2, one launch (start us, length us, event | category | flops | bytes accessed | tf_op | source)
XLA Modules:
  0.0 69.7 jit_solution(13459437246835721310)
XLA Ops:
  0.6 0.0 copy-start
  0.6 1.0 %copy-done = f32[5,4,16,256]{3,2,1,0:T(8,128)S(1)} copy-done((f32[5,4,16,256]{3,2,1,0:T(8,128)S(1)}, f32[5,4,16,256]{3,2,1,0:T(8,128)}, u32[]{:S(2)}) %copy-start) | copy-done | bytes 327704
  1.6 0.2 shard_map.59
  1.8 0.7 copy-done.2
  2.5 0.2 shard_map.60
  2.7 10.9 %collective-permute-start.1 = (f32[30,8,128]{2,1,0:T(8,128)S(1)}, f32[30,8,128]{2,1,0:T(8,128)S(1)}, u32[]{:S(2)}, u32[]{:S(2)}) collective-permute-start(f32[30,8,128]{2,1,0:T(8,128)S(1)} %get-tuple-element.20), channel_id=1, source_target_pairs={{64,0},{128,64},{192,128},{256,192},{320,256},{384,320},{448,384},... | collective-permute-start | bytes 368648 | tf_op jit(solution)/shard_map/ppermute | solution.py:405
  13.6 1.9 %collective-permute-start = (f32[30,8,128]{2,1,0:T(8,128)S(1)}, f32[30,8,128]{2,1,0:T(8,128)S(1)}, u32[]{:S(2)}, u32[]{:S(2)}) collective-permute-start(f32[30,8,128]{2,1,0:T(8,128)S(1)} %get-tuple-element.19.mine_ref), channel_id=1, source_target_pairs={{0,64},{64,128},{128,192},{192,256},{256,320},{320,384},{384,448},... | collective-permute-start | bytes 368648 | tf_op jit(solution)/shard_map/ppermute | solution.py:404
  15.6 0.6 collective-permute-done.1.high_ref.x2_ref
  16.2 5.4 %collective-permute-done.low_ref.x1_ref = f32[30,8,128]{2,1,0:T(8,128)S(1)} collective-permute-done((f32[30,8,128]{2,1,0:T(8,128)S(1)}, f32[30,8,128]{2,1,0:T(8,128)S(1)}, u32[]{:S(2)}, u32[]{:S(2)}) %collective-permute-start) | collective-permute-done | bytes 122912 | tf_op jit(solution)/shard_map/ppermute | solution.py:404
  21.7 5.5 %collective-permute-start.3 = (f32[15,8,128]{2,1,0:T(8,128)S(1)}, f32[15,8,128]{2,1,0:T(8,128)S(1)}, u32[]{:S(2)}, u32[]{:S(2)}) collective-permute-start(f32[15,8,128]{2,1,0:T(8,128)S(1)} %get-tuple-element.24), channel_id=1, source_target_pairs={{8,0},{16,8},{24,16},{32,24},{40,32},{48,40},{56,48},{0,56},{9,1},... | collective-permute-start | bytes 184328 | tf_op jit(solution)/shard_map/ppermute | solution.py:405
  27.2 1.9 %collective-permute-start.2 = (f32[15,8,128]{2,1,0:T(8,128)S(1)}, f32[15,8,128]{2,1,0:T(8,128)S(1)}, u32[]{:S(2)}, u32[]{:S(2)}) collective-permute-start(f32[15,8,128]{2,1,0:T(8,128)S(1)} %get-tuple-element.23.mine_ref), channel_id=1, source_target_pairs={{0,8},{8,16},{16,24},{24,32},{32,40},{40,48},{48,56},{56,0},{1,9},... | collective-permute-start | bytes 184328 | tf_op jit(solution)/shard_map/ppermute | solution.py:404
  29.1 5.4 %collective-permute-done.2.low_ref.y1_ref = f32[15,8,128]{2,1,0:T(8,128)S(1)} collective-permute-done((f32[15,8,128]{2,1,0:T(8,128)S(1)}, f32[15,8,128]{2,1,0:T(8,128)S(1)}, u32[]{:S(2)}, u32[]{:S(2)}) %collective-permute-start.2) | collective-permute-done | bytes 61472 | tf_op jit(solution)/shard_map/ppermute | solution.py:404
  34.5 0.0 collective-permute-start.5
  34.5 0.5 collective-permute-start.4
  35.0 1.2 %collective-permute-done.5.z2_ref.high_ref = f32[12,8,128]{2,1,0:T(8,128)S(1)} collective-permute-done((f32[12,8,128]{2,1,0:T(8,128)S(1)}, f32[12,8,128]{2,1,0:T(8,128)S(1)}, u32[]{:S(2)}, u32[]{:S(2)}) %collective-permute-start.5) | collective-permute-done | bytes 49184 | tf_op jit(solution)/shard_map/ppermute | solution.py:405
  36.3 1.8 %collective-permute-done.4.z1_ref.low_ref = f32[12,8,128]{2,1,0:T(8,128)S(1)} collective-permute-done((f32[12,8,128]{2,1,0:T(8,128)S(1)}, f32[12,8,128]{2,1,0:T(8,128)S(1)}, u32[]{:S(2)}, u32[]{:S(2)}) %collective-permute-start.4) | collective-permute-done | bytes 49184 | tf_op jit(solution)/shard_map/ppermute | solution.py:404
  38.1 10.0 %all_to_all.33 = f32[4,1,128]{2,1,0:T(1,128)S(1)} all-to-all(f32[4,1,128]{2,1,0:T(1,128)S(1)} %bitcast.13), channel_id=1, replica_groups={{0,128,256,384},{64,192,320,448},{1,129,257,385},{65,193,321,449},{2,13..., dimensions={0} | all-to-all | bytes 4096 | tf_op jit(solution)/shard_map/all_to_all | solution.py:412
  48.1 11.5 %all_to_all.34 = f32[4,1,128]{2,1,0:T(1,128)S(1)} all-to-all(f32[4,1,128]{2,1,0:T(1,128)S(1)} %bitcast.15), channel_id=1, replica_groups={{0,16,32,48},{8,24,40,56},{1,17,33,49},{9,25,41,57},{2,18,34,50},{10,26..., dimensions={0} | all-to-all | bytes 4096 | tf_op jit(solution)/shard_map/all_to_all | solution.py:412
  59.6 0.6 shard_map.67
  60.2 4.9 %all-to-all-start.2 = ((f32[4,1,128]{2,1,0:T(1,128)}), f32[4,1,128]{2,1,0:T(1,128)S(1)}, u32[]{:S(2)}, u32[]{:S(2)}) async-start(f32[4,1,128]{2,1,0:T(1,128)} %bitcast.7), calls=%async_computation.2 | async-start | bytes 4096 | tf_op jit(solution)/shard_map/all_to_all | solution.py:412
  65.1 1.1 %shard_map.63.rate_ref = f32[5,4,16,256]{3,2,1,0:T(8,128)S(1)} custom-call(f32[5,4,16,256]{3,2,1,0:T(8,128)S(1)} %copy-done.1, f32[30,8,128]{2,1,0:T(8,128)S(1)} %collective-permute-done.low_ref.x1_ref, f32[30,8,128]{2,1,0:T(8,128)S(1)} %collective-permute-done.1.high_ref.x2_ref, f32[15,8,128]{2,1,0:T(8,128)S(1)} %collective-permute-done.2.low_ref.y1_ref, ...), custom_call_target="tpu_custom_call" | custom-call | tf_op jit(solution)/shard_map/pallas_call | solution.py:443
  66.3 2.1 %shard_map.64 = (f32[4,4,16,256]{3,2,1,0:T(8,128)S(1)}, f32[14,8,128]{2,1,0:T(8,128)S(1)}, f32[14,8,128]{2,1,0:T(8,128)S(1)}) custom-call(f32[5,4,16,256]{3,2,1,0:T(8,128)S(1)} %copy-done.1, f32[12,8,128]{2,1,0:T(8,128)S(1)} %collective-permute-done.4.z1_ref.low_ref, f32[12,8,128]{2,1,0:T(8,128)S(1)} %collective-permute-done.5.z2_ref.high_ref, ...), custom_call_target="tpu_custom_call" | custom-call | tf_op jit(solution)/shard_map/pallas_call | solution.py:446
  68.4 0.5 all-to-all-done.2
  68.9 0.9 %shard_map.68 = (f32[5,4,16,256]{3,2,1,0:T(8,128)}, f32[3,3,3,3,64]{4,3,2,1,0:T(4,128)}) custom-call(f32[5,4,16,256]{3,2,1,0:T(8,128)S(1)} %copy-done.1, f32[5,4,16,256]{3,2,1,0:T(8,128)S(1)} %shard_map.63.rate_ref, f32[4,4,16,256]{3,2,1,0:T(8,128)S(1)} %get-tuple-element.29.dep_ref, f32[4,128]{1,0:T(4,128)S(1)} %bitcast.12, ...), custom_call_target="tpu_custom_call" | custom-call | tf_op jit(solution)/shard_map/pallas_call | solution.py:458
  (12 shorter events, 0.1 us)
Async XLA Ops:
  0.6 1.0 %copy-start = (f32[5,4,16,256]{3,2,1,0:T(8,128)S(1)}, f32[5,4,16,256]{3,2,1,0:T(8,128)}, u32[]{:S(2)}) copy-start(f32[5,4,16,256]{3,2,1,0:T(8,128)} %u_ref.7) | copy-start | bytes 983044
  1.6 0.9 %copy-start.2 = (f32[3,3,3,8,64]{4,3,2,1,0:T(8,128)S(1)}, f32[3,3,3,8,64]{4,3,2,1,0:T(8,128)}, u32[]{:S(2)}) copy-start(f32[3,3,3,8,64]{4,3,2,1,0:T(8,128)} %data_ref.1) | copy-start | bytes 165892
  1.6 0.9 %copy-start.3 = (s32[3,3,3,64]{3,2,1,0:T(4,128)S(1)}, s32[3,3,3,64]{3,2,1,0:T(4,128)}, u32[]{:S(2)}) copy-start(s32[3,3,3,64]{3,2,1,0:T(4,128)} %host_ref.1) | copy-start | bytes 20740
  1.6 0.9 %copy-start.4 = (s32[3,3,3]{2,1,0:T(4,128)S(1)}, s32[3,3,3]{2,1,0:T(4,128)}, u32[]{:S(2)}) copy-start(s32[3,3,3]{2,1,0:T(4,128)} %count_ref.1) | copy-start | bytes 328
  2.7 13.5 %collective-permute-start.1 = (f32[30,8,128]{2,1,0:T(8,128)S(1)}, f32[30,8,128]{2,1,0:T(8,128)S(1)}, u32[]{:S(2)}, u32[]{:S(2)}) collective-permute-start(f32[30,8,128]{2,1,0:T(8,128)S(1)} %get-tuple-element.20), channel_id=1, source_target_pairs={{64,0},{128,64},{192,128},{256,192},{320,256},{384,320},{448,384},... | collective-permute-start | bytes 368648 | tf_op jit(solution)/shard_map/ppermute | solution.py:405
  13.6 8.0 %collective-permute-start = (f32[30,8,128]{2,1,0:T(8,128)S(1)}, f32[30,8,128]{2,1,0:T(8,128)S(1)}, u32[]{:S(2)}, u32[]{:S(2)}) collective-permute-start(f32[30,8,128]{2,1,0:T(8,128)S(1)} %get-tuple-element.19.mine_ref), channel_id=1, source_target_pairs={{0,64},{64,128},{128,192},{192,256},{256,320},{320,384},{384,448},... | collective-permute-start | bytes 368648 | tf_op jit(solution)/shard_map/ppermute | solution.py:404
  21.6 43.5 %copy-start.1 = (f32[5,4,16,256]{3,2,1,0:T(8,128)S(1)}, f32[5,4,16,256]{3,2,1,0:T(8,128)}, u32[]{:S(2)}) copy-start(f32[5,4,16,256]{3,2,1,0:T(8,128)} %u_ref.7) | copy-start | bytes 983044
  21.7 7.4 %collective-permute-start.3 = (f32[15,8,128]{2,1,0:T(8,128)S(1)}, f32[15,8,128]{2,1,0:T(8,128)S(1)}, u32[]{:S(2)}, u32[]{:S(2)}) collective-permute-start(f32[15,8,128]{2,1,0:T(8,128)S(1)} %get-tuple-element.24), channel_id=1, source_target_pairs={{8,0},{16,8},{24,16},{32,24},{40,32},{48,40},{56,48},{0,56},{9,1},... | collective-permute-start | bytes 184328 | tf_op jit(solution)/shard_map/ppermute | solution.py:405
  27.2 7.3 %collective-permute-start.2 = (f32[15,8,128]{2,1,0:T(8,128)S(1)}, f32[15,8,128]{2,1,0:T(8,128)S(1)}, u32[]{:S(2)}, u32[]{:S(2)}) collective-permute-start(f32[15,8,128]{2,1,0:T(8,128)S(1)} %get-tuple-element.23.mine_ref), channel_id=1, source_target_pairs={{0,8},{8,16},{16,24},{24,32},{32,40},{40,48},{48,56},{56,0},{1,9},... | collective-permute-start | bytes 184328 | tf_op jit(solution)/shard_map/ppermute | solution.py:404
  34.5 1.8 %collective-permute-start.5 = (f32[12,8,128]{2,1,0:T(8,128)S(1)}, f32[12,8,128]{2,1,0:T(8,128)S(1)}, u32[]{:S(2)}, u32[]{:S(2)}) collective-permute-start(f32[12,8,128]{2,1,0:T(8,128)S(1)} %get-tuple-element.27), channel_id=1, source_target_pairs={{1,0},{2,1},{3,2},{4,3},{5,4},{6,5},{7,6},{0,7},{9,8},{10,9},{11,1... | collective-permute-start | bytes 147464 | tf_op jit(solution)/shard_map/ppermute | solution.py:405
  34.5 3.5 %collective-permute-start.4 = (f32[12,8,128]{2,1,0:T(8,128)S(1)}, f32[12,8,128]{2,1,0:T(8,128)S(1)}, u32[]{:S(2)}, u32[]{:S(2)}) collective-permute-start(f32[12,8,128]{2,1,0:T(8,128)S(1)} %get-tuple-element.26.mine_ref), channel_id=1, source_target_pairs={{0,1},{1,2},{2,3},{3,4},{4,5},{5,6},{6,7},{7,0},{8,9},{9,10},{10,1... | collective-permute-start | bytes 147464 | tf_op jit(solution)/shard_map/ppermute | solution.py:404
  60.2 8.7 %all-to-all-start.2 = ((f32[4,1,128]{2,1,0:T(1,128)}), f32[4,1,128]{2,1,0:T(1,128)S(1)}, u32[]{:S(2)}, u32[]{:S(2)}) async-start(f32[4,1,128]{2,1,0:T(1,128)} %bitcast.7), calls=%async_computation.2 | async-start | bytes 4096 | tf_op jit(solution)/shard_map/all_to_all | solution.py:412

commit v5 on v4

--- a/solution.py
+++ b/solution.py
@@ -9,6 +9,7 @@
 F32 = jnp.float32
 BF16 = jnp.bfloat16
 VMEM_BYTES = 24 * 1024 * 1024
+TURN_BYTES = 16 * 1024 * 1024
 
 NODES = np.array([-1.0, -1.0 / np.sqrt(5.0), 1.0 / np.sqrt(5.0), 1.0])
 WEIGHTS = np.array([1.0 / 6.0, 5.0 / 6.0, 5.0 / 6.0, 1.0 / 6.0])
@@ -27,7 +28,7 @@
 DERIV = derivative_table()
 SCALE = [1.0 / np.prod([NODES[i] - NODES[j] for j in range(4) if j != i]) for i in range(4)]
 
-TOP, FACE = 9, 10
+FACE = 9
 
 
 def by_pos(pos, values):
@@ -65,20 +66,18 @@
     return lambda tile: ref[tile]
 
 
-def face_kernel(u_ref, up_ref, down_ref, face_ref):
+def face_kernel(u_ref, up_ref, down_ref, face_ref, top_ref):
     top = None
     for i in range(4):
         _, _, sound, square = primitives([u_ref[v, i] for v in range(5)])
         speed = jnp.sqrt(square) + sound
         top = speed if top is None else jnp.maximum(top, speed)
     top = jnp.maximum(top[:, :128], top[:, 128:])
-    top = jnp.maximum(top[:8], top[8:])
-    up_ref[0] = top
-    down_ref[0] = top
+    top_ref[...] = jnp.broadcast_to(jnp.max(top, axis=0, keepdims=True), top_ref.shape)
     for v in range(5):
         for yh in range(2):
             for zh in range(2):
-                tile = 1 + 4 * v + 2 * yh + zh
+                tile = 4 * v + 2 * yh + zh
                 ys, zs = slice(8 * yh, 8 * yh + 8), slice(128 * zh, 128 * zh + 128)
                 up_ref[tile] = u_ref[v, 3, ys, zs]
                 down_ref[tile] = u_ref[v, 0, ys, zs]
@@ -111,45 +110,34 @@
                 code = jnp.where(slot < count, host + 1, 0).astype(F32)
                 out[3 * b + c, :, 0:64] = data_ref[a, b, c]
                 out[3 * b + c, :, 64:128] = jnp.broadcast_to(code, (8, 64))
-    for t in range(21):
-        up_ref[TOP + t] = face_up_ref[t]
-        down_ref[TOP + t] = face_down_ref[t]
-
-
-def turn_y_kernel(low_ref, high_ref, own_ref, face_ref, mine_ref, up_ref, down_ref, keep_ref):
+    for t in range(20):
+        up_ref[FACE + t] = face_up_ref[t]
+        down_ref[FACE + t] = face_down_ref[t]
+
+
+def turn_y_kernel(low_ref, high_ref, own_ref, face_ref, up_ref, down_ref, keep_ref):
     for a, source in enumerate((low_ref, own_ref, high_ref)):
         for c in range(3):
             up_ref[3 * a + c] = source[6 + c]
             down_ref[3 * a + c] = source[c]
             keep_ref[3 * a + c] = source[3 + c]
-    top = jnp.maximum(jnp.maximum(low_ref[TOP], high_ref[TOP]), mine_ref[TOP])
-    up_ref[TOP] = top
-    down_ref[TOP] = top
     for v in range(5):
         up_ref[FACE + v] = face_ref[v]
         down_ref[FACE + v] = face_ref[5 + v]
 
 
-def turn_z_kernel(low_ref, high_ref, own_ref, face_ref, mine_ref, up_ref, down_ref, keep_ref):
+def turn_z_kernel(low_ref, high_ref, own_ref, face_ref, up_ref, down_ref, keep_ref):
     for b, source in enumerate((low_ref, own_ref, high_ref)):
         for a in range(3):
             up_ref[3 * a + b] = source[3 * a + 2]
             down_ref[3 * a + b] = source[3 * a]
             keep_ref[3 * a + b] = source[3 * a + 1]
-    top = jnp.maximum(jnp.maximum(low_ref[TOP], high_ref[TOP]), mine_ref[TOP])
-    up_ref[TOP] = top
-    down_ref[TOP] = top
     for yh in range(2):
         up_ref[FACE + yh] = face_ref[10 + yh]
         down_ref[FACE + yh] = face_ref[12 + yh]
 
 
-def top_kernel(low_ref, high_ref, mine_ref, top_ref):
-    top = jnp.maximum(jnp.maximum(low_ref[TOP], high_ref[TOP]), mine_ref[TOP])
-    top_ref[...] = jnp.broadcast_to(jnp.max(top, axis=0, keepdims=True), top_ref.shape)
-
-
-def fold_kernel(tops_ref, top_ref):
+def fold_kernel(tops_ref, turned_ref, top_ref):
     top_ref[...] = jnp.broadcast_to(jnp.max(tops_ref[...], axis=0, keepdims=True), top_ref.shape)
 
 
@@ -398,26 +386,27 @@
                 vel_ref[g // 9, g // 3 % 3, g % 3] = value[0:3, 64 * h : 64 * h + 64]
 
 
-def exchanged(up, down, axis):
+def exchanged(up, down, axis, wrap):
     count = lax.axis_size(axis)
+    pairs = [(i, (i + 1) % count) for i in range(count if wrap else count - 1)]
     return (
-        lax.ppermute(up, axis, [(i, (i + 1) % count) for i in range(count)]),
-        lax.ppermute(down, axis, [((i + 1) % count, i) for i in range(count)]),
-    )
-
-
-def spread_top(top, axis):
-    count = lax.axis_size(axis)
-    groups = [list(range(0, count, 2)), list(range(1, count, 2))]
-    return lax.all_to_all(top, axis, 0, 0, axis_index_groups=groups, tiled=True)
-
-
-def call(kernel, outs, scratch=()):
+        lax.ppermute(up, axis, pairs),
+        lax.ppermute(down, axis, [(j, i) for i, j in pairs]),
+    )
+
+
+def all_tops(top, axis):
+    return lax.all_to_all(top, axis, 0, 0, tiled=True)
+
+
+def call(kernel, outs, scratch=(), nbytes=None):
+    cost = None if nbytes is None else pl.CostEstimate(flops=0, bytes_accessed=nbytes, transcendentals=0)
     return pl.pallas_call(
         kernel,
         out_shape=outs,
         scratch_shapes=list(scratch),
         compiler_params=pltpu.CompilerParams(vmem_limit_bytes=VMEM_BYTES),
+        cost_estimate=cost,
     )
 
 
@@ -426,19 +415,23 @@
 
 
 def local(fluid_state, parcel_data, host_element, slot_counts):
-    face_up, face_down, faces = call(face_kernel, (tiles_of(21), tiles_of(21), tiles_of(14)))(fluid_state)
-    x_up, x_down, keep_x = call(pack_kernel, (tiles_of(30), tiles_of(30), tiles_of(9)))(
+    rows = [jax.ShapeDtypeStruct((lax.axis_size(axis), 128), F32) for axis in ("gx", "gy", "gz")]
+    face_up, face_down, faces, top = call(face_kernel, (tiles_of(20), tiles_of(20), tiles_of(14), rows[0]))(fluid_state)
+    x_up, x_down, keep_x = call(pack_kernel, (tiles_of(29), tiles_of(29), tiles_of(9)))(
         parcel_data, host_element, slot_counts, face_up, face_down
     )
-    x1, x2 = exchanged(x_up, x_down, "gx")
-    y_up, y_down, keep_y = call(turn_y_kernel, (tiles_of(15), tiles_of(15), tiles_of(9)))(x1, x2, keep_x, faces, x_up)
-    y1, y2 = exchanged(y_up, y_down, "gy")
-    z_up, z_down, keep_z = call(turn_z_kernel, (tiles_of(12), tiles_of(12), tiles_of(9)))(y1, y2, keep_y, faces, y_up)
-    z1, z2 = exchanged(z_up, z_down, "gz")
-    rows = [jax.ShapeDtypeStruct((max(1, lax.axis_size(axis) // 2), 128), F32) for axis in ("gx", "gy", "gz")]
-    top = spread_top(call(top_kernel, rows[0])(z1, z2, z_up), "gx")
-    top = spread_top(call(fold_kernel, rows[1])(top), "gy")
-    top = spread_top(call(fold_kernel, rows[2])(top), "gz")
+    x1, x2 = exchanged(x_up, x_down, "gx", False)
+    tops = all_tops(top, "gx")
+    y_up, y_down, keep_y = call(turn_y_kernel, (tiles_of(14), tiles_of(14), tiles_of(9)), nbytes=TURN_BYTES)(
+        x1, x2, keep_x, faces
+    )
+    y1, y2 = exchanged(y_up, y_down, "gy", False)
+    tops = all_tops(call(fold_kernel, rows[1])(tops, keep_y), "gy")
+    z_up, z_down, keep_z = call(turn_z_kernel, (tiles_of(11), tiles_of(11), tiles_of(9)), nbytes=TURN_BYTES)(
+        y1, y2, keep_y, faces
+    )
+    z1, z2 = exchanged(z_up, z_down, "gz", True)
+    top = all_tops(call(fold_kernel, rows[2])(tops, keep_z), "gz")
     field = jax.ShapeDtypeStruct((5, 4, 16, 256), F32)
     rate = call(
         rate_kernel, field, [pltpu.VMEM((5, 4, 16, 256), F32), pltpu.VMEM((2, 16, 256), F32)],

time: 70.1 us -> 69.4 us (0.990)
  the two profiles are of different devices: /device:TPU:2 before, /device:TPU:1 now
where the time goes in v5:
time: 69.4 us; the launch traced here: 69 us
  blocking collectives  28.6 us (41%)
  starting transfers between devices  23.2 us (33%)
  waiting for transfers between devices  9.77 us (14%)
  Pallas kernels  5.1 us (7%)
  local copies, waits for them, and re-layouts  1.67 us (2%)
  between operations  0.73 us (1%)
    all_to_all x2, blocking collectives, all_tops(): return lax.all_to_all(top, axis, 0, 0, tiled=True)  28.6 us
    ppermute x3, starting transfers between devices, exchanged(): lax.ppermute(up, axis, pairs)  12.7 us
    ppermute x3, waiting for transfers between devices, exchanged(): lax.ppermute(down, axis, [(j, i) for i, j in pairs])  8.02 us
    all_to_all x1, starting transfers between devices, all_tops(): return lax.all_to_all(top, axis, 0, 0, tiled=True)  7.93 us
    ppermute x3, starting transfers between devices, exchanged(): lax.ppermute(down, axis, [(j, i) for i, j in pairs])  2.59 us
    pallas_call x1, Pallas kernels, local(): call(parcel_kernel, (jax.ShapeDtypeStruct((4, 4, 16, 256), F32), tiles_of...  2.1 us
    unnamed x10, local copies, waits for them, and re-layouts  1.67 us
  transfers between devices with their start and end apart: 7, of which 4 were waited for; matrix products, arithmetic and copies ran while one was open for 0% of the time, Pallas kernels for 6%

profile of v5, /device:TPU:1, one launch (start us, length us, event | category | flops | bytes accessed | tf_op | source)
XLA Modules:
  0.0 69.0 jit_solution(15913319297480652457)
XLA Ops:
  0.6 0.0 copy-start
  0.6 1.0 %copy-done = f32[5,4,16,256]{3,2,1,0:T(8,128)S(1)} copy-done((f32[5,4,16,256]{3,2,1,0:T(8,128)S(1)}, f32[5,4,16,256]{3,2,1,0:T(8,128)}, u32[]{:S(2)}) %copy-start) | copy-done | bytes 327704
  1.6 0.2 shard_map.59
  1.8 0.7 %copy-done.2 = f32[3,3,3,8,64]{4,3,2,1,0:T(8,128)S(1)} copy-done((f32[3,3,3,8,64]{4,3,2,1,0:T(8,128)S(1)}, f32[3,3,3,8,64]{4,3,2,1,0:T(8,128)}, u32[]{:S(2)}) %copy-start.2) | copy-done | bytes 55320
  2.5 0.2 shard_map.60
  2.7 4.8 %collective-permute-start = (f32[29,8,128]{2,1,0:T(8,128)S(1)}, f32[29,8,128]{2,1,0:T(8,128)S(1)}, u32[]{:S(2)}, u32[]{:S(2)}) collective-permute-start(f32[29,8,128]{2,1,0:T(8,128)S(1)} %get-tuple-element.20), channel_id=1, source_target_pairs={{0,64},{64,128},{128,192},{192,256},{256,320},{320,384},{384,448},... | collective-permute-start | bytes 356360 | tf_op jit(solution)/shard_map/ppermute | solution.py:393
  7.5 1.3 %collective-permute-start.1 = (f32[29,8,128]{2,1,0:T(8,128)S(1)}, f32[29,8,128]{2,1,0:T(8,128)S(1)}, u32[]{:S(2)}, u32[]{:S(2)}) collective-permute-start(f32[29,8,128]{2,1,0:T(8,128)S(1)} %get-tuple-element.21), channel_id=1, source_target_pairs={{64,0},{128,64},{192,128},{256,192},{320,256},{384,320},{448,384},... | collective-permute-start | bytes 356360 | tf_op jit(solution)/shard_map/ppermute | solution.py:394
  8.8 0.5 collective-permute-done.low_ref.x1_ref
  9.3 4.4 %collective-permute-done.1.high_ref.x2_ref = f32[29,8,128]{2,1,0:T(8,128)S(1)} collective-permute-done((f32[29,8,128]{2,1,0:T(8,128)S(1)}, f32[29,8,128]{2,1,0:T(8,128)S(1)}, u32[]{:S(2)}, u32[]{:S(2)}) %collective-permute-start.1) | collective-permute-done | bytes 118816 | tf_op jit(solution)/shard_map/ppermute | solution.py:394
  13.8 3.8 %collective-permute-start.2 = (f32[14,8,128]{2,1,0:T(8,128)S(1)}, f32[14,8,128]{2,1,0:T(8,128)S(1)}, u32[]{:S(2)}, u32[]{:S(2)}) collective-permute-start(f32[14,8,128]{2,1,0:T(8,128)S(1)} %get-tuple-element.24), channel_id=1, source_target_pairs={{0,8},{8,16},{16,24},{24,32},{32,40},{40,48},{48,56},{1,9},{9,17},... | collective-permute-start | bytes 172040 | tf_op jit(solution)/shard_map/ppermute | solution.py:393
  17.5 1.3 %collective-permute-start.3 = (f32[14,8,128]{2,1,0:T(8,128)S(1)}, f32[14,8,128]{2,1,0:T(8,128)S(1)}, u32[]{:S(2)}, u32[]{:S(2)}) collective-permute-start(f32[14,8,128]{2,1,0:T(8,128)S(1)} %get-tuple-element.25), channel_id=1, source_target_pairs={{8,0},{16,8},{24,16},{32,24},{40,32},{48,40},{56,48},{9,1},{17,9},... | collective-permute-start | bytes 172040 | tf_op jit(solution)/shard_map/ppermute | solution.py:394
  18.8 0.0 collective-permute-done.2.low_ref.y1_ref
  18.8 3.6 %collective-permute-done.3.high_ref.y2_ref = f32[14,8,128]{2,1,0:T(8,128)S(1)} collective-permute-done((f32[14,8,128]{2,1,0:T(8,128)S(1)}, f32[14,8,128]{2,1,0:T(8,128)S(1)}, u32[]{:S(2)}, u32[]{:S(2)}) %collective-permute-start.3) | collective-permute-done | bytes 57376 | tf_op jit(solution)/shard_map/ppermute | solution.py:394
  22.5 4.1 %collective-permute-start.4 = (f32[11,8,128]{2,1,0:T(8,128)S(1)}, f32[11,8,128]{2,1,0:T(8,128)S(1)}, u32[]{:S(2)}, u32[]{:S(2)}) collective-permute-start(f32[11,8,128]{2,1,0:T(8,128)S(1)} %get-tuple-element.27), channel_id=1, source_target_pairs={{0,1},{1,2},{2,3},{3,4},{4,5},{5,6},{6,7},{7,0},{8,9},{9,10},{10,1... | collective-permute-start | bytes 135176 | tf_op jit(solution)/shard_map/ppermute | solution.py:393
  26.5 0.0 collective-permute-start.5
  26.5 15.2 %all_to_all.33 = f32[8,1,128]{2,1,0:T(1,128)S(1)} all-to-all(f32[8,1,128]{2,1,0:T(1,128)S(1)} %bitcast.16), channel_id=1, replica_groups=mesh['gx'=8,'gy'=8,'gz'=8] {'gx'}, dimensions={0} | all-to-all | bytes 8192 | tf_op jit(solution)/shard_map/all_to_all | solution.py:399
  41.8 13.3 %all_to_all.34 = f32[8,1,128]{2,1,0:T(1,128)S(1)} all-to-all(f32[8,1,128]{2,1,0:T(1,128)S(1)} %bitcast.14), channel_id=1, replica_groups=mesh['gx'=8,'gy'=8,'gz'=8] {'gy'}, dimensions={0} | all-to-all | bytes 8192 | tf_op jit(solution)/shard_map/all_to_all | solution.py:399
  55.1 0.6 shard_map.66
  55.7 7.9 %all-to-all-start.2 = ((f32[8,1,128]{2,1,0:T(1,128)}), f32[8,1,128]{2,1,0:T(1,128)S(1)}, u32[]{:S(2)}, u32[]{:S(2)}) async-start(f32[8,1,128]{2,1,0:T(1,128)} %bitcast.7), calls=%async_computation.2 | async-start | bytes 8192 | tf_op jit(solution)/shard_map/all_to_all | solution.py:399
  63.6 0.0 collective-permute-done.5.z2_ref
  63.7 1.1 %shard_map.63.rate_ref = f32[5,4,16,256]{3,2,1,0:T(8,128)S(1)} custom-call(f32[5,4,16,256]{3,2,1,0:T(8,128)S(1)} %copy-done.1, f32[29,8,128]{2,1,0:T(8,128)S(1)} %collective-permute-done.low_ref.x1_ref, f32[29,8,128]{2,1,0:T(8,128)S(1)} %collective-permute-done.1.high_ref.x2_ref, f32[14,8,128]{2,1,0:T(8,128)S(1)} %collective-permute-done.2.low_ref.y1_ref, ...), custom_call_target="tpu_custom_call" | custom-call | tf_op jit(solution)/shard_map/pallas_call | solution.py:436
  64.8 2.1 %shard_map.64 = (f32[4,4,16,256]{3,2,1,0:T(8,128)S(1)}, f32[14,8,128]{2,1,0:T(8,128)S(1)}, f32[14,8,128]{2,1,0:T(8,128)S(1)}) custom-call(f32[5,4,16,256]{3,2,1,0:T(8,128)S(1)} %copy-done.1, f32[11,8,128]{2,1,0:T(8,128)S(1)} %collective-permute-done.4.z1_ref, f32[11,8,128]{2,1,0:T(8,128)S(1)} %collective-permute-done.5.z2_ref, ...), custom_call_target="tpu_custom_call" | custom-call | tf_op jit(solution)/shard_map/pallas_call | solution.py:439
  66.9 1.2 %all-to-all-done.2 = f32[8,1,128]{2,1,0:T(1,128)S(1)} async-done(((f32[8,1,128]{2,1,0:T(1,128)}), f32[8,1,128]{2,1,0:T(1,128)S(1)}, u32[]{:S(2)}, u32[]{:S(2)}) %all-to-all-start.2) | async-done | bytes 4128 | tf_op jit(solution)/shard_map/all_to_all | solution.py:399
  68.2 0.9 %shard_map.67 = (f32[5,4,16,256]{3,2,1,0:T(8,128)}, f32[3,3,3,3,64]{4,3,2,1,0:T(4,128)}) custom-call(f32[5,4,16,256]{3,2,1,0:T(8,128)S(1)} %copy-done.1, f32[5,4,16,256]{3,2,1,0:T(8,128)S(1)} %shard_map.63.rate_ref, f32[4,4,16,256]{3,2,1,0:T(8,128)S(1)} %get-tuple-element.30.dep_ref, f32[8,128]{1,0:T(8,128)S(1)} %bitcast.12, ...), custom_call_target="tpu_custom_call" | custom-call | tf_op jit(solution)/shard_map/pallas_call | solution.py:451
  (11 shorter events, 0.0 us)
Async XLA Ops:
  0.6 1.0 %copy-start = (f32[5,4,16,256]{3,2,1,0:T(8,128)S(1)}, f32[5,4,16,256]{3,2,1,0:T(8,128)}, u32[]{:S(2)}) copy-start(f32[5,4,16,256]{3,2,1,0:T(8,128)} %u_ref.7) | copy-start | bytes 983044
  1.6 0.9 %copy-start.2 = (f32[3,3,3,8,64]{4,3,2,1,0:T(8,128)S(1)}, f32[3,3,3,8,64]{4,3,2,1,0:T(8,128)}, u32[]{:S(2)}) copy-start(f32[3,3,3,8,64]{4,3,2,1,0:T(8,128)} %data_ref.1) | copy-start | bytes 165892
  1.6 0.9 %copy-start.3 = (s32[3,3,3,64]{3,2,1,0:T(4,128)S(1)}, s32[3,3,3,64]{3,2,1,0:T(4,128)}, u32[]{:S(2)}) copy-start(s32[3,3,3,64]{3,2,1,0:T(4,128)} %host_ref.1) | copy-start | bytes 20740
  1.6 0.9 %copy-start.4 = (s32[3,3,3]{2,1,0:T(4,128)S(1)}, s32[3,3,3]{2,1,0:T(4,128)}, u32[]{:S(2)}) copy-start(s32[3,3,3]{2,1,0:T(4,128)} %count_ref.1) | copy-start | bytes 328
  2.7 6.6 %collective-permute-start = (f32[29,8,128]{2,1,0:T(8,128)S(1)}, f32[29,8,128]{2,1,0:T(8,128)S(1)}, u32[]{:S(2)}, u32[]{:S(2)}) collective-permute-start(f32[29,8,128]{2,1,0:T(8,128)S(1)} %get-tuple-element.20), channel_id=1, source_target_pairs={{0,64},{64,128},{128,192},{192,256},{256,320},{320,384},{384,448},... | collective-permute-start | bytes 356360 | tf_op jit(solution)/shard_map/ppermute | solution.py:393
  7.5 6.2 %collective-permute-start.1 = (f32[29,8,128]{2,1,0:T(8,128)S(1)}, f32[29,8,128]{2,1,0:T(8,128)S(1)}, u32[]{:S(2)}, u32[]{:S(2)}) collective-permute-start(f32[29,8,128]{2,1,0:T(8,128)S(1)} %get-tuple-element.21), channel_id=1, source_target_pairs={{64,0},{128,64},{192,128},{256,192},{320,256},{384,320},{448,384},... | collective-permute-start | bytes 356360 | tf_op jit(solution)/shard_map/ppermute | solution.py:394
  13.7 49.9 %copy-start.1 = (f32[5,4,16,256]{3,2,1,0:T(8,128)S(1)}, f32[5,4,16,256]{3,2,1,0:T(8,128)}, u32[]{:S(2)}) copy-start(f32[5,4,16,256]{3,2,1,0:T(8,128)} %u_ref.7) | copy-start | bytes 983044
  13.8 5.1 %collective-permute-start.2 = (f32[14,8,128]{2,1,0:T(8,128)S(1)}, f32[14,8,128]{2,1,0:T(8,128)S(1)}, u32[]{:S(2)}, u32[]{:S(2)}) collective-permute-start(f32[14,8,128]{2,1,0:T(8,128)S(1)} %get-tuple-element.24), channel_id=1, source_target_pairs={{0,8},{8,16},{16,24},{24,32},{32,40},{40,48},{48,56},{1,9},{9,17},... | collective-permute-start | bytes 172040 | tf_op jit(solution)/shard_map/ppermute | solution.py:393
  17.5 4.9 %collective-permute-start.3 = (f32[14,8,128]{2,1,0:T(8,128)S(1)}, f32[14,8,128]{2,1,0:T(8,128)S(1)}, u32[]{:S(2)}, u32[]{:S(2)}) collective-permute-start(f32[14,8,128]{2,1,0:T(8,128)S(1)} %get-tuple-element.25), channel_id=1, source_target_pairs={{8,0},{16,8},{24,16},{32,24},{40,32},{48,40},{56,48},{9,1},{17,9},... | collective-permute-start | bytes 172040 | tf_op jit(solution)/shard_map/ppermute | solution.py:394
  22.5 41.2 %collective-permute-start.4 = (f32[11,8,128]{2,1,0:T(8,128)S(1)}, f32[11,8,128]{2,1,0:T(8,128)S(1)}, u32[]{:S(2)}, u32[]{:S(2)}) collective-permute-start(f32[11,8,128]{2,1,0:T(8,128)S(1)} %get-tuple-element.27), channel_id=1, source_target_pairs={{0,1},{1,2},{2,3},{3,4},{4,5},{5,6},{6,7},{7,0},{8,9},{9,10},{10,1... | collective-permute-start | bytes 135176 | tf_op jit(solution)/shard_map/ppermute | solution.py:393
  26.5 37.1 %collective-permute-start.5 = (f32[11,8,128]{2,1,0:T(8,128)S(1)}, f32[11,8,128]{2,1,0:T(8,128)S(1)}, u32[]{:S(2)}, u32[]{:S(2)}) collective-permute-start(f32[11,8,128]{2,1,0:T(8,128)S(1)} %get-tuple-element.28), channel_id=1, source_target_pairs={{1,0},{2,1},{3,2},{4,3},{5,4},{6,5},{7,6},{0,7},{9,8},{10,9},{11,1... | collective-permute-start | bytes 135176 | tf_op jit(solution)/shard_map/ppermute | solution.py:394
  55.7 12.4 %all-to-all-start.2 = ((f32[8,1,128]{2,1,0:T(1,128)}), f32[8,1,128]{2,1,0:T(1,128)S(1)}, u32[]{:S(2)}, u32[]{:S(2)}) async-start(f32[8,1,128]{2,1,0:T(1,128)} %bitcast.7), calls=%async_computation.2 | async-start | bytes 8192 | tf_op jit(solution)/shard_map/all_to_all | solution.py:399

commit v6 on v5

--- a/solution.py
+++ b/solution.py
@@ -9,7 +9,7 @@
 F32 = jnp.float32
 BF16 = jnp.bfloat16
 VMEM_BYTES = 24 * 1024 * 1024
-TURN_BYTES = 16 * 1024 * 1024
+TURN_BYTES = 64 * 1024 * 1024
 
 NODES = np.array([-1.0, -1.0 / np.sqrt(5.0), 1.0 / np.sqrt(5.0), 1.0])
 WEIGHTS = np.array([1.0 / 6.0, 5.0 / 6.0, 5.0 / 6.0, 1.0 / 6.0])
@@ -126,7 +126,7 @@
         down_ref[FACE + v] = face_ref[5 + v]
 
 
-def turn_z_kernel(low_ref, high_ref, own_ref, face_ref, up_ref, down_ref, keep_ref):
+def turn_z_kernel(low_ref, high_ref, own_ref, face_ref, folded_ref, up_ref, down_ref, keep_ref):
     for b, source in enumerate((low_ref, own_ref, high_ref)):
         for a in range(3):
             up_ref[3 * a + b] = source[3 * a + 2]
@@ -172,7 +172,7 @@
     return out
 
 
-def rate_kernel(u_ref, x1_ref, x2_ref, y1_ref, y2_ref, z1_ref, z2_ref, face_ref, rate_ref, fx_ref, sx_ref):
+def rate_kernel(u_ref, x1_ref, x2_ref, y1_ref, y2_ref, z1_ref, z2_ref, face_ref, folded_ref, rate_ref, fx_ref, sx_ref):
     x_side = tile_of(x1_ref), tile_of(x2_ref)
     y_side = tile_of(y1_ref), tile_of(y2_ref)
     z_side = tile_of(z1_ref), tile_of(z2_ref)
@@ -426,16 +426,18 @@
         x1, x2, keep_x, faces
     )
     y1, y2 = exchanged(y_up, y_down, "gy", False)
-    tops = all_tops(call(fold_kernel, rows[1])(tops, keep_y), "gy")
+    fold = call(fold_kernel, rows[1])(tops, keep_y)
+    tops = all_tops(fold, "gy")
     z_up, z_down, keep_z = call(turn_z_kernel, (tiles_of(11), tiles_of(11), tiles_of(9)), nbytes=TURN_BYTES)(
-        y1, y2, keep_y, faces
+        y1, y2, keep_y, faces, fold
     )
     z1, z2 = exchanged(z_up, z_down, "gz", True)
-    top = all_tops(call(fold_kernel, rows[2])(tops, keep_z), "gz")
+    fold = call(fold_kernel, rows[2])(tops, keep_z)
+    top = all_tops(fold, "gz")
     field = jax.ShapeDtypeStruct((5, 4, 16, 256), F32)
     rate = call(
         rate_kernel, field, [pltpu.VMEM((5, 4, 16, 256), F32), pltpu.VMEM((2, 16, 256), F32)],
-    )(fluid_state, x1, x2, y1, y2, z1, z2, faces)
+    )(fluid_state, x1, x2, y1, y2, z1, z2, faces, fold)
     deposit, base, acc = call(
         parcel_kernel,
         (jax.ShapeDtypeStruct((4, 4, 16, 256), F32), tiles_of(14), tiles_of(14)),

time: 69.4 us -> 66.8 us (0.963)
  waiting for transfers between devices: 9.77 us -> 5.45 us
  blocking collectives: 28.6 us -> 30.1 us
  Pallas kernels: 5.1 us -> 5.81 us
    ppermute x3, waiting for transfers between devices: 8.02 us -> 4.41 us  [exchanged(): lax.ppermute(down, axis, [(j, i) for i, j in pairs])]
    all_to_all x2, blocking collectives: 28.6 us -> 30.1 us  [all_tops(): return lax.all_to_all(top, axis, 0, 0, tiled=True)]
    all_to_all x1, starting transfers between devices: 7.93 us -> 6.5 us  [all_tops(): return lax.all_to_all(top, axis, 0, 0, tiled=True)]
    ppermute x3, starting transfers between devices: 12.7 us -> 13.5 us  [exchanged(): lax.ppermute(up, axis, pairs)]
    pallas_call x1, Pallas kernels: 1.15 us -> 1.86 us  [local(): call(rate_kernel, field, [pltpu.VMEM((5, 4, 16, 256), F32), pltpu.VMEM((2...]
    all_to_all x1, waiting for transfers between devices: 1.24 us -> 0.53 us  [all_tops(): return lax.all_to_all(top, axis, 0, 0, tiled=True)]
  transfers between devices with their start and end apart: 7 -> 7, of which waited for: 4 -> 3; matrix products, arithmetic and copies ran while one was open for 0% -> 0% of each run, Pallas kernels for 6% -> 7%
where the time goes in v6:
time: 66.8 us; the launch traced here: 66.3 us
  blocking collectives  30.1 us (45%)
  starting transfers between devices  22.6 us (34%)
  Pallas kernels  5.81 us (9%)
  waiting for transfers between devices  5.45 us (8%)
  local copies, waits for them, and re-layouts  1.67 us (2%)
  between operations  0.73 us (1%)
    all_to_all x2, blocking collectives, all_tops(): return lax.all_to_all(top, axis, 0, 0, tiled=True)  30.1 us
    ppermute x3, starting transfers between devices, exchanged(): lax.ppermute(up, axis, pairs)  13.5 us
    all_to_all x1, starting transfers between devices, all_tops(): return lax.all_to_all(top, axis, 0, 0, tiled=True)  6.5 us
    ppermute x3, waiting for transfers between devices, exchanged(): lax.ppermute(down, axis, [(j, i) for i, j in pairs])  4.41 us
    ppermute x3, starting transfers between devices, exchanged(): lax.ppermute(down, axis, [(j, i) for i, j in pairs])  2.59 us
    pallas_call x1, Pallas kernels, local(): call(parcel_kernel, (jax.ShapeDtypeStruct((4, 4, 16, 256), F32), tiles_of...  2.1 us
    pallas_call x1, Pallas kernels, local(): call(rate_kernel, field, [pltpu.VMEM((5, 4, 16, 256), F32), pltpu.VMEM((2...  1.86 us
    unnamed x10, local copies, waits for them, and re-layouts  1.67 us
  transfers between devices with their start and end apart: 7, of which 3 were waited for; matrix products, arithmetic and copies ran while one was open for 0% of the time, Pallas kernels for 7%

profile of v6, /device:TPU:1, one launch (start us, length us, event | category | flops | bytes accessed | tf_op | source)
XLA Modules:
  0.0 66.3 jit_solution(11395895323770275267)
XLA Ops:
  0.6 0.0 copy-start
  0.6 1.0 %copy-done = f32[5,4,16,256]{3,2,1,0:T(8,128)S(1)} copy-done((f32[5,4,16,256]{3,2,1,0:T(8,128)S(1)}, f32[5,4,16,256]{3,2,1,0:T(8,128)}, u32[]{:S(2)}) %copy-start) | copy-done | bytes 327704
  1.6 0.2 shard_map.59
  1.8 0.7 %copy-done.2 = f32[3,3,3,8,64]{4,3,2,1,0:T(8,128)S(1)} copy-done((f32[3,3,3,8,64]{4,3,2,1,0:T(8,128)S(1)}, f32[3,3,3,8,64]{4,3,2,1,0:T(8,128)}, u32[]{:S(2)}) %copy-start.2) | copy-done | bytes 55320
  2.5 0.2 shard_map.60
  2.7 4.8 %collective-permute-start = (f32[29,8,128]{2,1,0:T(8,128)S(1)}, f32[29,8,128]{2,1,0:T(8,128)S(1)}, u32[]{:S(2)}, u32[]{:S(2)}) collective-permute-start(f32[29,8,128]{2,1,0:T(8,128)S(1)} %get-tuple-element.20), channel_id=1, source_target_pairs={{0,64},{64,128},{128,192},{192,256},{256,320},{320,384},{384,448},... | collective-permute-start | bytes 356360 | tf_op jit(solution)/shard_map/ppermute | solution.py:393
  7.5 1.3 %collective-permute-start.1 = (f32[29,8,128]{2,1,0:T(8,128)S(1)}, f32[29,8,128]{2,1,0:T(8,128)S(1)}, u32[]{:S(2)}, u32[]{:S(2)}) collective-permute-start(f32[29,8,128]{2,1,0:T(8,128)S(1)} %get-tuple-element.21), channel_id=1, source_target_pairs={{64,0},{128,64},{192,128},{256,192},{320,256},{384,320},{448,384},... | collective-permute-start | bytes 356360 | tf_op jit(solution)/shard_map/ppermute | solution.py:394
  8.8 0.5 collective-permute-done.low_ref.x1_ref
  9.3 4.4 %collective-permute-done.1.high_ref.x2_ref = f32[29,8,128]{2,1,0:T(8,128)S(1)} collective-permute-done((f32[29,8,128]{2,1,0:T(8,128)S(1)}, f32[29,8,128]{2,1,0:T(8,128)S(1)}, u32[]{:S(2)}, u32[]{:S(2)}) %collective-permute-start.1) | collective-permute-done | bytes 118816 | tf_op jit(solution)/shard_map/ppermute | solution.py:394
  13.8 3.8 %collective-permute-start.2 = (f32[14,8,128]{2,1,0:T(8,128)S(1)}, f32[14,8,128]{2,1,0:T(8,128)S(1)}, u32[]{:S(2)}, u32[]{:S(2)}) collective-permute-start(f32[14,8,128]{2,1,0:T(8,128)S(1)} %get-tuple-element.24), channel_id=1, source_target_pairs={{0,8},{8,16},{16,24},{24,32},{32,40},{40,48},{48,56},{1,9},{9,17},... | collective-permute-start | bytes 172040 | tf_op jit(solution)/shard_map/ppermute | solution.py:393
  17.5 1.3 %collective-permute-start.3 = (f32[14,8,128]{2,1,0:T(8,128)S(1)}, f32[14,8,128]{2,1,0:T(8,128)S(1)}, u32[]{:S(2)}, u32[]{:S(2)}) collective-permute-start(f32[14,8,128]{2,1,0:T(8,128)S(1)} %get-tuple-element.25), channel_id=1, source_target_pairs={{8,0},{16,8},{24,16},{32,24},{40,32},{48,40},{56,48},{9,1},{17,9},... | collective-permute-start | bytes 172040 | tf_op jit(solution)/shard_map/ppermute | solution.py:394
  18.8 14.7 %all_to_all.33 = f32[8,1,128]{2,1,0:T(1,128)S(1)} all-to-all(f32[8,1,128]{2,1,0:T(1,128)S(1)} %bitcast.16), channel_id=1, replica_groups=mesh['gx'=8,'gy'=8,'gz'=8] {'gx'}, dimensions={0} | all-to-all | bytes 8192 | tf_op jit(solution)/shard_map/all_to_all | solution.py:399
  33.5 0.0 collective-permute-done.2.low_ref.y1_ref
  33.5 0.0 collective-permute-done.3.high_ref.y2_ref
  33.5 4.9 %collective-permute-start.4 = (f32[11,8,128]{2,1,0:T(8,128)S(1)}, f32[11,8,128]{2,1,0:T(8,128)S(1)}, u32[]{:S(2)}, u32[]{:S(2)}) collective-permute-start(f32[11,8,128]{2,1,0:T(8,128)S(1)} %get-tuple-element.28), channel_id=1, source_target_pairs={{0,1},{1,2},{2,3},{3,4},{4,5},{5,6},{6,7},{7,0},{8,9},{9,10},{10,1... | collective-permute-start | bytes 135176 | tf_op jit(solution)/shard_map/ppermute | solution.py:393
  38.5 0.0 collective-permute-start.5
  38.5 15.4 %all_to_all.34 = f32[8,1,128]{2,1,0:T(1,128)S(1)} all-to-all(f32[8,1,128]{2,1,0:T(1,128)S(1)} %bitcast.12), channel_id=1, replica_groups=mesh['gx'=8,'gy'=8,'gz'=8] {'gy'}, dimensions={0} | all-to-all | bytes 8192 | tf_op jit(solution)/shard_map/all_to_all | solution.py:399
  53.9 0.6 shard_map.64.folded_ref
  54.5 6.5 %all-to-all-start.2 = ((f32[8,1,128]{2,1,0:T(1,128)}), f32[8,1,128]{2,1,0:T(1,128)S(1)}, u32[]{:S(2)}, u32[]{:S(2)}) async-start(f32[8,1,128]{2,1,0:T(1,128)} %bitcast.7), calls=%async_computation.2 | async-start | bytes 8192 | tf_op jit(solution)/shard_map/all_to_all | solution.py:399
  61.0 0.0 collective-permute-done.5.z2_ref
  61.0 1.9 %shard_map.65.rate_ref = f32[5,4,16,256]{3,2,1,0:T(8,128)S(1)} custom-call(f32[5,4,16,256]{3,2,1,0:T(8,128)S(1)} %copy-done.1, f32[29,8,128]{2,1,0:T(8,128)S(1)} %collective-permute-done.low_ref.x1_ref, f32[29,8,128]{2,1,0:T(8,128)S(1)} %collective-permute-done.1.high_ref.x2_ref, f32[14,8,128]{2,1,0:T(8,128)S(1)} %collective-permute-done.2.low_ref.y1_ref, ...), custom_call_target="tpu_custom_call" | custom-call | tf_op jit(solution)/shard_map/pallas_call | solution.py:438
  62.9 2.1 %shard_map.66 = (f32[4,4,16,256]{3,2,1,0:T(8,128)S(1)}, f32[14,8,128]{2,1,0:T(8,128)S(1)}, f32[14,8,128]{2,1,0:T(8,128)S(1)}) custom-call(f32[5,4,16,256]{3,2,1,0:T(8,128)S(1)} %copy-done.1, f32[11,8,128]{2,1,0:T(8,128)S(1)} %collective-permute-done.4.z1_ref, f32[11,8,128]{2,1,0:T(8,128)S(1)} %collective-permute-done.5.z2_ref, ...), custom_call_target="tpu_custom_call" | custom-call | tf_op jit(solution)/shard_map/pallas_call | solution.py:441
  65.0 0.5 all-to-all-done.2
  65.5 0.9 %shard_map.67 = (f32[5,4,16,256]{3,2,1,0:T(8,128)}, f32[3,3,3,3,64]{4,3,2,1,0:T(4,128)}) custom-call(f32[5,4,16,256]{3,2,1,0:T(8,128)S(1)} %copy-done.1, f32[5,4,16,256]{3,2,1,0:T(8,128)S(1)} %shard_map.65.rate_ref, f32[4,4,16,256]{3,2,1,0:T(8,128)S(1)} %get-tuple-element.31.dep_ref, f32[8,128]{1,0:T(8,128)S(1)} %bitcast.13, ...), custom_call_target="tpu_custom_call" | custom-call | tf_op jit(solution)/shard_map/pallas_call | solution.py:453
  (11 shorter events, 0.0 us)
Async XLA Ops:
  0.6 1.0 %copy-start = (f32[5,4,16,256]{3,2,1,0:T(8,128)S(1)}, f32[5,4,16,256]{3,2,1,0:T(8,128)}, u32[]{:S(2)}) copy-start(f32[5,4,16,256]{3,2,1,0:T(8,128)} %u_ref.7) | copy-start | bytes 983044
  1.6 0.9 %copy-start.2 = (f32[3,3,3,8,64]{4,3,2,1,0:T(8,128)S(1)}, f32[3,3,3,8,64]{4,3,2,1,0:T(8,128)}, u32[]{:S(2)}) copy-start(f32[3,3,3,8,64]{4,3,2,1,0:T(8,128)} %data_ref.1) | copy-start | bytes 165892
  1.6 0.9 %copy-start.3 = (s32[3,3,3,64]{3,2,1,0:T(4,128)S(1)}, s32[3,3,3,64]{3,2,1,0:T(4,128)}, u32[]{:S(2)}) copy-start(s32[3,3,3,64]{3,2,1,0:T(4,128)} %host_ref.1) | copy-start | bytes 20740
  1.6 0.9 %copy-start.4 = (s32[3,3,3]{2,1,0:T(4,128)S(1)}, s32[3,3,3]{2,1,0:T(4,128)}, u32[]{:S(2)}) copy-start(s32[3,3,3]{2,1,0:T(4,128)} %count_ref.1) | copy-start | bytes 328
  2.7 6.6 %collective-permute-start = (f32[29,8,128]{2,1,0:T(8,128)S(1)}, f32[29,8,128]{2,1,0:T(8,128)S(1)}, u32[]{:S(2)}, u32[]{:S(2)}) collective-permute-start(f32[29,8,128]{2,1,0:T(8,128)S(1)} %get-tuple-element.20), channel_id=1, source_target_pairs={{0,64},{64,128},{128,192},{192,256},{256,320},{320,384},{384,448},... | collective-permute-start | bytes 356360 | tf_op jit(solution)/shard_map/ppermute | solution.py:393
  7.5 6.2 %collective-permute-start.1 = (f32[29,8,128]{2,1,0:T(8,128)S(1)}, f32[29,8,128]{2,1,0:T(8,128)S(1)}, u32[]{:S(2)}, u32[]{:S(2)}) collective-permute-start(f32[29,8,128]{2,1,0:T(8,128)S(1)} %get-tuple-element.21), channel_id=1, source_target_pairs={{64,0},{128,64},{192,128},{256,192},{320,256},{384,320},{448,384},... | collective-permute-start | bytes 356360 | tf_op jit(solution)/shard_map/ppermute | solution.py:394
  13.7 47.2 %copy-start.1 = (f32[5,4,16,256]{3,2,1,0:T(8,128)S(1)}, f32[5,4,16,256]{3,2,1,0:T(8,128)}, u32[]{:S(2)}) copy-start(f32[5,4,16,256]{3,2,1,0:T(8,128)} %u_ref.7) | copy-start | bytes 983044
  13.8 19.7 %collective-permute-start.2 = (f32[14,8,128]{2,1,0:T(8,128)S(1)}, f32[14,8,128]{2,1,0:T(8,128)S(1)}, u32[]{:S(2)}, u32[]{:S(2)}) collective-permute-start(f32[14,8,128]{2,1,0:T(8,128)S(1)} %get-tuple-element.24), channel_id=1, source_target_pairs={{0,8},{8,16},{16,24},{24,32},{32,40},{40,48},{48,56},{1,9},{9,17},... | collective-permute-start | bytes 172040 | tf_op jit(solution)/shard_map/ppermute | solution.py:393
  17.5 16.0 %collective-permute-start.3 = (f32[14,8,128]{2,1,0:T(8,128)S(1)}, f32[14,8,128]{2,1,0:T(8,128)S(1)}, u32[]{:S(2)}, u32[]{:S(2)}) collective-permute-start(f32[14,8,128]{2,1,0:T(8,128)S(1)} %get-tuple-element.25), channel_id=1, source_target_pairs={{8,0},{16,8},{24,16},{32,24},{40,32},{48,40},{56,48},{9,1},{17,9},... | collective-permute-start | bytes 172040 | tf_op jit(solution)/shard_map/ppermute | solution.py:394
  33.5 27.4 %collective-permute-start.4 = (f32[11,8,128]{2,1,0:T(8,128)S(1)}, f32[11,8,128]{2,1,0:T(8,128)S(1)}, u32[]{:S(2)}, u32[]{:S(2)}) collective-permute-start(f32[11,8,128]{2,1,0:T(8,128)S(1)} %get-tuple-element.28), channel_id=1, source_target_pairs={{0,1},{1,2},{2,3},{3,4},{4,5},{5,6},{6,7},{7,0},{8,9},{9,10},{10,1... | collective-permute-start | bytes 135176 | tf_op jit(solution)/shard_map/ppermute | solution.py:393
  38.5 22.5 %collective-permute-start.5 = (f32[11,8,128]{2,1,0:T(8,128)S(1)}, f32[11,8,128]{2,1,0:T(8,128)S(1)}, u32[]{:S(2)}, u32[]{:S(2)}) collective-permute-start(f32[11,8,128]{2,1,0:T(8,128)S(1)} %get-tuple-element.29), channel_id=1, source_target_pairs={{1,0},{2,1},{3,2},{4,3},{5,4},{6,5},{7,6},{0,7},{9,8},{10,9},{11,1... | collective-permute-start | bytes 135176 | tf_op jit(solution)/shard_map/ppermute | solution.py:394
  54.5 11.0 %all-to-all-start.2 = ((f32[8,1,128]{2,1,0:T(1,128)}), f32[8,1,128]{2,1,0:T(1,128)S(1)}, u32[]{:S(2)}, u32[]{:S(2)}) async-start(f32[8,1,128]{2,1,0:T(1,128)} %bitcast.7), calls=%async_computation.2 | async-start | bytes 8192 | tf_op jit(solution)/shard_map/all_to_all | solution.py:399

commit v7 on v5

--- a/solution.py
+++ b/solution.py
@@ -9,7 +9,6 @@
 F32 = jnp.float32
 BF16 = jnp.bfloat16
 VMEM_BYTES = 24 * 1024 * 1024
-TURN_BYTES = 16 * 1024 * 1024
 
 NODES = np.array([-1.0, -1.0 / np.sqrt(5.0), 1.0 / np.sqrt(5.0), 1.0])
 WEIGHTS = np.array([1.0 / 6.0, 5.0 / 6.0, 5.0 / 6.0, 1.0 / 6.0])
@@ -115,7 +114,8 @@
         down_ref[FACE + t] = face_down_ref[t]
 
 
-def turn_y_kernel(low_ref, high_ref, own_ref, face_ref, up_ref, down_ref, keep_ref):
+def turn_y_kernel(low_ref, high_ref, own_ref, face_ref, tops_ref, up_ref, down_ref, keep_ref, top_ref):
+    top_ref[...] = jnp.broadcast_to(jnp.max(tops_ref[...], axis=0, keepdims=True), top_ref.shape)
     for a, source in enumerate((low_ref, own_ref, high_ref)):
         for c in range(3):
             up_ref[3 * a + c] = source[6 + c]
@@ -135,10 +135,6 @@
     for yh in range(2):
         up_ref[FACE + yh] = face_ref[10 + yh]
         down_ref[FACE + yh] = face_ref[12 + yh]
-
-
-def fold_kernel(tops_ref, turned_ref, top_ref):
-    top_ref[...] = jnp.broadcast_to(jnp.max(tops_ref[...], axis=0, keepdims=True), top_ref.shape)
 
 
 def wall(axis, last, own, received, sign_of):
@@ -399,14 +395,12 @@
     return lax.all_to_all(top, axis, 0, 0, tiled=True)
 
 
-def call(kernel, outs, scratch=(), nbytes=None):
-    cost = None if nbytes is None else pl.CostEstimate(flops=0, bytes_accessed=nbytes, transcendentals=0)
+def call(kernel, outs, scratch=()):
     return pl.pallas_call(
         kernel,
         out_shape=outs,
         scratch_shapes=list(scratch),
         compiler_params=pltpu.CompilerParams(vmem_limit_bytes=VMEM_BYTES),
-        cost_estimate=cost,
     )
 
 
@@ -415,23 +409,22 @@
 
 
 def local(fluid_state, parcel_data, host_element, slot_counts):
-    rows = [jax.ShapeDtypeStruct((lax.axis_size(axis), 128), F32) for axis in ("gx", "gy", "gz")]
-    face_up, face_down, faces, top = call(face_kernel, (tiles_of(20), tiles_of(20), tiles_of(14), rows[0]))(fluid_state)
+    planes = lax.axis_size("gx") * lax.axis_size("gy")
+    row = jax.ShapeDtypeStruct((planes, 128), F32)
+    face_up, face_down, faces, top = call(face_kernel, (tiles_of(20), tiles_of(20), tiles_of(14), row))(fluid_state)
     x_up, x_down, keep_x = call(pack_kernel, (tiles_of(29), tiles_of(29), tiles_of(9)))(
         parcel_data, host_element, slot_counts, face_up, face_down
     )
     x1, x2 = exchanged(x_up, x_down, "gx", False)
-    tops = all_tops(top, "gx")
-    y_up, y_down, keep_y = call(turn_y_kernel, (tiles_of(14), tiles_of(14), tiles_of(9)), nbytes=TURN_BYTES)(
-        x1, x2, keep_x, faces
+    tops = all_tops(top, ("gx", "gy"))
+    row = jax.ShapeDtypeStruct((lax.axis_size("gz"), 128), F32)
+    y_up, y_down, keep_y, top = call(turn_y_kernel, (tiles_of(14), tiles_of(14), tiles_of(9), row))(
+        x1, x2, keep_x, faces, tops
     )
     y1, y2 = exchanged(y_up, y_down, "gy", False)
-    tops = all_tops(call(fold_kernel, rows[1])(tops, keep_y), "gy")
-    z_up, z_down, keep_z = call(turn_z_kernel, (tiles_of(11), tiles_of(11), tiles_of(9)), nbytes=TURN_BYTES)(
-        y1, y2, keep_y, faces
-    )
+    z_up, z_down, keep_z = call(turn_z_kernel, (tiles_of(11), tiles_of(11), tiles_of(9)))(y1, y2, keep_y, faces)
     z1, z2 = exchanged(z_up, z_down, "gz", True)
-    top = all_tops(call(fold_kernel, rows[2])(tops, keep_z), "gz")
+    top = all_tops(top, "gz")
     field = jax.ShapeDtypeStruct((5, 4, 16, 256), F32)
     rate = call(
         rate_kernel, field, [pltpu.VMEM((5, 4, 16, 256), F32), pltpu.VMEM((2, 16, 256), F32)],

time: 69.4 us -> 60.8 us (0.88)
  waiting for transfers between devices: 9.77 us -> 4.87 us
  starting transfers between devices: 23.2 us -> 19.9 us
    ppermute x3, waiting for transfers between devices: 8.02 us -> 3.62 us  [exchanged(): lax.ppermute(down, axis, [(j, i) for i, j in pairs])]
    all_to_all x1, starting transfers between devices: 7.93 us -> 5.07 us  [all_tops(): return lax.all_to_all(top, axis, 0, 0, tiled=True)]
    all_to_all x2 -> x1, blocking collectives: 28.6 us -> 28.2 us  [all_tops(): return lax.all_to_all(top, axis, 0, 0, tiled=True)]
  transfers between devices with their start and end apart: 7 -> 7, of which waited for: 4 -> 2; matrix products, arithmetic and copies ran while one was open for 0% -> 0% of each run, Pallas kernels for 6% -> 5%
where the time goes in v7:
time: 60.8 us; the launch traced here: 60.5 us
  blocking collectives  28.2 us (46%)
  starting transfers between devices  19.9 us (33%)
  Pallas kernels  5.09 us (8%)
  waiting for transfers between devices  4.87 us (8%)
  local copies, waits for them, and re-layouts  1.68 us (3%)
  between operations  0.73 us (1%)
    all_to_all x1, blocking collectives, all_tops(): return lax.all_to_all(top, axis, 0, 0, tiled=True)  28.2 us
    ppermute x3, starting transfers between devices, exchanged(): lax.ppermute(up, axis, pairs)  12.3 us
    all_to_all x1, starting transfers between devices, all_tops(): return lax.all_to_all(top, axis, 0, 0, tiled=True)  5.07 us
    ppermute x3, waiting for transfers between devices, exchanged(): lax.ppermute(down, axis, [(j, i) for i, j in pairs])  3.62 us
    ppermute x3, starting transfers between devices, exchanged(): lax.ppermute(down, axis, [(j, i) for i, j in pairs])  2.59 us
    pallas_call x1, Pallas kernels, local(): call(parcel_kernel, (jax.ShapeDtypeStruct((4, 4, 16, 256), F32), tiles_of...  2.09 us
    unnamed x10, local copies, waits for them, and re-layouts  1.68 us
    all_to_all x1, waiting for transfers between devices, all_tops(): return lax.all_to_all(top, axis, 0, 0, tiled=True)  1.24 us
  transfers between devices with their start and end apart: 7, of which 2 were waited for; matrix products, arithmetic and copies ran while one was open for 0% of the time, Pallas kernels for 5%

profile of v7, /device:TPU:1, one launch (start us, length us, event | category | flops | bytes accessed | tf_op | source)
XLA Modules:
  0.0 60.5 jit_solution(2152989458599933603)
XLA Ops:
  0.6 0.0 copy-start
  0.6 1.0 %copy-done = f32[5,4,16,256]{3,2,1,0:T(8,128)S(1)} copy-done((f32[5,4,16,256]{3,2,1,0:T(8,128)S(1)}, f32[5,4,16,256]{3,2,1,0:T(8,128)}, u32[]{:S(2)}) %copy-start) | copy-done | bytes 327704
  1.6 0.2 shard_map.59
  1.8 0.7 %copy-done.2 = f32[3,3,3,8,64]{4,3,2,1,0:T(8,128)S(1)} copy-done((f32[3,3,3,8,64]{4,3,2,1,0:T(8,128)S(1)}, f32[3,3,3,8,64]{4,3,2,1,0:T(8,128)}, u32[]{:S(2)}) %copy-start.2) | copy-done | bytes 55320
  2.5 0.2 shard_map.60
  2.7 4.8 %collective-permute-start = (f32[29,8,128]{2,1,0:T(8,128)S(1)}, f32[29,8,128]{2,1,0:T(8,128)S(1)}, u32[]{:S(2)}, u32[]{:S(2)}) collective-permute-start(f32[29,8,128]{2,1,0:T(8,128)S(1)} %get-tuple-element.21), channel_id=1, source_target_pairs={{0,64},{64,128},{128,192},{192,256},{256,320},{320,384},{384,448},... | collective-permute-start | bytes 356360 | tf_op jit(solution)/shard_map/ppermute | solution.py:389
  7.5 1.3 %collective-permute-start.1 = (f32[29,8,128]{2,1,0:T(8,128)S(1)}, f32[29,8,128]{2,1,0:T(8,128)S(1)}, u32[]{:S(2)}, u32[]{:S(2)}) collective-permute-start(f32[29,8,128]{2,1,0:T(8,128)S(1)} %get-tuple-element.22), channel_id=1, source_target_pairs={{64,0},{128,64},{192,128},{256,192},{320,256},{384,320},{448,384},... | collective-permute-start | bytes 356360 | tf_op jit(solution)/shard_map/ppermute | solution.py:390
  8.8 0.0 copy-start.1
  8.8 28.2 %all_to_all.22 = f32[64,1,128]{2,1,0:T(1,128)S(1)} all-to-all(f32[64,1,128]{2,1,0:T(1,128)S(1)} %bitcast.9), channel_id=1, replica_groups=mesh['gx'=8,'gy'=8,'gz'=8] {'gx','gy'}, dimensions={0} | all-to-all | bytes 65536 | tf_op jit(solution)/shard_map/all_to_all | solution.py:395
  37.1 0.0 collective-permute-done.low_ref.x1_ref
  37.1 0.0 collective-permute-done.1.high_ref.x2_ref
  37.1 0.6 %shard_map.61 = (f32[14,8,128]{2,1,0:T(8,128)S(1)}, f32[14,8,128]{2,1,0:T(8,128)S(1)}, f32[9,8,128]{2,1,0:T(8,128)S(1)}, f32[8,128]{1,0:T(8,128)}) custom-call(f32[29,8,128]{2,1,0:T(8,128)S(1)} %collective-permute-done.low_ref.x1_ref, f32[29,8,128]{2,1,0:T(8,128)S(1)} %collective-permute-done.1.high_ref.x2_ref, f32[9,8,128]{2,1,0:T(8,128)S(1)} %get-tuple-element.23.own_ref, ...), custom_call_target="tpu_custom_call" | custom-call | tf_op jit(solution)/shard_map/pallas_call | solution.py:421
  37.7 2.2 %collective-permute-start.2 = (f32[14,8,128]{2,1,0:T(8,128)S(1)}, f32[14,8,128]{2,1,0:T(8,128)S(1)}, u32[]{:S(2)}, u32[]{:S(2)}) collective-permute-start(f32[14,8,128]{2,1,0:T(8,128)S(1)} %get-tuple-element.26), channel_id=1, source_target_pairs={{0,8},{8,16},{16,24},{24,32},{32,40},{40,48},{48,56},{1,9},{9,17},... | collective-permute-start | bytes 172040 | tf_op jit(solution)/shard_map/ppermute | solution.py:389
  39.9 1.3 %collective-permute-start.3 = (f32[14,8,128]{2,1,0:T(8,128)S(1)}, f32[14,8,128]{2,1,0:T(8,128)S(1)}, u32[]{:S(2)}, u32[]{:S(2)}) collective-permute-start(f32[14,8,128]{2,1,0:T(8,128)S(1)} %get-tuple-element.27), channel_id=1, source_target_pairs={{8,0},{16,8},{24,16},{32,24},{40,32},{48,40},{56,48},{9,1},{17,9},... | collective-permute-start | bytes 172040 | tf_op jit(solution)/shard_map/ppermute | solution.py:390
  41.2 0.0 collective-permute-done.2.low_ref.y1_ref
  41.2 3.6 %collective-permute-done.3.high_ref.y2_ref = f32[14,8,128]{2,1,0:T(8,128)S(1)} collective-permute-done((f32[14,8,128]{2,1,0:T(8,128)S(1)}, f32[14,8,128]{2,1,0:T(8,128)S(1)}, u32[]{:S(2)}, u32[]{:S(2)}) %collective-permute-start.3) | collective-permute-done | bytes 57376 | tf_op jit(solution)/shard_map/ppermute | solution.py:390
  44.9 5.2 %collective-permute-start.4 = (f32[11,8,128]{2,1,0:T(8,128)S(1)}, f32[11,8,128]{2,1,0:T(8,128)S(1)}, u32[]{:S(2)}, u32[]{:S(2)}) collective-permute-start(f32[11,8,128]{2,1,0:T(8,128)S(1)} %get-tuple-element.29), channel_id=1, source_target_pairs={{0,1},{1,2},{2,3},{3,4},{4,5},{5,6},{6,7},{7,0},{8,9},{9,10},{10,1... | collective-permute-start | bytes 135176 | tf_op jit(solution)/shard_map/ppermute | solution.py:389
  50.1 5.1 %all-to-all-start.1 = ((f32[8,1,128]{2,1,0:T(1,128)}), f32[8,1,128]{2,1,0:T(1,128)S(1)}, u32[]{:S(2)}, u32[]{:S(2)}) async-start(f32[8,1,128]{2,1,0:T(1,128)} %bitcast.4), calls=%async_computation.1 | async-start | bytes 8192 | tf_op jit(solution)/shard_map/all_to_all | solution.py:395
  55.1 0.0 collective-permute-done.4.z1_ref
  55.1 0.0 collective-permute-done.5.z2_ref
  55.2 1.1 %shard_map.63.rate_ref = f32[5,4,16,256]{3,2,1,0:T(8,128)S(1)} custom-call(f32[5,4,16,256]{3,2,1,0:T(8,128)S(1)} %copy-done.1, f32[29,8,128]{2,1,0:T(8,128)S(1)} %collective-permute-done.low_ref.x1_ref, f32[29,8,128]{2,1,0:T(8,128)S(1)} %collective-permute-done.1.high_ref.x2_ref, f32[14,8,128]{2,1,0:T(8,128)S(1)} %collective-permute-done.2.low_ref.y1_ref, ...), custom_call_target="tpu_custom_call" | custom-call | tf_op jit(solution)/shard_map/pallas_call | solution.py:429
  56.3 2.1 %shard_map.64 = (f32[4,4,16,256]{3,2,1,0:T(8,128)S(1)}, f32[14,8,128]{2,1,0:T(8,128)S(1)}, f32[14,8,128]{2,1,0:T(8,128)S(1)}) custom-call(f32[5,4,16,256]{3,2,1,0:T(8,128)S(1)} %copy-done.1, f32[11,8,128]{2,1,0:T(8,128)S(1)} %collective-permute-done.4.z1_ref, f32[11,8,128]{2,1,0:T(8,128)S(1)} %collective-permute-done.5.z2_ref, ...), custom_call_target="tpu_custom_call" | custom-call | tf_op jit(solution)/shard_map/pallas_call | solution.py:432
  58.4 1.2 %all-to-all-done.1 = f32[8,1,128]{2,1,0:T(1,128)S(1)} async-done(((f32[8,1,128]{2,1,0:T(1,128)}), f32[8,1,128]{2,1,0:T(1,128)S(1)}, u32[]{:S(2)}, u32[]{:S(2)}) %all-to-all-start.1) | async-done | bytes 4128 | tf_op jit(solution)/shard_map/all_to_all | solution.py:395
  59.7 0.9 %shard_map.65 = (f32[5,4,16,256]{3,2,1,0:T(8,128)}, f32[3,3,3,3,64]{4,3,2,1,0:T(4,128)}) custom-call(f32[5,4,16,256]{3,2,1,0:T(8,128)S(1)} %copy-done.1, f32[5,4,16,256]{3,2,1,0:T(8,128)S(1)} %shard_map.63.rate_ref, f32[4,4,16,256]{3,2,1,0:T(8,128)S(1)} %get-tuple-element.32.dep_ref, f32[8,128]{1,0:T(8,128)S(1)} %bitcast.10, ...), custom_call_target="tpu_custom_call" | custom-call | tf_op jit(solution)/shard_map/pallas_call | solution.py:444
  (8 shorter events, 0.0 us)
Async XLA Ops:
  0.6 1.0 %copy-start = (f32[5,4,16,256]{3,2,1,0:T(8,128)S(1)}, f32[5,4,16,256]{3,2,1,0:T(8,128)}, u32[]{:S(2)}) copy-start(f32[5,4,16,256]{3,2,1,0:T(8,128)} %u_ref.7) | copy-start | bytes 983044
  1.6 0.9 %copy-start.2 = (f32[3,3,3,8,64]{4,3,2,1,0:T(8,128)S(1)}, f32[3,3,3,8,64]{4,3,2,1,0:T(8,128)}, u32[]{:S(2)}) copy-start(f32[3,3,3,8,64]{4,3,2,1,0:T(8,128)} %data_ref.1) | copy-start | bytes 165892
  1.6 0.9 %copy-start.3 = (s32[3,3,3,64]{3,2,1,0:T(4,128)S(1)}, s32[3,3,3,64]{3,2,1,0:T(4,128)}, u32[]{:S(2)}) copy-start(s32[3,3,3,64]{3,2,1,0:T(4,128)} %host_ref.1) | copy-start | bytes 20740
  1.6 0.9 %copy-start.4 = (s32[3,3,3]{2,1,0:T(4,128)S(1)}, s32[3,3,3]{2,1,0:T(4,128)}, u32[]{:S(2)}) copy-start(s32[3,3,3]{2,1,0:T(4,128)} %count_ref.1) | copy-start | bytes 328
  2.7 34.4 %collective-permute-start = (f32[29,8,128]{2,1,0:T(8,128)S(1)}, f32[29,8,128]{2,1,0:T(8,128)S(1)}, u32[]{:S(2)}, u32[]{:S(2)}) collective-permute-start(f32[29,8,128]{2,1,0:T(8,128)S(1)} %get-tuple-element.21), channel_id=1, source_target_pairs={{0,64},{64,128},{128,192},{192,256},{256,320},{320,384},{384,448},... | collective-permute-start | bytes 356360 | tf_op jit(solution)/shard_map/ppermute | solution.py:389
  7.5 29.6 %collective-permute-start.1 = (f32[29,8,128]{2,1,0:T(8,128)S(1)}, f32[29,8,128]{2,1,0:T(8,128)S(1)}, u32[]{:S(2)}, u32[]{:S(2)}) collective-permute-start(f32[29,8,128]{2,1,0:T(8,128)S(1)} %get-tuple-element.22), channel_id=1, source_target_pairs={{64,0},{128,64},{192,128},{256,192},{320,256},{384,320},{448,384},... | collective-permute-start | bytes 356360 | tf_op jit(solution)/shard_map/ppermute | solution.py:390
  8.8 46.3 %copy-start.1 = (f32[5,4,16,256]{3,2,1,0:T(8,128)S(1)}, f32[5,4,16,256]{3,2,1,0:T(8,128)}, u32[]{:S(2)}) copy-start(f32[5,4,16,256]{3,2,1,0:T(8,128)} %u_ref.7) | copy-start | bytes 983044
  37.7 3.5 %collective-permute-start.2 = (f32[14,8,128]{2,1,0:T(8,128)S(1)}, f32[14,8,128]{2,1,0:T(8,128)S(1)}, u32[]{:S(2)}, u32[]{:S(2)}) collective-permute-start(f32[14,8,128]{2,1,0:T(8,128)S(1)} %get-tuple-element.26), channel_id=1, source_target_pairs={{0,8},{8,16},{16,24},{24,32},{32,40},{40,48},{48,56},{1,9},{9,17},... | collective-permute-start | bytes 172040 | tf_op jit(solution)/shard_map/ppermute | solution.py:389
  39.9 4.9 %collective-permute-start.3 = (f32[14,8,128]{2,1,0:T(8,128)S(1)}, f32[14,8,128]{2,1,0:T(8,128)S(1)}, u32[]{:S(2)}, u32[]{:S(2)}) collective-permute-start(f32[14,8,128]{2,1,0:T(8,128)S(1)} %get-tuple-element.27), channel_id=1, source_target_pairs={{8,0},{16,8},{24,16},{32,24},{40,32},{48,40},{56,48},{9,1},{17,9},... | collective-permute-start | bytes 172040 | tf_op jit(solution)/shard_map/ppermute | solution.py:390
  44.9 10.3 %collective-permute-start.4 = (f32[11,8,128]{2,1,0:T(8,128)S(1)}, f32[11,8,128]{2,1,0:T(8,128)S(1)}, u32[]{:S(2)}, u32[]{:S(2)}) collective-permute-start(f32[11,8,128]{2,1,0:T(8,128)S(1)} %get-tuple-element.29), channel_id=1, source_target_pairs={{0,1},{1,2},{2,3},{3,4},{4,5},{5,6},{6,7},{7,0},{8,9},{9,10},{10,1... | collective-permute-start | bytes 135176 | tf_op jit(solution)/shard_map/ppermute | solution.py:389
  50.1 5.1 %collective-permute-start.5 = (f32[11,8,128]{2,1,0:T(8,128)S(1)}, f32[11,8,128]{2,1,0:T(8,128)S(1)}, u32[]{:S(2)}, u32[]{:S(2)}) collective-permute-start(f32[11,8,128]{2,1,0:T(8,128)S(1)} %get-tuple-element.30), channel_id=1, source_target_pairs={{1,0},{2,1},{3,2},{4,3},{5,4},{6,5},{7,6},{0,7},{9,8},{10,9},{11,1... | collective-permute-start | bytes 135176 | tf_op jit(solution)/shard_map/ppermute | solution.py:390
  50.1 9.6 %all-to-all-start.1 = ((f32[8,1,128]{2,1,0:T(1,128)}), f32[8,1,128]{2,1,0:T(1,128)S(1)}, u32[]{:S(2)}, u32[]{:S(2)}) async-start(f32[8,1,128]{2,1,0:T(1,128)} %bitcast.4), calls=%async_computation.1 | async-start | bytes 8192 | tf_op jit(solution)/shard_map/all_to_all | solution.py:395

commit v8 on v7

--- a/solution.py
+++ b/solution.py
@@ -126,7 +126,8 @@
         down_ref[FACE + v] = face_ref[5 + v]
 
 
-def turn_z_kernel(low_ref, high_ref, own_ref, face_ref, up_ref, down_ref, keep_ref):
+def turn_z_kernel(low_ref, high_ref, own_ref, face_ref, tops_ref, up_ref, down_ref, keep_ref, top_ref):
+    top_ref[...] = jnp.broadcast_to(jnp.max(tops_ref[...], axis=0, keepdims=True), top_ref.shape)
     for b, source in enumerate((low_ref, own_ref, high_ref)):
         for a in range(3):
             up_ref[3 * a + b] = source[3 * a + 2]
@@ -409,20 +410,21 @@
 
 
 def local(fluid_state, parcel_data, host_element, slot_counts):
-    planes = lax.axis_size("gx") * lax.axis_size("gy")
-    row = jax.ShapeDtypeStruct((planes, 128), F32)
-    face_up, face_down, faces, top = call(face_kernel, (tiles_of(20), tiles_of(20), tiles_of(14), row))(fluid_state)
+    rows = [jax.ShapeDtypeStruct((lax.axis_size(axis), 128), F32) for axis in ("gx", "gy", "gz")]
+    face_up, face_down, faces, top = call(face_kernel, (tiles_of(20), tiles_of(20), tiles_of(14), rows[0]))(fluid_state)
     x_up, x_down, keep_x = call(pack_kernel, (tiles_of(29), tiles_of(29), tiles_of(9)))(
         parcel_data, host_element, slot_counts, face_up, face_down
     )
     x1, x2 = exchanged(x_up, x_down, "gx", False)
-    tops = all_tops(top, ("gx", "gy"))
-    row = jax.ShapeDtypeStruct((lax.axis_size("gz"), 128), F32)
-    y_up, y_down, keep_y, top = call(turn_y_kernel, (tiles_of(14), tiles_of(14), tiles_of(9), row))(
+    tops = all_tops(top, "gx")
+    y_up, y_down, keep_y, top = call(turn_y_kernel, (tiles_of(14), tiles_of(14), tiles_of(9), rows[1]))(
         x1, x2, keep_x, faces, tops
     )
     y1, y2 = exchanged(y_up, y_down, "gy", False)
-    z_up, z_down, keep_z = call(turn_z_kernel, (tiles_of(11), tiles_of(11), tiles_of(9)))(y1, y2, keep_y, faces)
+    tops = all_tops(top, "gy")
+    z_up, z_down, keep_z, top = call(turn_z_kernel, (tiles_of(11), tiles_of(11), tiles_of(9), rows[2]))(
+        y1, y2, keep_y, faces, tops
+    )
     z1, z2 = exchanged(z_up, z_down, "gz", True)
     top = all_tops(top, "gz")
     field = jax.ShapeDtypeStruct((5, 4, 16, 256), F32)

time: 60.8 us -> 63.4 us (1.043)
  blocking collectives: 28.2 us -> 32.7 us
  waiting for transfers between devices: 4.87 us -> 1.26 us
  starting transfers between devices: 19.9 us -> 21.6 us
    all_to_all x1 -> x2, blocking collectives: 28.2 us -> 32.7 us  [all_tops(): return lax.all_to_all(top, axis, 0, 0, tiled=True)]
    ppermute x3, waiting for transfers between devices: 3.62 us -> 0.01 us  [exchanged(): lax.ppermute(down, axis, [(j, i) for i, j in pairs])]
    ppermute x3, starting transfers between devices: 12.3 us -> 13.9 us  [exchanged(): lax.ppermute(up, axis, pairs)]
  transfers between devices with their start and end apart: 7 -> 7, of which waited for: 2 -> 1; matrix products, arithmetic and copies ran while one was open for 0% -> 0% of each run, Pallas kernels for 5% -> 5%
where the time goes in v8:
time: 63.4 us; the launch traced here: 63 us
  blocking collectives  32.7 us (52%)
  starting transfers between devices  21.6 us (34%)
  Pallas kernels  5.08 us (8%)
  local copies, waits for them, and re-layouts  1.68 us (3%)
  waiting for transfers between devices  1.26 us (2%)
  between operations  0.72 us (1%)
    all_to_all x2, blocking collectives, all_tops(): return lax.all_to_all(top, axis, 0, 0, tiled=True)  32.7 us
    ppermute x3, starting transfers between devices, exchanged(): lax.ppermute(up, axis, pairs)  13.9 us
    all_to_all x1, starting transfers between devices, all_tops(): return lax.all_to_all(top, axis, 0, 0, tiled=True)  5.07 us
    ppermute x3, starting transfers between devices, exchanged(): lax.ppermute(down, axis, [(j, i) for i, j in pairs])  2.59 us
    pallas_call x1, Pallas kernels, local(): call(parcel_kernel, (jax.ShapeDtypeStruct((4, 4, 16, 256), F32), tiles_of...  2.09 us
    unnamed x10, local copies, waits for them, and re-layouts  1.68 us
  transfers between devices with their start and end apart: 7, of which 1 were waited for; matrix products, arithmetic and copies ran while one was open for 0% of the time, Pallas kernels for 5%

profile of v8, /device:TPU:1, one launch (start us, length us, event | category | flops | bytes accessed | tf_op | source)
XLA Modules:
  0.0 63.0 jit_solution(18305181164163091601)
XLA Ops:
  0.6 0.0 copy-start
  0.6 1.0 %copy-done = f32[5,4,16,256]{3,2,1,0:T(8,128)S(1)} copy-done((f32[5,4,16,256]{3,2,1,0:T(8,128)S(1)}, f32[5,4,16,256]{3,2,1,0:T(8,128)}, u32[]{:S(2)}) %copy-start) | copy-done | bytes 327704
  1.6 0.2 shard_map.59
  1.8 0.7 %copy-done.2 = f32[3,3,3,8,64]{4,3,2,1,0:T(8,128)S(1)} copy-done((f32[3,3,3,8,64]{4,3,2,1,0:T(8,128)S(1)}, f32[3,3,3,8,64]{4,3,2,1,0:T(8,128)}, u32[]{:S(2)}) %copy-start.2) | copy-done | bytes 55320
  2.5 0.2 shard_map.60
  2.7 0.0 copy-start.1
  2.7 5.0 %collective-permute-start = (f32[29,8,128]{2,1,0:T(8,128)S(1)}, f32[29,8,128]{2,1,0:T(8,128)S(1)}, u32[]{:S(2)}, u32[]{:S(2)}) collective-permute-start(f32[29,8,128]{2,1,0:T(8,128)S(1)} %get-tuple-element.22), channel_id=1, source_target_pairs={{0,64},{64,128},{128,192},{192,256},{256,320},{320,384},{384,448},... | collective-permute-start | bytes 356360 | tf_op jit(solution)/shard_map/ppermute | solution.py:390
  7.7 1.3 %collective-permute-start.1 = (f32[29,8,128]{2,1,0:T(8,128)S(1)}, f32[29,8,128]{2,1,0:T(8,128)S(1)}, u32[]{:S(2)}, u32[]{:S(2)}) collective-permute-start(f32[29,8,128]{2,1,0:T(8,128)S(1)} %get-tuple-element.23), channel_id=1, source_target_pairs={{64,0},{128,64},{192,128},{256,192},{320,256},{384,320},{448,384},... | collective-permute-start | bytes 356360 | tf_op jit(solution)/shard_map/ppermute | solution.py:391
  9.0 17.5 %all_to_all.33 = f32[8,1,128]{2,1,0:T(1,128)S(1)} all-to-all(f32[8,1,128]{2,1,0:T(1,128)S(1)} %bitcast.15), channel_id=1, replica_groups=mesh['gx'=8,'gy'=8,'gz'=8] {'gx'}, dimensions={0} | all-to-all | bytes 8192 | tf_op jit(solution)/shard_map/all_to_all | solution.py:396
  26.5 0.0 collective-permute-done.low_ref.x1_ref
  26.5 3.2 %collective-permute-start.2 = (f32[14,8,128]{2,1,0:T(8,128)S(1)}, f32[14,8,128]{2,1,0:T(8,128)S(1)}, u32[]{:S(2)}, u32[]{:S(2)}) collective-permute-start(f32[14,8,128]{2,1,0:T(8,128)S(1)} %get-tuple-element.27), channel_id=1, source_target_pairs={{0,8},{8,16},{16,24},{24,32},{32,40},{40,48},{48,56},{1,9},{9,17},... | collective-permute-start | bytes 172040 | tf_op jit(solution)/shard_map/ppermute | solution.py:390
  29.7 1.3 %collective-permute-start.3 = (f32[14,8,128]{2,1,0:T(8,128)S(1)}, f32[14,8,128]{2,1,0:T(8,128)S(1)}, u32[]{:S(2)}, u32[]{:S(2)}) collective-permute-start(f32[14,8,128]{2,1,0:T(8,128)S(1)} %get-tuple-element.28), channel_id=1, source_target_pairs={{8,0},{16,8},{24,16},{32,24},{40,32},{48,40},{56,48},{9,1},{17,9},... | collective-permute-start | bytes 172040 | tf_op jit(solution)/shard_map/ppermute | solution.py:391
  31.0 15.1 %all_to_all.34 = f32[8,1,128]{2,1,0:T(1,128)S(1)} all-to-all(f32[8,1,128]{2,1,0:T(1,128)S(1)} %bitcast.16), channel_id=1, replica_groups=mesh['gx'=8,'gy'=8,'gz'=8] {'gy'}, dimensions={0} | all-to-all | bytes 8192 | tf_op jit(solution)/shard_map/all_to_all | solution.py:396
  46.2 0.0 collective-permute-done.2.low_ref.y1_ref
  46.2 0.0 collective-permute-done.3.high_ref.y2_ref
  46.2 0.6 shard_map.62
  46.8 5.8 %collective-permute-start.4 = (f32[11,8,128]{2,1,0:T(8,128)S(1)}, f32[11,8,128]{2,1,0:T(8,128)S(1)}, u32[]{:S(2)}, u32[]{:S(2)}) collective-permute-start(f32[11,8,128]{2,1,0:T(8,128)S(1)} %get-tuple-element.31), channel_id=1, source_target_pairs={{0,1},{1,2},{2,3},{3,4},{4,5},{5,6},{6,7},{7,0},{8,9},{9,10},{10,1... | collective-permute-start | bytes 135176 | tf_op jit(solution)/shard_map/ppermute | solution.py:390
  52.5 5.1 %all-to-all-start.2 = ((f32[8,1,128]{2,1,0:T(1,128)}), f32[8,1,128]{2,1,0:T(1,128)S(1)}, u32[]{:S(2)}, u32[]{:S(2)}) async-start(f32[8,1,128]{2,1,0:T(1,128)} %bitcast.7), calls=%async_computation.2 | async-start | bytes 8192 | tf_op jit(solution)/shard_map/all_to_all | solution.py:396
  57.6 0.0 collective-permute-done.4.z1_ref
  57.6 0.0 collective-permute-done.5.z2_ref
  57.6 1.1 %shard_map.63.rate_ref = f32[5,4,16,256]{3,2,1,0:T(8,128)S(1)} custom-call(f32[5,4,16,256]{3,2,1,0:T(8,128)S(1)} %copy-done.1, f32[29,8,128]{2,1,0:T(8,128)S(1)} %collective-permute-done.low_ref.x1_ref, f32[29,8,128]{2,1,0:T(8,128)S(1)} %collective-permute-done.1.high_ref.x2_ref, f32[14,8,128]{2,1,0:T(8,128)S(1)} %collective-permute-done.2.low_ref.y1_ref, ...), custom_call_target="tpu_custom_call" | custom-call | tf_op jit(solution)/shard_map/pallas_call | solution.py:431
  58.8 2.1 %shard_map.64 = (f32[4,4,16,256]{3,2,1,0:T(8,128)S(1)}, f32[14,8,128]{2,1,0:T(8,128)S(1)}, f32[14,8,128]{2,1,0:T(8,128)S(1)}) custom-call(f32[5,4,16,256]{3,2,1,0:T(8,128)S(1)} %copy-done.1, f32[11,8,128]{2,1,0:T(8,128)S(1)} %collective-permute-done.4.z1_ref, f32[11,8,128]{2,1,0:T(8,128)S(1)} %collective-permute-done.5.z2_ref, ...), custom_call_target="tpu_custom_call" | custom-call | tf_op jit(solution)/shard_map/pallas_call | solution.py:434
  60.9 1.2 %all-to-all-done.2 = f32[8,1,128]{2,1,0:T(1,128)S(1)} async-done(((f32[8,1,128]{2,1,0:T(1,128)}), f32[8,1,128]{2,1,0:T(1,128)S(1)}, u32[]{:S(2)}, u32[]{:S(2)}) %all-to-all-start.2) | async-done | bytes 4128 | tf_op jit(solution)/shard_map/all_to_all | solution.py:396
  62.1 0.9 %shard_map.65 = (f32[5,4,16,256]{3,2,1,0:T(8,128)}, f32[3,3,3,3,64]{4,3,2,1,0:T(4,128)}) custom-call(f32[5,4,16,256]{3,2,1,0:T(8,128)S(1)} %copy-done.1, f32[5,4,16,256]{3,2,1,0:T(8,128)S(1)} %shard_map.63.rate_ref, f32[4,4,16,256]{3,2,1,0:T(8,128)S(1)} %get-tuple-element.34.dep_ref, f32[8,128]{1,0:T(8,128)S(1)} %bitcast.12, ...), custom_call_target="tpu_custom_call" | custom-call | tf_op jit(solution)/shard_map/pallas_call | solution.py:446
  (9 shorter events, 0.0 us)
Async XLA Ops:
  0.6 1.0 %copy-start = (f32[5,4,16,256]{3,2,1,0:T(8,128)S(1)}, f32[5,4,16,256]{3,2,1,0:T(8,128)}, u32[]{:S(2)}) copy-start(f32[5,4,16,256]{3,2,1,0:T(8,128)} %u_ref.7) | copy-start | bytes 983044
  1.6 0.9 %copy-start.2 = (f32[3,3,3,8,64]{4,3,2,1,0:T(8,128)S(1)}, f32[3,3,3,8,64]{4,3,2,1,0:T(8,128)}, u32[]{:S(2)}) copy-start(f32[3,3,3,8,64]{4,3,2,1,0:T(8,128)} %data_ref.1) | copy-start | bytes 165892
  1.6 0.9 %copy-start.3 = (s32[3,3,3,64]{3,2,1,0:T(4,128)S(1)}, s32[3,3,3,64]{3,2,1,0:T(4,128)}, u32[]{:S(2)}) copy-start(s32[3,3,3,64]{3,2,1,0:T(4,128)} %host_ref.1) | copy-start | bytes 20740
  1.6 0.9 %copy-start.4 = (s32[3,3,3]{2,1,0:T(4,128)S(1)}, s32[3,3,3]{2,1,0:T(4,128)}, u32[]{:S(2)}) copy-start(s32[3,3,3]{2,1,0:T(4,128)} %count_ref.1) | copy-start | bytes 328
  2.7 54.9 %copy-start.1 = (f32[5,4,16,256]{3,2,1,0:T(8,128)S(1)}, f32[5,4,16,256]{3,2,1,0:T(8,128)}, u32[]{:S(2)}) copy-start(f32[5,4,16,256]{3,2,1,0:T(8,128)} %u_ref.7) | copy-start | bytes 983044
  2.7 23.8 %collective-permute-start = (f32[29,8,128]{2,1,0:T(8,128)S(1)}, f32[29,8,128]{2,1,0:T(8,128)S(1)}, u32[]{:S(2)}, u32[]{:S(2)}) collective-permute-start(f32[29,8,128]{2,1,0:T(8,128)S(1)} %get-tuple-element.22), channel_id=1, source_target_pairs={{0,64},{64,128},{128,192},{192,256},{256,320},{320,384},{384,448},... | collective-permute-start | bytes 356360 | tf_op jit(solution)/shard_map/ppermute | solution.py:390
  7.7 18.8 %collective-permute-start.1 = (f32[29,8,128]{2,1,0:T(8,128)S(1)}, f32[29,8,128]{2,1,0:T(8,128)S(1)}, u32[]{:S(2)}, u32[]{:S(2)}) collective-permute-start(f32[29,8,128]{2,1,0:T(8,128)S(1)} %get-tuple-element.23), channel_id=1, source_target_pairs={{64,0},{128,64},{192,128},{256,192},{320,256},{384,320},{448,384},... | collective-permute-start | bytes 356360 | tf_op jit(solution)/shard_map/ppermute | solution.py:391
  26.5 19.7 %collective-permute-start.2 = (f32[14,8,128]{2,1,0:T(8,128)S(1)}, f32[14,8,128]{2,1,0:T(8,128)S(1)}, u32[]{:S(2)}, u32[]{:S(2)}) collective-permute-start(f32[14,8,128]{2,1,0:T(8,128)S(1)} %get-tuple-element.27), channel_id=1, source_target_pairs={{0,8},{8,16},{16,24},{24,32},{32,40},{40,48},{48,56},{1,9},{9,17},... | collective-permute-start | bytes 172040 | tf_op jit(solution)/shard_map/ppermute | solution.py:390
  29.7 16.5 %collective-permute-start.3 = (f32[14,8,128]{2,1,0:T(8,128)S(1)}, f32[14,8,128]{2,1,0:T(8,128)S(1)}, u32[]{:S(2)}, u32[]{:S(2)}) collective-permute-start(f32[14,8,128]{2,1,0:T(8,128)S(1)} %get-tuple-element.28), channel_id=1, source_target_pairs={{8,0},{16,8},{24,16},{32,24},{40,32},{48,40},{56,48},{9,1},{17,9},... | collective-permute-start | bytes 172040 | tf_op jit(solution)/shard_map/ppermute | solution.py:391
  46.8 10.8 %collective-permute-start.4 = (f32[11,8,128]{2,1,0:T(8,128)S(1)}, f32[11,8,128]{2,1,0:T(8,128)S(1)}, u32[]{:S(2)}, u32[]{:S(2)}) collective-permute-start(f32[11,8,128]{2,1,0:T(8,128)S(1)} %get-tuple-element.31), channel_id=1, source_target_pairs={{0,1},{1,2},{2,3},{3,4},{4,5},{5,6},{6,7},{7,0},{8,9},{9,10},{10,1... | collective-permute-start | bytes 135176 | tf_op jit(solution)/shard_map/ppermute | solution.py:390
  52.5 5.1 %collective-permute-start.5 = (f32[11,8,128]{2,1,0:T(8,128)S(1)}, f32[11,8,128]{2,1,0:T(8,128)S(1)}, u32[]{:S(2)}, u32[]{:S(2)}) collective-permute-start(f32[11,8,128]{2,1,0:T(8,128)S(1)} %get-tuple-element.32), channel_id=1, source_target_pairs={{1,0},{2,1},{3,2},{4,3},{5,4},{6,5},{7,6},{0,7},{9,8},{10,9},{11,1... | collective-permute-start | bytes 135176 | tf_op jit(solution)/shard_map/ppermute | solution.py:391
  52.5 9.6 %all-to-all-start.2 = ((f32[8,1,128]{2,1,0:T(1,128)}), f32[8,1,128]{2,1,0:T(1,128)S(1)}, u32[]{:S(2)}, u32[]{:S(2)}) async-start(f32[8,1,128]{2,1,0:T(1,128)} %bitcast.7), calls=%async_computation.2 | async-start | bytes 8192 | tf_op jit(solution)/shard_map/all_to_all | solution.py:396

commit v9 on v7

--- a/solution.py
+++ b/solution.py
@@ -391,8 +391,8 @@
     )
 
 
-def all_tops(top, axis):
-    return lax.all_to_all(top, axis, 0, 0, tiled=True)
+def all_tops(top, axes, groups):
+    return lax.all_to_all(top, axes, 0, 0, axis_index_groups=groups, tiled=True)
 
 
 def call(kernel, outs, scratch=()):
@@ -409,22 +409,24 @@
 
 
 def local(fluid_state, parcel_data, host_element, slot_counts):
-    planes = lax.axis_size("gx") * lax.axis_size("gy")
-    row = jax.ShapeDtypeStruct((planes, 128), F32)
+    nx, ny, nz = (lax.axis_size(axis) for axis in ("gx", "gy", "gz"))
+    spaced = [[x * nz + z for x in range(p, nx, 2) for z in range(nz)] for p in range(2)]
+    paired = [[x * ny + y for x in (2 * k, 2 * k + 1) for y in range(ny)] for k in range(nx // 2)]
+    row = jax.ShapeDtypeStruct((len(spaced[0]), 128), F32)
     face_up, face_down, faces, top = call(face_kernel, (tiles_of(20), tiles_of(20), tiles_of(14), row))(fluid_state)
     x_up, x_down, keep_x = call(pack_kernel, (tiles_of(29), tiles_of(29), tiles_of(9)))(
         parcel_data, host_element, slot_counts, face_up, face_down
     )
     x1, x2 = exchanged(x_up, x_down, "gx", False)
-    tops = all_tops(top, ("gx", "gy"))
-    row = jax.ShapeDtypeStruct((lax.axis_size("gz"), 128), F32)
+    tops = all_tops(top, ("gx", "gz"), spaced)
+    row = jax.ShapeDtypeStruct((len(paired[0]), 128), F32)
     y_up, y_down, keep_y, top = call(turn_y_kernel, (tiles_of(14), tiles_of(14), tiles_of(9), row))(
         x1, x2, keep_x, faces, tops
     )
     y1, y2 = exchanged(y_up, y_down, "gy", False)
     z_up, z_down, keep_z = call(turn_z_kernel, (tiles_of(11), tiles_of(11), tiles_of(9)))(y1, y2, keep_y, faces)
     z1, z2 = exchanged(z_up, z_down, "gz", True)
-    top = all_tops(top, "gz")
+    top = all_tops(top, ("gx", "gy"), paired)
     field = jax.ShapeDtypeStruct((5, 4, 16, 256), F32)
     rate = call(
         rate_kernel, field, [pltpu.VMEM((5, 4, 16, 256), F32), pltpu.VMEM((2, 16, 256), F32)],

time: 60.8 us -> 61.8 us (1.016)
  the two profiles are of different devices: /device:TPU:1 before, /device:TPU:8 now
where the time goes in v9:
time: 61.8 us; the launch traced here: 61.4 us
  blocking collectives  24.2 us (39%)
  starting transfers between devices  22.3 us (36%)
  waiting for transfers between devices  7.48 us (12%)
  Pallas kernels  5.09 us (8%)
  local copies, waits for them, and re-layouts  1.67 us (3%)
  between operations  0.74 us (1%)
    all_to_all x1, blocking collectives, all_tops(): return lax.all_to_all(top, axes, 0, 0, axis_index_groups=groups, tiled=True)  24.2 us
    ppermute x3, starting transfers between devices, exchanged(): lax.ppermute(up, axis, pairs)  7.9 us
    all_to_all x1, starting transfers between devices, all_tops(): return lax.all_to_all(top, axes, 0, 0, axis_index_groups=groups, tiled=True)  7.76 us
    ppermute x3, starting transfers between devices, exchanged(): lax.ppermute(down, axis, [(j, i) for i, j in pairs])  6.59 us
    all_to_all x1, waiting for transfers between devices, all_tops(): return lax.all_to_all(top, axes, 0, 0, axis_index_groups=groups, tiled=True)  3.76 us
    ppermute x3, waiting for transfers between devices, exchanged(): lax.ppermute(down, axis, [(j, i) for i, j in pairs])  3.5 us
    pallas_call x1, Pallas kernels, local(): call(parcel_kernel, (jax.ShapeDtypeStruct((4, 4, 16, 256), F32), tiles_of...  2.1 us
    unnamed x10, local copies, waits for them, and re-layouts  1.67 us
  transfers between devices with their start and end apart: 7, of which 3 were waited for; matrix products, arithmetic and copies ran while one was open for 0% of the time, Pallas kernels for 5%

profile of v9, /device:TPU:8, one launch (start us, length us, event | category | flops | bytes accessed | tf_op | source)
XLA Modules:
  0.0 61.4 jit_solution(1137227536612258065)
XLA Ops:
  0.6 0.0 copy-start
  0.6 1.0 %copy-done = f32[5,4,16,256]{3,2,1,0:T(8,128)S(1)} copy-done((f32[5,4,16,256]{3,2,1,0:T(8,128)S(1)}, f32[5,4,16,256]{3,2,1,0:T(8,128)}, u32[]{:S(2)}) %copy-start) | copy-done | bytes 327704
  1.6 0.2 shard_map.59
  1.8 0.7 %copy-done.2 = f32[3,3,3,8,64]{4,3,2,1,0:T(8,128)S(1)} copy-done((f32[3,3,3,8,64]{4,3,2,1,0:T(8,128)S(1)}, f32[3,3,3,8,64]{4,3,2,1,0:T(8,128)}, u32[]{:S(2)}) %copy-start.2) | copy-done | bytes 55320
  2.5 0.2 shard_map.60
  2.7 0.0 copy-start.1
  2.7 4.4 %collective-permute-start = (f32[29,8,128]{2,1,0:T(8,128)S(1)}, f32[29,8,128]{2,1,0:T(8,128)S(1)}, u32[]{:S(2)}, u32[]{:S(2)}) collective-permute-start(f32[29,8,128]{2,1,0:T(8,128)S(1)} %get-tuple-element.21), channel_id=1, source_target_pairs={{0,64},{64,128},{128,192},{192,256},{256,320},{320,384},{384,448},... | collective-permute-start | bytes 356360 | tf_op jit(solution)/shard_map/ppermute | solution.py:389
  7.1 1.3 %collective-permute-start.1 = (f32[29,8,128]{2,1,0:T(8,128)S(1)}, f32[29,8,128]{2,1,0:T(8,128)S(1)}, u32[]{:S(2)}, u32[]{:S(2)}) collective-permute-start(f32[29,8,128]{2,1,0:T(8,128)S(1)} %get-tuple-element.22), channel_id=1, source_target_pairs={{64,0},{128,64},{192,128},{256,192},{320,256},{384,320},{448,384},... | collective-permute-start | bytes 356360 | tf_op jit(solution)/shard_map/ppermute | solution.py:390
  8.4 24.2 %all_to_all.22 = f32[32,1,128]{2,1,0:T(1,128)S(1)} all-to-all(f32[32,1,128]{2,1,0:T(1,128)S(1)} %bitcast.10), channel_id=1, replica_groups={{0,1,2,3,4,5,6,7,128,129,130,131,132,133,134,135,256,257,258,259,260,26..., dimensions={0} | all-to-all | bytes 32768 | tf_op jit(solution)/shard_map/all_to_all | solution.py:395
  32.6 0.0 collective-permute-done.low_ref.x1_ref
  32.6 0.0 collective-permute-done.1.high_ref.x2_ref
  32.6 0.6 shard_map.61
  33.2 3.5 %collective-permute-start.2 = (f32[14,8,128]{2,1,0:T(8,128)S(1)}, f32[14,8,128]{2,1,0:T(8,128)S(1)}, u32[]{:S(2)}, u32[]{:S(2)}) collective-permute-start(f32[14,8,128]{2,1,0:T(8,128)S(1)} %get-tuple-element.26), channel_id=1, source_target_pairs={{0,8},{8,16},{16,24},{24,32},{32,40},{40,48},{48,56},{1,9},{9,17},... | collective-permute-start | bytes 172040 | tf_op jit(solution)/shard_map/ppermute | solution.py:389
  36.7 2.4 %collective-permute-start.3 = (f32[14,8,128]{2,1,0:T(8,128)S(1)}, f32[14,8,128]{2,1,0:T(8,128)S(1)}, u32[]{:S(2)}, u32[]{:S(2)}) collective-permute-start(f32[14,8,128]{2,1,0:T(8,128)S(1)} %get-tuple-element.27), channel_id=1, source_target_pairs={{8,0},{16,8},{24,16},{32,24},{40,32},{48,40},{56,48},{9,1},{17,9},... | collective-permute-start | bytes 172040 | tf_op jit(solution)/shard_map/ppermute | solution.py:390
  39.1 0.2 collective-permute-done.2.low_ref.y1_ref
  39.3 3.5 %collective-permute-done.3.high_ref.y2_ref = f32[14,8,128]{2,1,0:T(8,128)S(1)} collective-permute-done((f32[14,8,128]{2,1,0:T(8,128)S(1)}, f32[14,8,128]{2,1,0:T(8,128)S(1)}, u32[]{:S(2)}, u32[]{:S(2)}) %collective-permute-start.3) | collective-permute-done | bytes 57376 | tf_op jit(solution)/shard_map/ppermute | solution.py:390
  42.8 0.0 collective-permute-start.4
  42.8 2.9 %collective-permute-start.5 = (f32[11,8,128]{2,1,0:T(8,128)S(1)}, f32[11,8,128]{2,1,0:T(8,128)S(1)}, u32[]{:S(2)}, u32[]{:S(2)}) collective-permute-start(f32[11,8,128]{2,1,0:T(8,128)S(1)} %get-tuple-element.30), channel_id=1, source_target_pairs={{1,0},{2,1},{3,2},{4,3},{5,4},{6,5},{7,6},{0,7},{9,8},{10,9},{11,1... | collective-permute-start | bytes 135176 | tf_op jit(solution)/shard_map/ppermute | solution.py:390
  45.8 7.8 %all-to-all-start.1 = ((f32[16,1,128]{2,1,0:T(1,128)}), f32[16,1,128]{2,1,0:T(1,128)S(1)}, u32[]{:S(2)}, u32[]{:S(2)}) async-start(f32[16,1,128]{2,1,0:T(1,128)} %bitcast.4), calls=%async_computation.1 | async-start | bytes 16384 | tf_op jit(solution)/shard_map/all_to_all | solution.py:395
  53.5 0.0 collective-permute-done.5.z2_ref
  53.6 1.1 %shard_map.63.rate_ref = f32[5,4,16,256]{3,2,1,0:T(8,128)S(1)} custom-call(f32[5,4,16,256]{3,2,1,0:T(8,128)S(1)} %copy-done.1, f32[29,8,128]{2,1,0:T(8,128)S(1)} %collective-permute-done.low_ref.x1_ref, f32[29,8,128]{2,1,0:T(8,128)S(1)} %collective-permute-done.1.high_ref.x2_ref, f32[14,8,128]{2,1,0:T(8,128)S(1)} %collective-permute-done.2.low_ref.y1_ref, ...), custom_call_target="tpu_custom_call" | custom-call | tf_op jit(solution)/shard_map/pallas_call | solution.py:431
  54.7 2.1 %shard_map.64 = (f32[4,4,16,256]{3,2,1,0:T(8,128)S(1)}, f32[14,8,128]{2,1,0:T(8,128)S(1)}, f32[14,8,128]{2,1,0:T(8,128)S(1)}) custom-call(f32[5,4,16,256]{3,2,1,0:T(8,128)S(1)} %copy-done.1, f32[11,8,128]{2,1,0:T(8,128)S(1)} %collective-permute-done.4.z1_ref, f32[11,8,128]{2,1,0:T(8,128)S(1)} %collective-permute-done.5.z2_ref, ...), custom_call_target="tpu_custom_call" | custom-call | tf_op jit(solution)/shard_map/pallas_call | solution.py:434
  56.8 3.8 %all-to-all-done.1 = f32[16,1,128]{2,1,0:T(1,128)S(1)} async-done(((f32[16,1,128]{2,1,0:T(1,128)}), f32[16,1,128]{2,1,0:T(1,128)S(1)}, u32[]{:S(2)}, u32[]{:S(2)}) %all-to-all-start.1) | async-done | bytes 8224 | tf_op jit(solution)/shard_map/all_to_all | solution.py:395
  60.6 0.9 %shard_map.65 = (f32[5,4,16,256]{3,2,1,0:T(8,128)}, f32[3,3,3,3,64]{4,3,2,1,0:T(4,128)}) custom-call(f32[5,4,16,256]{3,2,1,0:T(8,128)S(1)} %copy-done.1, f32[5,4,16,256]{3,2,1,0:T(8,128)S(1)} %shard_map.63.rate_ref, f32[4,4,16,256]{3,2,1,0:T(8,128)S(1)} %get-tuple-element.32.dep_ref, f32[16,128]{1,0:T(8,128)S(1)} %bitcast.9, ...), custom_call_target="tpu_custom_call" | custom-call | tf_op jit(solution)/shard_map/pallas_call | solution.py:446
  (8 shorter events, 0.0 us)
Async XLA Ops:
  0.6 1.0 %copy-start = (f32[5,4,16,256]{3,2,1,0:T(8,128)S(1)}, f32[5,4,16,256]{3,2,1,0:T(8,128)}, u32[]{:S(2)}) copy-start(f32[5,4,16,256]{3,2,1,0:T(8,128)} %u_ref.7) | copy-start | bytes 983044
  1.6 0.9 %copy-start.2 = (f32[3,3,3,8,64]{4,3,2,1,0:T(8,128)S(1)}, f32[3,3,3,8,64]{4,3,2,1,0:T(8,128)}, u32[]{:S(2)}) copy-start(f32[3,3,3,8,64]{4,3,2,1,0:T(8,128)} %data_ref.1) | copy-start | bytes 165892
  1.6 0.9 %copy-start.3 = (s32[3,3,3,64]{3,2,1,0:T(4,128)S(1)}, s32[3,3,3,64]{3,2,1,0:T(4,128)}, u32[]{:S(2)}) copy-start(s32[3,3,3,64]{3,2,1,0:T(4,128)} %host_ref.1) | copy-start | bytes 20740
  1.6 0.9 %copy-start.4 = (s32[3,3,3]{2,1,0:T(4,128)S(1)}, s32[3,3,3]{2,1,0:T(4,128)}, u32[]{:S(2)}) copy-start(s32[3,3,3]{2,1,0:T(4,128)} %count_ref.1) | copy-start | bytes 328
  2.7 50.9 %copy-start.1 = (f32[5,4,16,256]{3,2,1,0:T(8,128)S(1)}, f32[5,4,16,256]{3,2,1,0:T(8,128)}, u32[]{:S(2)}) copy-start(f32[5,4,16,256]{3,2,1,0:T(8,128)} %u_ref.7) | copy-start | bytes 983044
  2.7 29.9 %collective-permute-start = (f32[29,8,128]{2,1,0:T(8,128)S(1)}, f32[29,8,128]{2,1,0:T(8,128)S(1)}, u32[]{:S(2)}, u32[]{:S(2)}) collective-permute-start(f32[29,8,128]{2,1,0:T(8,128)S(1)} %get-tuple-element.21), channel_id=1, source_target_pairs={{0,64},{64,128},{128,192},{192,256},{256,320},{320,384},{384,448},... | collective-permute-start | bytes 356360 | tf_op jit(solution)/shard_map/ppermute | solution.py:389
  7.1 25.5 %collective-permute-start.1 = (f32[29,8,128]{2,1,0:T(8,128)S(1)}, f32[29,8,128]{2,1,0:T(8,128)S(1)}, u32[]{:S(2)}, u32[]{:S(2)}) collective-permute-start(f32[29,8,128]{2,1,0:T(8,128)S(1)} %get-tuple-element.22), channel_id=1, source_target_pairs={{64,0},{128,64},{192,128},{256,192},{320,256},{384,320},{448,384},... | collective-permute-start | bytes 356360 | tf_op jit(solution)/shard_map/ppermute | solution.py:390
  33.2 6.1 %collective-permute-start.2 = (f32[14,8,128]{2,1,0:T(8,128)S(1)}, f32[14,8,128]{2,1,0:T(8,128)S(1)}, u32[]{:S(2)}, u32[]{:S(2)}) collective-permute-start(f32[14,8,128]{2,1,0:T(8,128)S(1)} %get-tuple-element.26), channel_id=1, source_target_pairs={{0,8},{8,16},{16,24},{24,32},{32,40},{40,48},{48,56},{1,9},{9,17},... | collective-permute-start | bytes 172040 | tf_op jit(solution)/shard_map/ppermute | solution.py:389
  36.7 6.1 %collective-permute-start.3 = (f32[14,8,128]{2,1,0:T(8,128)S(1)}, f32[14,8,128]{2,1,0:T(8,128)S(1)}, u32[]{:S(2)}, u32[]{:S(2)}) collective-permute-start(f32[14,8,128]{2,1,0:T(8,128)S(1)} %get-tuple-element.27), channel_id=1, source_target_pairs={{8,0},{16,8},{24,16},{32,24},{40,32},{48,40},{56,48},{9,1},{17,9},... | collective-permute-start | bytes 172040 | tf_op jit(solution)/shard_map/ppermute | solution.py:390
  42.8 10.7 %collective-permute-start.4 = (f32[11,8,128]{2,1,0:T(8,128)S(1)}, f32[11,8,128]{2,1,0:T(8,128)S(1)}, u32[]{:S(2)}, u32[]{:S(2)}) collective-permute-start(f32[11,8,128]{2,1,0:T(8,128)S(1)} %get-tuple-element.29), channel_id=1, source_target_pairs={{0,1},{1,2},{2,3},{3,4},{4,5},{5,6},{6,7},{7,0},{8,9},{9,10},{10,1... | collective-permute-start | bytes 135176 | tf_op jit(solution)/shard_map/ppermute | solution.py:389
  42.8 10.7 %collective-permute-start.5 = (f32[11,8,128]{2,1,0:T(8,128)S(1)}, f32[11,8,128]{2,1,0:T(8,128)S(1)}, u32[]{:S(2)}, u32[]{:S(2)}) collective-permute-start(f32[11,8,128]{2,1,0:T(8,128)S(1)} %get-tuple-element.30), channel_id=1, source_target_pairs={{1,0},{2,1},{3,2},{4,3},{5,4},{6,5},{7,6},{0,7},{9,8},{10,9},{11,1... | collective-permute-start | bytes 135176 | tf_op jit(solution)/shard_map/ppermute | solution.py:390
  45.8 14.8 %all-to-all-start.1 = ((f32[16,1,128]{2,1,0:T(1,128)}), f32[16,1,128]{2,1,0:T(1,128)S(1)}, u32[]{:S(2)}, u32[]{:S(2)}) async-start(f32[16,1,128]{2,1,0:T(1,128)} %bitcast.4), calls=%async_computation.1 | async-start | bytes 16384 | tf_op jit(solution)/shard_map/all_to_all | solution.py:395

commit v10 on v9

--- a/solution.py
+++ b/solution.py
@@ -410,15 +410,15 @@
 
 def local(fluid_state, parcel_data, host_element, slot_counts):
     nx, ny, nz = (lax.axis_size(axis) for axis in ("gx", "gy", "gz"))
-    spaced = [[x * nz + z for x in range(p, nx, 2) for z in range(nz)] for p in range(2)]
-    paired = [[x * ny + y for x in (2 * k, 2 * k + 1) for y in range(ny)] for k in range(nx // 2)]
+    spaced = [[x * ny + y for x in range(p, nx, 2) for y in range(ny)] for p in range(2)]
+    paired = [[x * nz + z for x in (2 * k, 2 * k + 1) for z in range(nz)] for k in range(nx // 2)]
     row = jax.ShapeDtypeStruct((len(spaced[0]), 128), F32)
     face_up, face_down, faces, top = call(face_kernel, (tiles_of(20), tiles_of(20), tiles_of(14), row))(fluid_state)
     x_up, x_down, keep_x = call(pack_kernel, (tiles_of(29), tiles_of(29), tiles_of(9)))(
         parcel_data, host_element, slot_counts, face_up, face_down
     )
     x1, x2 = exchanged(x_up, x_down, "gx", False)
-    tops = all_tops(top, ("gx", "gz"), spaced)
+    tops = all_tops(top, ("gx", "gy"), spaced)
     row = jax.ShapeDtypeStruct((len(paired[0]), 128), F32)
     y_up, y_down, keep_y, top = call(turn_y_kernel, (tiles_of(14), tiles_of(14), tiles_of(9), row))(
         x1, x2, keep_x, faces, tops
@@ -426,7 +426,7 @@
     y1, y2 = exchanged(y_up, y_down, "gy", False)
     z_up, z_down, keep_z = call(turn_z_kernel, (tiles_of(11), tiles_of(11), tiles_of(9)))(y1, y2, keep_y, faces)
     z1, z2 = exchanged(z_up, z_down, "gz", True)
-    top = all_tops(top, ("gx", "gy"), paired)
+    top = all_tops(top, ("gx", "gz"), paired)
     field = jax.ShapeDtypeStruct((5, 4, 16, 256), F32)
     rate = call(
         rate_kernel, field, [pltpu.VMEM((5, 4, 16, 256), F32), pltpu.VMEM((2, 16, 256), F32)],

time: 61.8 us -> 61.4 us (level)
  the two profiles are of different devices: /device:TPU:8 before, /device:TPU:1 now
where the time goes in v10:
time: 61.4 us; the launch traced here: 61.1 us
  blocking collectives  27.7 us (45%)
  starting transfers between devices  20.1 us (33%)
  waiting for transfers between devices  5.82 us (9%)
  Pallas kernels  5.09 us (8%)
  local copies, waits for them, and re-layouts  1.67 us (3%)
  between operations  0.74 us (1%)
    all_to_all x1, blocking collectives, all_tops(): return lax.all_to_all(top, axes, 0, 0, axis_index_groups=groups, tiled=True)  27.7 us
    ppermute x3, starting transfers between devices, exchanged(): lax.ppermute(up, axis, pairs)  12.4 us
    all_to_all x1, starting transfers between devices, all_tops(): return lax.all_to_all(top, axes, 0, 0, axis_index_groups=groups, tiled=True)  5.12 us
    ppermute x3, waiting for transfers between devices, exchanged(): lax.ppermute(down, axis, [(j, i) for i, j in pairs])  3.62 us
    ppermute x3, starting transfers between devices, exchanged(): lax.ppermute(down, axis, [(j, i) for i, j in pairs])  2.59 us
    all_to_all x1, waiting for transfers between devices, all_tops(): return lax.all_to_all(top, axes, 0, 0, axis_index_groups=groups, tiled=True)  2.19 us
    pallas_call x1, Pallas kernels, local(): call(parcel_kernel, (jax.ShapeDtypeStruct((4, 4, 16, 256), F32), tiles_of...  2.1 us
    unnamed x10, local copies, waits for them, and re-layouts  1.67 us
  transfers between devices with their start and end apart: 7, of which 2 were waited for; matrix products, arithmetic and copies ran while one was open for 0% of the time, Pallas kernels for 5%

profile of v10, /device:TPU:1, one launch (start us, length us, event | category | flops | bytes accessed | tf_op | source)
XLA Modules:
  0.0 61.1 jit_solution(5205362018614339646)
XLA Ops:
  0.6 0.0 copy-start
  0.6 1.0 %copy-done = f32[5,4,16,256]{3,2,1,0:T(8,128)S(1)} copy-done((f32[5,4,16,256]{3,2,1,0:T(8,128)S(1)}, f32[5,4,16,256]{3,2,1,0:T(8,128)}, u32[]{:S(2)}) %copy-start) | copy-done | bytes 327704
  1.6 0.2 shard_map.59
  1.8 0.7 %copy-done.2 = f32[3,3,3,8,64]{4,3,2,1,0:T(8,128)S(1)} copy-done((f32[3,3,3,8,64]{4,3,2,1,0:T(8,128)S(1)}, f32[3,3,3,8,64]{4,3,2,1,0:T(8,128)}, u32[]{:S(2)}) %copy-start.2) | copy-done | bytes 55320
  2.5 0.2 shard_map.60
  2.7 0.0 copy-start.1
  2.7 5.0 %collective-permute-start = (f32[29,8,128]{2,1,0:T(8,128)S(1)}, f32[29,8,128]{2,1,0:T(8,128)S(1)}, u32[]{:S(2)}, u32[]{:S(2)}) collective-permute-start(f32[29,8,128]{2,1,0:T(8,128)S(1)} %get-tuple-element.21), channel_id=1, source_target_pairs={{0,64},{64,128},{128,192},{192,256},{256,320},{320,384},{384,448},... | collective-permute-start | bytes 356360 | tf_op jit(solution)/shard_map/ppermute | solution.py:389
  7.7 1.3 %collective-permute-start.1 = (f32[29,8,128]{2,1,0:T(8,128)S(1)}, f32[29,8,128]{2,1,0:T(8,128)S(1)}, u32[]{:S(2)}, u32[]{:S(2)}) collective-permute-start(f32[29,8,128]{2,1,0:T(8,128)S(1)} %get-tuple-element.22), channel_id=1, source_target_pairs={{64,0},{128,64},{192,128},{256,192},{320,256},{384,320},{448,384},... | collective-permute-start | bytes 356360 | tf_op jit(solution)/shard_map/ppermute | solution.py:390
  9.0 27.7 %all_to_all.22 = f32[32,1,128]{2,1,0:T(1,128)S(1)} all-to-all(f32[32,1,128]{2,1,0:T(1,128)S(1)} %bitcast.10), channel_id=1, replica_groups={{0,8,16,24,32,40,48,56,128,136,144,152,160,168,176,184,256,264,272,280,..., dimensions={0} | all-to-all | bytes 32768 | tf_op jit(solution)/shard_map/all_to_all | solution.py:395
  36.7 0.0 collective-permute-done.low_ref.x1_ref
  36.7 0.0 collective-permute-done.1.high_ref.x2_ref
  36.7 0.6 %shard_map.61 = (f32[14,8,128]{2,1,0:T(8,128)S(1)}, f32[14,8,128]{2,1,0:T(8,128)S(1)}, f32[9,8,128]{2,1,0:T(8,128)S(1)}, f32[16,128]{1,0:T(8,128)}) custom-call(f32[29,8,128]{2,1,0:T(8,128)S(1)} %collective-permute-done.low_ref.x1_ref, f32[29,8,128]{2,1,0:T(8,128)S(1)} %collective-permute-done.1.high_ref.x2_ref, f32[9,8,128]{2,1,0:T(8,128)S(1)} %get-tuple-element.23.own_ref, ...), custom_call_target="tpu_custom_call" | custom-call | tf_op jit(solution)/shard_map/pallas_call | solution.py:423
  37.3 2.2 %collective-permute-start.2 = (f32[14,8,128]{2,1,0:T(8,128)S(1)}, f32[14,8,128]{2,1,0:T(8,128)S(1)}, u32[]{:S(2)}, u32[]{:S(2)}) collective-permute-start(f32[14,8,128]{2,1,0:T(8,128)S(1)} %get-tuple-element.26), channel_id=1, source_target_pairs={{0,8},{8,16},{16,24},{24,32},{32,40},{40,48},{48,56},{1,9},{9,17},... | collective-permute-start | bytes 172040 | tf_op jit(solution)/shard_map/ppermute | solution.py:389
  39.5 1.3 %collective-permute-start.3 = (f32[14,8,128]{2,1,0:T(8,128)S(1)}, f32[14,8,128]{2,1,0:T(8,128)S(1)}, u32[]{:S(2)}, u32[]{:S(2)}) collective-permute-start(f32[14,8,128]{2,1,0:T(8,128)S(1)} %get-tuple-element.27), channel_id=1, source_target_pairs={{8,0},{16,8},{24,16},{32,24},{40,32},{48,40},{56,48},{9,1},{17,9},... | collective-permute-start | bytes 172040 | tf_op jit(solution)/shard_map/ppermute | solution.py:390
  40.8 3.6 %collective-permute-done.3.high_ref.y2_ref = f32[14,8,128]{2,1,0:T(8,128)S(1)} collective-permute-done((f32[14,8,128]{2,1,0:T(8,128)S(1)}, f32[14,8,128]{2,1,0:T(8,128)S(1)}, u32[]{:S(2)}, u32[]{:S(2)}) %collective-permute-start.3) | collective-permute-done | bytes 57376 | tf_op jit(solution)/shard_map/ppermute | solution.py:390
  44.5 5.2 %collective-permute-start.4 = (f32[11,8,128]{2,1,0:T(8,128)S(1)}, f32[11,8,128]{2,1,0:T(8,128)S(1)}, u32[]{:S(2)}, u32[]{:S(2)}) collective-permute-start(f32[11,8,128]{2,1,0:T(8,128)S(1)} %get-tuple-element.29), channel_id=1, source_target_pairs={{0,1},{1,2},{2,3},{3,4},{4,5},{5,6},{6,7},{7,0},{8,9},{9,10},{10,1... | collective-permute-start | bytes 135176 | tf_op jit(solution)/shard_map/ppermute | solution.py:389
  49.7 0.0 collective-permute-start.5
  49.7 5.1 %all-to-all-start.1 = ((f32[16,1,128]{2,1,0:T(1,128)}), f32[16,1,128]{2,1,0:T(1,128)S(1)}, u32[]{:S(2)}, u32[]{:S(2)}) async-start(f32[16,1,128]{2,1,0:T(1,128)} %bitcast.4), calls=%async_computation.1 | async-start | bytes 16384 | tf_op jit(solution)/shard_map/all_to_all | solution.py:395
  54.8 0.0 collective-permute-done.4.z1_ref
  54.8 0.0 collective-permute-done.5.z2_ref
  54.8 1.1 %shard_map.63.rate_ref = f32[5,4,16,256]{3,2,1,0:T(8,128)S(1)} custom-call(f32[5,4,16,256]{3,2,1,0:T(8,128)S(1)} %copy-done.1, f32[29,8,128]{2,1,0:T(8,128)S(1)} %collective-permute-done.low_ref.x1_ref, f32[29,8,128]{2,1,0:T(8,128)S(1)} %collective-permute-done.1.high_ref.x2_ref, f32[14,8,128]{2,1,0:T(8,128)S(1)} %collective-permute-done.2.low_ref.y1_ref, ...), custom_call_target="tpu_custom_call" | custom-call | tf_op jit(solution)/shard_map/pallas_call | solution.py:431
  56.0 2.1 %shard_map.64 = (f32[4,4,16,256]{3,2,1,0:T(8,128)S(1)}, f32[14,8,128]{2,1,0:T(8,128)S(1)}, f32[14,8,128]{2,1,0:T(8,128)S(1)}) custom-call(f32[5,4,16,256]{3,2,1,0:T(8,128)S(1)} %copy-done.1, f32[11,8,128]{2,1,0:T(8,128)S(1)} %collective-permute-done.4.z1_ref, f32[11,8,128]{2,1,0:T(8,128)S(1)} %collective-permute-done.5.z2_ref, ...), custom_call_target="tpu_custom_call" | custom-call | tf_op jit(solution)/shard_map/pallas_call | solution.py:434
  58.1 2.2 %all-to-all-done.1 = f32[16,1,128]{2,1,0:T(1,128)S(1)} async-done(((f32[16,1,128]{2,1,0:T(1,128)}), f32[16,1,128]{2,1,0:T(1,128)S(1)}, u32[]{:S(2)}, u32[]{:S(2)}) %all-to-all-start.1) | async-done | bytes 8224 | tf_op jit(solution)/shard_map/all_to_all | solution.py:395
  60.3 0.9 %shard_map.65 = (f32[5,4,16,256]{3,2,1,0:T(8,128)}, f32[3,3,3,3,64]{4,3,2,1,0:T(4,128)}) custom-call(f32[5,4,16,256]{3,2,1,0:T(8,128)S(1)} %copy-done.1, f32[5,4,16,256]{3,2,1,0:T(8,128)S(1)} %shard_map.63.rate_ref, f32[4,4,16,256]{3,2,1,0:T(8,128)S(1)} %get-tuple-element.32.dep_ref, f32[16,128]{1,0:T(8,128)S(1)} %bitcast.9, ...), custom_call_target="tpu_custom_call" | custom-call | tf_op jit(solution)/shard_map/pallas_call | solution.py:446
  (8 shorter events, 0.0 us)
Async XLA Ops:
  0.6 1.0 %copy-start = (f32[5,4,16,256]{3,2,1,0:T(8,128)S(1)}, f32[5,4,16,256]{3,2,1,0:T(8,128)}, u32[]{:S(2)}) copy-start(f32[5,4,16,256]{3,2,1,0:T(8,128)} %u_ref.7) | copy-start | bytes 983044
  1.6 0.9 %copy-start.2 = (f32[3,3,3,8,64]{4,3,2,1,0:T(8,128)S(1)}, f32[3,3,3,8,64]{4,3,2,1,0:T(8,128)}, u32[]{:S(2)}) copy-start(f32[3,3,3,8,64]{4,3,2,1,0:T(8,128)} %data_ref.1) | copy-start | bytes 165892
  1.6 0.9 %copy-start.3 = (s32[3,3,3,64]{3,2,1,0:T(4,128)S(1)}, s32[3,3,3,64]{3,2,1,0:T(4,128)}, u32[]{:S(2)}) copy-start(s32[3,3,3,64]{3,2,1,0:T(4,128)} %host_ref.1) | copy-start | bytes 20740
  1.6 0.9 %copy-start.4 = (s32[3,3,3]{2,1,0:T(4,128)S(1)}, s32[3,3,3]{2,1,0:T(4,128)}, u32[]{:S(2)}) copy-start(s32[3,3,3]{2,1,0:T(4,128)} %count_ref.1) | copy-start | bytes 328
  2.7 52.1 %copy-start.1 = (f32[5,4,16,256]{3,2,1,0:T(8,128)S(1)}, f32[5,4,16,256]{3,2,1,0:T(8,128)}, u32[]{:S(2)}) copy-start(f32[5,4,16,256]{3,2,1,0:T(8,128)} %u_ref.7) | copy-start | bytes 983044
  2.7 34.0 %collective-permute-start = (f32[29,8,128]{2,1,0:T(8,128)S(1)}, f32[29,8,128]{2,1,0:T(8,128)S(1)}, u32[]{:S(2)}, u32[]{:S(2)}) collective-permute-start(f32[29,8,128]{2,1,0:T(8,128)S(1)} %get-tuple-element.21), channel_id=1, source_target_pairs={{0,64},{64,128},{128,192},{192,256},{256,320},{320,384},{384,448},... | collective-permute-start | bytes 356360 | tf_op jit(solution)/shard_map/ppermute | solution.py:389
  7.7 29.0 %collective-permute-start.1 = (f32[29,8,128]{2,1,0:T(8,128)S(1)}, f32[29,8,128]{2,1,0:T(8,128)S(1)}, u32[]{:S(2)}, u32[]{:S(2)}) collective-permute-start(f32[29,8,128]{2,1,0:T(8,128)S(1)} %get-tuple-element.22), channel_id=1, source_target_pairs={{64,0},{128,64},{192,128},{256,192},{320,256},{384,320},{448,384},... | collective-permute-start | bytes 356360 | tf_op jit(solution)/shard_map/ppermute | solution.py:390
  37.3 3.5 %collective-permute-start.2 = (f32[14,8,128]{2,1,0:T(8,128)S(1)}, f32[14,8,128]{2,1,0:T(8,128)S(1)}, u32[]{:S(2)}, u32[]{:S(2)}) collective-permute-start(f32[14,8,128]{2,1,0:T(8,128)S(1)} %get-tuple-element.26), channel_id=1, source_target_pairs={{0,8},{8,16},{16,24},{24,32},{32,40},{40,48},{48,56},{1,9},{9,17},... | collective-permute-start | bytes 172040 | tf_op jit(solution)/shard_map/ppermute | solution.py:389
  39.5 4.9 %collective-permute-start.3 = (f32[14,8,128]{2,1,0:T(8,128)S(1)}, f32[14,8,128]{2,1,0:T(8,128)S(1)}, u32[]{:S(2)}, u32[]{:S(2)}) collective-permute-start(f32[14,8,128]{2,1,0:T(8,128)S(1)} %get-tuple-element.27), channel_id=1, source_target_pairs={{8,0},{16,8},{24,16},{32,24},{40,32},{48,40},{56,48},{9,1},{17,9},... | collective-permute-start | bytes 172040 | tf_op jit(solution)/shard_map/ppermute | solution.py:390
  44.5 10.3 %collective-permute-start.4 = (f32[11,8,128]{2,1,0:T(8,128)S(1)}, f32[11,8,128]{2,1,0:T(8,128)S(1)}, u32[]{:S(2)}, u32[]{:S(2)}) collective-permute-start(f32[11,8,128]{2,1,0:T(8,128)S(1)} %get-tuple-element.29), channel_id=1, source_target_pairs={{0,1},{1,2},{2,3},{3,4},{4,5},{5,6},{6,7},{7,0},{8,9},{9,10},{10,1... | collective-permute-start | bytes 135176 | tf_op jit(solution)/shard_map/ppermute | solution.py:389
  49.7 5.1 %collective-permute-start.5 = (f32[11,8,128]{2,1,0:T(8,128)S(1)}, f32[11,8,128]{2,1,0:T(8,128)S(1)}, u32[]{:S(2)}, u32[]{:S(2)}) collective-permute-start(f32[11,8,128]{2,1,0:T(8,128)S(1)} %get-tuple-element.30), channel_id=1, source_target_pairs={{1,0},{2,1},{3,2},{4,3},{5,4},{6,5},{7,6},{0,7},{9,8},{10,9},{11,1... | collective-permute-start | bytes 135176 | tf_op jit(solution)/shard_map/ppermute | solution.py:390
  49.7 10.6 %all-to-all-start.1 = ((f32[16,1,128]{2,1,0:T(1,128)}), f32[16,1,128]{2,1,0:T(1,128)S(1)}, u32[]{:S(2)}, u32[]{:S(2)}) async-start(f32[16,1,128]{2,1,0:T(1,128)} %bitcast.4), calls=%async_computation.1 | async-start | bytes 16384 | tf_op jit(solution)/shard_map/all_to_all | solution.py:395

commit v11 on v7

--- a/solution.py
+++ b/solution.py
@@ -114,27 +114,27 @@
         down_ref[FACE + t] = face_down_ref[t]
 
 
-def turn_y_kernel(low_ref, high_ref, own_ref, face_ref, tops_ref, up_ref, down_ref, keep_ref, top_ref):
+def turn_z_kernel(low_ref, high_ref, own_ref, face_ref, tops_ref, up_ref, down_ref, keep_ref, top_ref):
     top_ref[...] = jnp.broadcast_to(jnp.max(tops_ref[...], axis=0, keepdims=True), top_ref.shape)
     for a, source in enumerate((low_ref, own_ref, high_ref)):
-        for c in range(3):
-            up_ref[3 * a + c] = source[6 + c]
-            down_ref[3 * a + c] = source[c]
-            keep_ref[3 * a + c] = source[3 + c]
+        for b in range(3):
+            up_ref[3 * a + b] = source[3 * b + 2]
+            down_ref[3 * a + b] = source[3 * b]
+            keep_ref[3 * a + b] = source[3 * b + 1]
+    for yh in range(2):
+        up_ref[FACE + yh] = face_ref[10 + yh]
+        down_ref[FACE + yh] = face_ref[12 + yh]
+
+
+def turn_y_kernel(low_ref, high_ref, own_ref, face_ref, up_ref, down_ref, keep_ref):
+    for c, source in enumerate((low_ref, own_ref, high_ref)):
+        for a in range(3):
+            up_ref[3 * a + c] = source[3 * a + 2]
+            down_ref[3 * a + c] = source[3 * a]
+            keep_ref[3 * a + c] = source[3 * a + 1]
     for v in range(5):
         up_ref[FACE + v] = face_ref[v]
         down_ref[FACE + v] = face_ref[5 + v]
-
-
-def turn_z_kernel(low_ref, high_ref, own_ref, face_ref, up_ref, down_ref, keep_ref):
-    for b, source in enumerate((low_ref, own_ref, high_ref)):
-        for a in range(3):
-            up_ref[3 * a + b] = source[3 * a + 2]
-            down_ref[3 * a + b] = source[3 * a]
-            keep_ref[3 * a + b] = source[3 * a + 1]
-    for yh in range(2):
-        up_ref[FACE + yh] = face_ref[10 + yh]
-        down_ref[FACE + yh] = face_ref[12 + yh]
 
 
 def wall(axis, last, own, received, sign_of):
@@ -268,9 +268,9 @@
     return high, (value - high.astype(F32)).astype(BF16)
 
 
-def parcel_kernel(u_ref, z1_ref, z2_ref, own_ref, dep_ref, base_ref, acc_ref, vel_hi, vel_lo, z_hi, z_lo, a_hi, a_lo):
-    sides = (z1_ref, own_ref, z2_ref)
-    tiles = [sides[g % 3][g // 3] for g in range(27)] + [jnp.zeros((8, 128), F32)]
+def parcel_kernel(u_ref, y1_ref, y2_ref, own_ref, dep_ref, base_ref, acc_ref, vel_hi, vel_lo, z_hi, z_lo, a_hi, a_lo):
+    sides = (y1_ref, own_ref, y2_ref)
+    tiles = [sides[g // 3 % 3][3 * (g // 9) + g % 3] for g in range(27)] + [jnp.zeros((8, 128), F32)]
     for i in range(4):
         inverse = 1.0 / u_ref[0, i]
         for d in range(3):
@@ -418,12 +418,12 @@
     x1, x2 = exchanged(x_up, x_down, "gx", False)
     tops = all_tops(top, ("gx", "gy"))
     row = jax.ShapeDtypeStruct((lax.axis_size("gz"), 128), F32)
-    y_up, y_down, keep_y, top = call(turn_y_kernel, (tiles_of(14), tiles_of(14), tiles_of(9), row))(
+    z_up, z_down, keep_z, top = call(turn_z_kernel, (tiles_of(11), tiles_of(11), tiles_of(9), row))(
         x1, x2, keep_x, faces, tops
     )
+    z1, z2 = exchanged(z_up, z_down, "gz", True)
+    y_up, y_down, keep_y = call(turn_y_kernel, (tiles_of(14), tiles_of(14), tiles_of(9)))(z1, z2, keep_z, faces)
     y1, y2 = exchanged(y_up, y_down, "gy", False)
-    z_up, z_down, keep_z = call(turn_z_kernel, (tiles_of(11), tiles_of(11), tiles_of(9)))(y1, y2, keep_y, faces)
-    z1, z2 = exchanged(z_up, z_down, "gz", True)
     top = all_tops(top, "gz")
     field = jax.ShapeDtypeStruct((5, 4, 16, 256), F32)
     rate = call(
@@ -440,7 +440,7 @@
             pltpu.VMEM((256, 1792), BF16),
             pltpu.VMEM((256, 1792), BF16),
         ],
-    )(fluid_state, z1, z2, keep_z)
+    )(fluid_state, y1, y2, keep_y)
     return call(finish_kernel, (field, jax.ShapeDtypeStruct((3, 3, 3, 3, 64), F32)))(
         fluid_state, rate, deposit, top, base, acc
     )

time: 60.8 us -> 58.5 us (0.962)
  starting transfers between devices: 19.9 us -> 17.9 us
    ppermute x3, starting transfers between devices: 12.3 us -> 11 us  [exchanged(): lax.ppermute(up, axis, pairs)]
    ppermute x3, waiting for transfers between devices: 3.62 us -> 2.34 us  [exchanged(): lax.ppermute(down, axis, [(j, i) for i, j in pairs])]
    ppermute x3, waiting for transfers between devices: 0.01 us -> 1.14 us  [exchanged(): lax.ppermute(up, axis, pairs)]
    all_to_all x1, starting transfers between devices: 5.07 us -> 4.35 us  [all_tops(): return lax.all_to_all(top, axis, 0, 0, tiled=True)]
  transfers between devices with their start and end apart: 7 -> 7, of which waited for: 2 -> 3; matrix products, arithmetic and copies ran while one was open for 0% -> 0% of each run, Pallas kernels for 5% -> 6%
where the time goes in v11:
time: 58.5 us; the launch traced here: 58.2 us
  blocking collectives  28.1 us (48%)
  starting transfers between devices  17.9 us (31%)
  Pallas kernels  5.09 us (9%)
  waiting for transfers between devices  4.7 us (8%)
  local copies, waits for them, and re-layouts  1.67 us (3%)
  between operations  0.72 us (1%)
    all_to_all x1, blocking collectives, all_tops(): return lax.all_to_all(top, axis, 0, 0, tiled=True)  28.1 us
    ppermute x3, starting transfers between devices, exchanged(): lax.ppermute(up, axis, pairs)  11 us
    all_to_all x1, starting transfers between devices, all_tops(): return lax.all_to_all(top, axis, 0, 0, tiled=True)  4.35 us
    ppermute x3, starting transfers between devices, exchanged(): lax.ppermute(down, axis, [(j, i) for i, j in pairs])  2.59 us
    ppermute x3, waiting for transfers between devices, exchanged(): lax.ppermute(down, axis, [(j, i) for i, j in pairs])  2.34 us
    pallas_call x1, Pallas kernels, local(): call(parcel_kernel, (jax.ShapeDtypeStruct((4, 4, 16, 256), F32), tiles_of...  2.1 us
    unnamed x10, local copies, waits for them, and re-layouts  1.67 us
    all_to_all x1, waiting for transfers between devices, all_tops(): return lax.all_to_all(top, axis, 0, 0, tiled=True)  1.22 us
  transfers between devices with their start and end apart: 7, of which 3 were waited for; matrix products, arithmetic and copies ran while one was open for 0% of the time, Pallas kernels for 6%

profile of v11, /device:TPU:1, one launch (start us, length us, event | category | flops | bytes accessed | tf_op | source)
XLA Modules:
  0.0 58.2 jit_solution(10377060395323447617)
XLA Ops:
  0.6 0.0 copy-start
  0.6 1.0 %copy-done = f32[5,4,16,256]{3,2,1,0:T(8,128)S(1)} copy-done((f32[5,4,16,256]{3,2,1,0:T(8,128)S(1)}, f32[5,4,16,256]{3,2,1,0:T(8,128)}, u32[]{:S(2)}) %copy-start) | copy-done | bytes 327704
  1.6 0.2 shard_map.59
  1.8 0.7 %copy-done.2 = f32[3,3,3,8,64]{4,3,2,1,0:T(8,128)S(1)} copy-done((f32[3,3,3,8,64]{4,3,2,1,0:T(8,128)S(1)}, f32[3,3,3,8,64]{4,3,2,1,0:T(8,128)}, u32[]{:S(2)}) %copy-start.2) | copy-done | bytes 55320
  2.5 0.2 shard_map.60
  2.7 0.0 copy-start.1
  2.7 5.0 %collective-permute-start = (f32[29,8,128]{2,1,0:T(8,128)S(1)}, f32[29,8,128]{2,1,0:T(8,128)S(1)}, u32[]{:S(2)}, u32[]{:S(2)}) collective-permute-start(f32[29,8,128]{2,1,0:T(8,128)S(1)} %get-tuple-element.21), channel_id=1, source_target_pairs={{0,64},{64,128},{128,192},{192,256},{256,320},{320,384},{384,448},... | collective-permute-start | bytes 356360 | tf_op jit(solution)/shard_map/ppermute | solution.py:389
  7.7 1.3 %collective-permute-start.1 = (f32[29,8,128]{2,1,0:T(8,128)S(1)}, f32[29,8,128]{2,1,0:T(8,128)S(1)}, u32[]{:S(2)}, u32[]{:S(2)}) collective-permute-start(f32[29,8,128]{2,1,0:T(8,128)S(1)} %get-tuple-element.22), channel_id=1, source_target_pairs={{64,0},{128,64},{192,128},{256,192},{320,256},{384,320},{448,384},... | collective-permute-start | bytes 356360 | tf_op jit(solution)/shard_map/ppermute | solution.py:390
  9.0 28.1 %all_to_all.22 = f32[64,1,128]{2,1,0:T(1,128)S(1)} all-to-all(f32[64,1,128]{2,1,0:T(1,128)S(1)} %bitcast.9), channel_id=1, replica_groups=mesh['gx'=8,'gy'=8,'gz'=8] {'gx','gy'}, dimensions={0} | all-to-all | bytes 65536 | tf_op jit(solution)/shard_map/all_to_all | solution.py:395
  37.1 0.0 collective-permute-done.low_ref.x1_ref
  37.1 0.0 collective-permute-done.1.high_ref.x2_ref
  37.1 0.6 %shard_map.61 = (f32[11,8,128]{2,1,0:T(8,128)S(1)}, f32[11,8,128]{2,1,0:T(8,128)S(1)}, f32[9,8,128]{2,1,0:T(8,128)S(1)}, f32[8,128]{1,0:T(8,128)}) custom-call(f32[29,8,128]{2,1,0:T(8,128)S(1)} %collective-permute-done.low_ref.x1_ref, f32[29,8,128]{2,1,0:T(8,128)S(1)} %collective-permute-done.1.high_ref.x2_ref, f32[9,8,128]{2,1,0:T(8,128)S(1)} %get-tuple-element.23.own_ref, ...), custom_call_target="tpu_custom_call" | custom-call | tf_op jit(solution)/shard_map/pallas_call | solution.py:421
  37.7 3.8 %collective-permute-start.2 = (f32[11,8,128]{2,1,0:T(8,128)S(1)}, f32[11,8,128]{2,1,0:T(8,128)S(1)}, u32[]{:S(2)}, u32[]{:S(2)}) collective-permute-start(f32[11,8,128]{2,1,0:T(8,128)S(1)} %get-tuple-element.26), channel_id=1, source_target_pairs={{0,1},{1,2},{2,3},{3,4},{4,5},{5,6},{6,7},{7,0},{8,9},{9,10},{10,1... | collective-permute-start | bytes 135176 | tf_op jit(solution)/shard_map/ppermute | solution.py:389
  41.5 0.0 collective-permute-start.3
  41.5 1.1 %collective-permute-done.2.low_ref.z1_ref = f32[11,8,128]{2,1,0:T(8,128)S(1)} collective-permute-done((f32[11,8,128]{2,1,0:T(8,128)S(1)}, f32[11,8,128]{2,1,0:T(8,128)S(1)}, u32[]{:S(2)}, u32[]{:S(2)}) %collective-permute-start.2) | collective-permute-done | bytes 45088 | tf_op jit(solution)/shard_map/ppermute | solution.py:389
  42.6 2.3 %collective-permute-done.3.high_ref.z2_ref = f32[11,8,128]{2,1,0:T(8,128)S(1)} collective-permute-done((f32[11,8,128]{2,1,0:T(8,128)S(1)}, f32[11,8,128]{2,1,0:T(8,128)S(1)}, u32[]{:S(2)}, u32[]{:S(2)}) %collective-permute-start.3) | collective-permute-done | bytes 45088 | tf_op jit(solution)/shard_map/ppermute | solution.py:390
  45.0 2.2 %collective-permute-start.4 = (f32[14,8,128]{2,1,0:T(8,128)S(1)}, f32[14,8,128]{2,1,0:T(8,128)S(1)}, u32[]{:S(2)}, u32[]{:S(2)}) collective-permute-start(f32[14,8,128]{2,1,0:T(8,128)S(1)} %get-tuple-element.29), channel_id=1, source_target_pairs={{0,8},{8,16},{16,24},{24,32},{32,40},{40,48},{48,56},{1,9},{9,17},... | collective-permute-start | bytes 172040 | tf_op jit(solution)/shard_map/ppermute | solution.py:389
  47.2 1.3 %collective-permute-start.5 = (f32[14,8,128]{2,1,0:T(8,128)S(1)}, f32[14,8,128]{2,1,0:T(8,128)S(1)}, u32[]{:S(2)}, u32[]{:S(2)}) collective-permute-start(f32[14,8,128]{2,1,0:T(8,128)S(1)} %get-tuple-element.30), channel_id=1, source_target_pairs={{8,0},{16,8},{24,16},{32,24},{40,32},{48,40},{56,48},{9,1},{17,9},... | collective-permute-start | bytes 172040 | tf_op jit(solution)/shard_map/ppermute | solution.py:390
  48.5 4.4 %all-to-all-start.1 = ((f32[8,1,128]{2,1,0:T(1,128)}), f32[8,1,128]{2,1,0:T(1,128)S(1)}, u32[]{:S(2)}, u32[]{:S(2)}) async-start(f32[8,1,128]{2,1,0:T(1,128)} %bitcast.4), calls=%async_computation.1 | async-start | bytes 8192 | tf_op jit(solution)/shard_map/all_to_all | solution.py:395
  52.8 0.0 collective-permute-done.4.y1_ref
  52.9 1.1 %shard_map.63.rate_ref = f32[5,4,16,256]{3,2,1,0:T(8,128)S(1)} custom-call(f32[5,4,16,256]{3,2,1,0:T(8,128)S(1)} %copy-done.1, f32[29,8,128]{2,1,0:T(8,128)S(1)} %collective-permute-done.low_ref.x1_ref, f32[29,8,128]{2,1,0:T(8,128)S(1)} %collective-permute-done.1.high_ref.x2_ref, f32[14,8,128]{2,1,0:T(8,128)S(1)} %collective-permute-done.4.y1_ref, ...), custom_call_target="tpu_custom_call" | custom-call | tf_op jit(solution)/shard_map/pallas_call | solution.py:429
  54.0 2.1 %shard_map.64 = (f32[4,4,16,256]{3,2,1,0:T(8,128)S(1)}, f32[14,8,128]{2,1,0:T(8,128)S(1)}, f32[14,8,128]{2,1,0:T(8,128)S(1)}) custom-call(f32[5,4,16,256]{3,2,1,0:T(8,128)S(1)} %copy-done.1, f32[14,8,128]{2,1,0:T(8,128)S(1)} %collective-permute-done.4.y1_ref, f32[14,8,128]{2,1,0:T(8,128)S(1)} %collective-permute-done.5.y2_ref, ...), custom_call_target="tpu_custom_call" | custom-call | tf_op jit(solution)/shard_map/pallas_call | solution.py:432
  56.1 1.2 %all-to-all-done.1 = f32[8,1,128]{2,1,0:T(1,128)S(1)} async-done(((f32[8,1,128]{2,1,0:T(1,128)}), f32[8,1,128]{2,1,0:T(1,128)S(1)}, u32[]{:S(2)}, u32[]{:S(2)}) %all-to-all-start.1) | async-done | bytes 4128 | tf_op jit(solution)/shard_map/all_to_all | solution.py:395
  57.3 0.9 %shard_map.65 = (f32[5,4,16,256]{3,2,1,0:T(8,128)}, f32[3,3,3,3,64]{4,3,2,1,0:T(4,128)}) custom-call(f32[5,4,16,256]{3,2,1,0:T(8,128)S(1)} %copy-done.1, f32[5,4,16,256]{3,2,1,0:T(8,128)S(1)} %shard_map.63.rate_ref, f32[4,4,16,256]{3,2,1,0:T(8,128)S(1)} %get-tuple-element.32.dep_ref, f32[8,128]{1,0:T(8,128)S(1)} %bitcast.10, ...), custom_call_target="tpu_custom_call" | custom-call | tf_op jit(solution)/shard_map/pallas_call | solution.py:444
  (8 shorter events, 0.0 us)
Async XLA Ops:
  0.6 1.0 %copy-start = (f32[5,4,16,256]{3,2,1,0:T(8,128)S(1)}, f32[5,4,16,256]{3,2,1,0:T(8,128)}, u32[]{:S(2)}) copy-start(f32[5,4,16,256]{3,2,1,0:T(8,128)} %u_ref.7) | copy-start | bytes 983044
  1.6 0.9 %copy-start.2 = (f32[3,3,3,8,64]{4,3,2,1,0:T(8,128)S(1)}, f32[3,3,3,8,64]{4,3,2,1,0:T(8,128)}, u32[]{:S(2)}) copy-start(f32[3,3,3,8,64]{4,3,2,1,0:T(8,128)} %data_ref.1) | copy-start | bytes 165892
  1.6 0.9 %copy-start.3 = (s32[3,3,3,64]{3,2,1,0:T(4,128)S(1)}, s32[3,3,3,64]{3,2,1,0:T(4,128)}, u32[]{:S(2)}) copy-start(s32[3,3,3,64]{3,2,1,0:T(4,128)} %host_ref.1) | copy-start | bytes 20740
  1.6 0.9 %copy-start.4 = (s32[3,3,3]{2,1,0:T(4,128)S(1)}, s32[3,3,3]{2,1,0:T(4,128)}, u32[]{:S(2)}) copy-start(s32[3,3,3]{2,1,0:T(4,128)} %count_ref.1) | copy-start | bytes 328
  2.7 50.2 %copy-start.1 = (f32[5,4,16,256]{3,2,1,0:T(8,128)S(1)}, f32[5,4,16,256]{3,2,1,0:T(8,128)}, u32[]{:S(2)}) copy-start(f32[5,4,16,256]{3,2,1,0:T(8,128)} %u_ref.7) | copy-start | bytes 983044
  2.7 34.4 %collective-permute-start = (f32[29,8,128]{2,1,0:T(8,128)S(1)}, f32[29,8,128]{2,1,0:T(8,128)S(1)}, u32[]{:S(2)}, u32[]{:S(2)}) collective-permute-start(f32[29,8,128]{2,1,0:T(8,128)S(1)} %get-tuple-element.21), channel_id=1, source_target_pairs={{0,64},{64,128},{128,192},{192,256},{256,320},{320,384},{384,448},... | collective-permute-start | bytes 356360 | tf_op jit(solution)/shard_map/ppermute | solution.py:389
  7.7 29.4 %collective-permute-start.1 = (f32[29,8,128]{2,1,0:T(8,128)S(1)}, f32[29,8,128]{2,1,0:T(8,128)S(1)}, u32[]{:S(2)}, u32[]{:S(2)}) collective-permute-start(f32[29,8,128]{2,1,0:T(8,128)S(1)} %get-tuple-element.22), channel_id=1, source_target_pairs={{64,0},{128,64},{192,128},{256,192},{320,256},{384,320},{448,384},... | collective-permute-start | bytes 356360 | tf_op jit(solution)/shard_map/ppermute | solution.py:390
  37.7 4.9 %collective-permute-start.2 = (f32[11,8,128]{2,1,0:T(8,128)S(1)}, f32[11,8,128]{2,1,0:T(8,128)S(1)}, u32[]{:S(2)}, u32[]{:S(2)}) collective-permute-start(f32[11,8,128]{2,1,0:T(8,128)S(1)} %get-tuple-element.26), channel_id=1, source_target_pairs={{0,1},{1,2},{2,3},{3,4},{4,5},{5,6},{6,7},{7,0},{8,9},{9,10},{10,1... | collective-permute-start | bytes 135176 | tf_op jit(solution)/shard_map/ppermute | solution.py:389
  41.5 3.5 %collective-permute-start.3 = (f32[11,8,128]{2,1,0:T(8,128)S(1)}, f32[11,8,128]{2,1,0:T(8,128)S(1)}, u32[]{:S(2)}, u32[]{:S(2)}) collective-permute-start(f32[11,8,128]{2,1,0:T(8,128)S(1)} %get-tuple-element.27), channel_id=1, source_target_pairs={{1,0},{2,1},{3,2},{4,3},{5,4},{6,5},{7,6},{0,7},{9,8},{10,9},{11,1... | collective-permute-start | bytes 135176 | tf_op jit(solution)/shard_map/ppermute | solution.py:390
  45.0 7.9 %collective-permute-start.4 = (f32[14,8,128]{2,1,0:T(8,128)S(1)}, f32[14,8,128]{2,1,0:T(8,128)S(1)}, u32[]{:S(2)}, u32[]{:S(2)}) collective-permute-start(f32[14,8,128]{2,1,0:T(8,128)S(1)} %get-tuple-element.29), channel_id=1, source_target_pairs={{0,8},{8,16},{16,24},{24,32},{32,40},{40,48},{48,56},{1,9},{9,17},... | collective-permute-start | bytes 172040 | tf_op jit(solution)/shard_map/ppermute | solution.py:389
  47.2 5.7 %collective-permute-start.5 = (f32[14,8,128]{2,1,0:T(8,128)S(1)}, f32[14,8,128]{2,1,0:T(8,128)S(1)}, u32[]{:S(2)}, u32[]{:S(2)}) collective-permute-start(f32[14,8,128]{2,1,0:T(8,128)S(1)} %get-tuple-element.30), channel_id=1, source_target_pairs={{8,0},{16,8},{24,16},{32,24},{40,32},{48,40},{56,48},{9,1},{17,9},... | collective-permute-start | bytes 172040 | tf_op jit(solution)/shard_map/ppermute | solution.py:390
  48.5 8.9 %all-to-all-start.1 = ((f32[8,1,128]{2,1,0:T(1,128)}), f32[8,1,128]{2,1,0:T(1,128)S(1)}, u32[]{:S(2)}, u32[]{:S(2)}) async-start(f32[8,1,128]{2,1,0:T(1,128)} %bitcast.4), calls=%async_computation.1 | async-start | bytes 8192 | tf_op jit(solution)/shard_map/all_to_all | solution.py:395
